TPU v7x, 256 devices: a whole 4x4x8 slice. The times are simulated.
256 devices in a mesh: grp: 8 (over x_hi, y), freq: 32 (over x_lo, z, core).
Axes of the slice: x: 4 (x_hi: 2, x_lo: 2; x = x_hi * 2 + x_lo), y: 4, z: 8, core: 2. Of those that a mesh axis runs over, the one named last changes fastest.
Arguments:
- residuals: bfloat16 [64, 32, 2, 4096], P('grp', None, None, 'freq'), may hold values from -6 to 6
- system_matrix: bfloat16 [4096, 2, 16384], P('freq'), may hold values from -0.0625 to 0.0625
- offsets: int32 [64], replicated, may hold values from 0 to 31
- patch_ids: int32 [64], replicated, may hold values from 0 to 63, each once
Outputs:
- volume: float32 [32, 2, 32, 16384], P(None, None, 'grp', 'freq')
All inputs are finite; a program needn't handle non-finite values.
Results may differ from a plain program's by a relative error of at most 0.0003.
Values may be sent and summed in bfloat16 or wider, within the bound.
No kernel may reach another device: no remote copies, remote signals or barrier semaphores. Data moves between devices by JAX's collectives and lax.ppermute only.
A program may use at most 192 MiB of HBM per device.

v0:
```python
import jax
import jax.numpy as jnp
from jax import lax
from jax.sharding import PartitionSpec as P

BR_DEV = 4


def adjoint_block(resid, matrix):
    groups, frames, parts, width = resid.shape
    voxels = matrix.shape[2]
    rows = resid.reshape(groups * frames * parts, width)
    flat = matrix.reshape(width, 2 * voxels)
    product = jnp.dot(rows, flat, preferred_element_type=jnp.float32)
    product = product.reshape(groups, frames, 2, 2, voxels)
    real_part = product[:, :, 0, 0] + product[:, :, 1, 1]
    imag_part = product[:, :, 1, 0] - product[:, :, 0, 1]
    return jnp.stack([real_part, imag_part], axis=2)


def lookup_targets(row_ids, offsets):
    count = offsets.shape[0]
    match = row_ids[:, None] == jnp.arange(count, dtype=jnp.int32)[None, :]
    return jnp.sum(jnp.where(match, offsets[None, :], 0), axis=1)


def on_device(residuals, system_matrix, offsets, patch_ids):
    high = lax.Precision.HIGHEST
    terms = adjoint_block(residuals, system_matrix)
    slab_terms = lax.psum_scatter(terms, "freq", scatter_dimension=3, tiled=True)
    group_index = lax.axis_index("grp")
    gathered = lax.all_gather(slab_terms, "grp", axis=0, tiled=True)
    targets = lookup_targets(patch_ids, offsets)
    owned = group_index * BR_DEV + jnp.arange(BR_DEV, dtype=jnp.int32)
    select = (targets[:, None] == owned[None, :]).astype(jnp.float32)
    volume = jnp.einsum("pk,ptcv->tckv", select, gathered, precision=high)
    return volume


def solution(mesh):
    in_specs = (P("grp", None, None, "freq"), P("freq", None, None), P(), P())
    out_specs = P(None, None, "grp", "freq")
    return jax.shard_map(
        on_device, mesh=mesh, in_specs=in_specs, out_specs=out_specs, check_vma=False
    )
```

profile of v0, /device:TPU:24, one launch (start us, length us, event | category | flops | bytes accessed | tf_op | source)
XLA Modules:
  0.0 427.0 jit_solution(11165024227217867020)
XLA Ops:
  6.5 0.0 reduce-scatter.2.cloned.1.call-start
  6.5 0.0 copy-start
  6.5 11.8 %copy.22 = bf16[16,8,2,16384]{3,1,2,0:T(8,128)(2,1)} copy(bf16[16,8,2,16384]{3,2,1,0:T(2,128)(2,1)} %bitcast.34) | data formatting | bytes 16777216
  18.4 11.9 %copy.10 = bf16[32768,128]{1,0:T(8,128)(2,1)} copy(bf16[32768,128]{0,1:T(8,128)(2,1)} %bitcast.33) | data formatting | bytes 16777216 | tf_op jit(solution)/shard_map/dot_general | solution.py:14
  30.3 0.0 copy-done
  30.3 26.5 %fusion.8 = f32[8,32,2,2,16384]{4,1,3,2,0:T(8,128)} fusion(bf16[2,16384,128,1,1]{2,1,0,4,3:T(8,128)(2,1)} %bitcast.32, bf16[8,32,2,128,1]{3,2,1,0,4:T(2,128)(2,1)S(1)} %bitcast.35), kind=kOutput, calls=%fused_computation.10 | convolution fusion | flops 4294967296 | bytes 75628544 | tf_op jit(solution)/shard_map/dot_general | solution.py:14
  56.8 11.3 %fusion = f32[8,32,1,16384]{3,1,0,2:T(8,128)S(1)} fusion(f32[8,32,2,2,16384]{4,1,3,2,0:T(8,128)} %fusion.8), kind=kLoop, calls=%fused_computation.2 | loop fusion | flops 4194304 | bytes 50331648 | tf_op jit(solution)/shard_map/sub | solution.py:17
  68.1 17.8 %fusion.2 = f32[8,32,1,16384]{3,1,0,2:T(8,128)} fusion(f32[8,32,2,2,16384]{4,1,3,2,0:T(8,128)} %fusion.8), kind=kLoop, calls=%fused_computation.5 | loop fusion | flops 4194304 | bytes 50331648 | tf_op jit(solution)/shard_map/add | solution.py:16
  85.9 18.4 %pad_maximum_fusion = f32[8,32,2,16384]{3,1,0,2:T(8,128)} fusion(f32[8,32,1,16384]{3,1,0,2:T(8,128)S(1)} %fusion, f32[8,32,1,16384]{3,1,0,2:T(8,128)} %fusion.2), kind=kLoop, calls=%fused_computation | loop fusion | flops 8388608 | bytes 67108864 | tf_op jit(solution)/shard_map/stack | solution.py:18
  104.3 0.0 copy-start.1
  104.3 0.0 copy-start.2
  104.3 0.0 reduce-scatter.2.cloned.1.call-update
  104.3 0.2 all-gather.2.cloned.1.call-start
  104.5 193.9 %reduce-scatter.2.cloned.1.call-done = f32[8,32,2,512]{3,1,0,2:T(8,128)} async-done(((f32[8,32,2,16384]{3,1,0,2:T(8,128)}), f32[8,32,2,512]{3,1,0,2:T(8,128)}) %reduce-scatter.2.cloned.1.call-update) | async-done | bytes 1048592 | tf_op jit(solution)/shard_map/reduce_scatter | solution.py:30
  298.5 0.0 all-gather.2.cloned.1.call-update
  298.5 0.0 copy-done.1
  298.5 0.0 copy-done.2
  298.5 0.2 select_reduce_fusion
  298.7 110.3 %all-gather.2.cloned.1.call-done = f32[64,32,2,512]{3,1,0,2:T(8,128)} async-done(((f32[8,32,2,512]{3,1,0,2:T(8,128)}), f32[64,32,2,512]{3,1,0,2:T(8,128)}) %all-gather.2.cloned.1.call-update) | async-done | bytes 8388624 | tf_op jit(solution)/shard_map/all_gather | solution.py:32
  409.0 11.2 %fusion.5 = f32[32,2,4,512]{3,2,1,0:T(4,128)} fusion(f32[64,32,2,512]{3,1,0,2:T(8,128)} %all-gather.2.cloned.1.call-done, s32[64]{0:T(128)S(1)} %select_reduce_fusion, s32[4]{0:T(128)S(1)} %iota_add_fusion), kind=kOutput, calls=%fused_computation.9 | convolution fusion | flops 100663552 | bytes 8913168 | tf_op jit(solution)/shard_map/pk,ptcv->tckv/dot_general | solution.py:36
  (1 shorter events, 0.0 us)
Async XLA Ops:
  6.5 291.9 %reduce-scatter.2.cloned.1.call-start = ((), (), s32[]{:S(2)}) async-start(), calls=%async_computation.1 | async-start | bytes 34603008 | tf_op jit(solution)/shard_map/reduce_scatter | solution.py:30
  6.5 23.8 %copy-start = (bf16[8,32,2,128]{3,2,1,0:T(2,128)(2,1)S(1)}, bf16[8,32,2,128]{3,2,1,0:T(2,128)(2,1)}, u32[]{:S(2)}) copy-start(bf16[8,32,2,128]{3,2,1,0:T(2,128)(2,1)} %param.4) | copy-start | bytes 393220
  104.3 194.2 %copy-start.1 = (s32[64]{0:T(128)S(1)}, s32[64]{0:T(128)}, u32[]{:S(2)}) copy-start(s32[64]{0:T(128)} %param.6) | copy-start | bytes 772
  104.3 194.2 %copy-start.2 = (s32[64]{0:T(128)S(1)}, s32[64]{0:T(128)}, u32[]{:S(2)}) copy-start(s32[64]{0:T(128)} %param.7) | copy-start | bytes 772
  104.3 304.7 %all-gather.2.cloned.1.call-start = ((), (), s32[]{:S(2)}) async-start(), calls=%async_computation.2 | async-start | bytes 9437184 | tf_op jit(solution)/shard_map/all_gather | solution.py:32
Sparse Core Ops, SparseCore 0:
  104.4 193.9 reduce-scatter.1
  301.0 107.8 all-gather.1
where the time goes:
time: 430 us; the launch traced here: 427 us
  waiting for transfers between devices  304 us (71%)
  other arithmetic  47.6 us (11%)
  matrix products  37.7 us (9%)
  local copies, waits for them, and re-layouts  23.8 us (6%)
  between operations  13.4 us (3%)
    reduce_scatter x1, waiting for transfers between devices, on_device(): lax.psum_scatter(terms, 'freq', scatter_dimension=3, tiled=True)  194 us
    all_gather x1, waiting for transfers between devices, on_device(): gathered = lax.all_gather(slab_terms, 'grp', axis=0, tiled=True)  110 us
    dot_general x1, matrix products, adjoint_block(): product = jnp.dot(rows, flat, preferred_element_type=jnp.float32)  26.5 us
    another operation x1, other arithmetic, adjoint_block(): return jnp.stack([real_part, imag_part], axis=2)  18.4 us
    add x1, other arithmetic, adjoint_block(): real_part = product[:, :, 0, 0] + product[:, :, 1, 1]  17.8 us
    dot_general x1, local copies, waits for them, and re-layouts, adjoint_block(): product = jnp.dot(rows, flat, preferred_element_type=jnp.float32)  11.9 us
    unnamed x7, local copies, waits for them, and re-layouts  11.9 us
    sub x1, other arithmetic, adjoint_block(): imag_part = product[:, :, 1, 0] - product[:, :, 0, 1]  11.3 us
  transfers between devices with their start and end apart: 2, of which 2 were waited for; matrix products, arithmetic and copies ran while one was open for 0% of the time, Pallas kernels for 0%

commit v1 on v0

v1 whole, which is shorter than its diff:
```python
import functools

import jax
import jax.numpy as jnp
from jax import lax
from jax.experimental import pallas as pl
from jax.experimental.pallas import tpu as pltpu
from jax.sharding import PartitionSpec as P

XH, Y, XL, Z, CORE = 2, 4, 2, 8, 2
NX = XH * XL
BR_DEV = 4
TARGETS = (4, -3, 3, -2, 2, -1, 1, 0)
MESSAGES = ((0, 1), (2,), (3,), (4,), (5,), (6,), (7,))
FREE = pl.CostEstimate(flops=1000, bytes_accessed=1000, transcendentals=0)
PARAMS = pltpu.CompilerParams(vmem_limit_bytes=24 * 2**20)
SMEM = pl.BlockSpec(memory_space=pltpu.SMEM)
VMEM = pl.BlockSpec(memory_space=pltpu.VMEM)
F32, BF16 = jnp.float32, jnp.bfloat16


def linear(xh, y, xl, z, c):
    return (((xh * Y + y) * XL + xl) * Z + z) * CORE + c


def shift(array, dx=0, dy=0, dz=0, dc=0, mirror=False):
    pairs = []
    for x in range(NX):
        for y in range(Y):
            for z in range(Z):
                for c in range(CORE):
                    way = -1 if mirror and c else 1
                    tx = (x + way * dx) % NX
                    ty, tz, t = (y + way * dy) % Y, (z + way * dz) % Z, (c + dc) % CORE
                    pairs.append((linear(x // 2, y, x % 2, z, c), linear(tx // 2, ty, tx % 2, tz, t)))
    return lax.ppermute(array, ("grp", "freq"), pairs)


def place():
    grp, freq = lax.axis_index("grp"), lax.axis_index("freq")
    return grp >> 2, grp & 3, freq >> 4, (freq >> 1) & 7, freq & 1


def add_rows_kernel(place_ref, offs_ref, ids_ref, r0, r1, r2, r3, same, plus, minus, other, acc):
    xh, y, xl = place_ref[0], place_ref[1], place_ref[2]
    rows = r0.shape[0]
    acc[...] = jnp.zeros_like(acc)
    for dy, ref in enumerate((r0, r1, r2, r3)):
        first = (xh * Y + (y + dy) % Y) * rows
        for i in range(rows):
            brick = offs_ref[ids_ref[first + i]]
            owner = brick // BR_DEV
            slot = (owner // Y) * BR_DEV + brick % BR_DEV
            slot = jnp.where(owner % Y == y, slot, XH * BR_DEV)
            acc[slot] += ref[i].astype(F32)
    here, there = pl.ds(xh * BR_DEV, BR_DEV), pl.ds((1 - xh) * BR_DEV, BR_DEV)
    same[...] = acc[here]
    other[...] = acc[there]
    right = jnp.where(xl == 0, xh, 1 - xh)
    plus[...] = acc[pl.ds(right * BR_DEV, BR_DEV)]
    minus[...] = acc[pl.ds((1 - right) * BR_DEV, BR_DEV)]


def add_rows(where, offsets, patch_ids, pieces):
    tc, width = pieces[0].shape[1:]
    out = jax.ShapeDtypeStruct((BR_DEV, tc, width), F32)
    return pl.pallas_call(
        add_rows_kernel,
        out_shape=[out] * 4,
        in_specs=[SMEM] * 3 + [VMEM] * 4,
        out_specs=[VMEM] * 4,
        compiler_params=PARAMS,
        cost_estimate=FREE,
        scratch_shapes=[pltpu.VMEM((XH * BR_DEV + 1, tc, width), F32)],
        name="add_rows",
    )(where, offsets, patch_ids, *pieces)


def expand_kernel(a0, a1, b0, b1, out):
    bricks, tc, width = a0.shape
    rows, depth = bricks * tc, 2 * width
    r = lax.broadcasted_iota(jnp.int32, (rows, rows), 0)
    s = lax.broadcasted_iota(jnp.int32, (rows, rows), 1)
    reorder = (s == (r % bricks) * tc + r // bricks).astype(F32).astype(BF16)
    f = lax.broadcasted_iota(jnp.int32, (depth, depth), 0)
    k = lax.broadcasted_iota(jnp.int32, (depth, depth), 1)
    weave = (k == 2 * (f % width) + f // width).astype(F32).astype(BF16)
    part = lax.broadcasted_iota(jnp.int32, (rows, width), 0) % 2
    dot = functools.partial(jnp.dot, preferred_element_type=F32)
    parts = []
    for u, v in ((a0, a1), (b0, b1)):
        x = (u[...] + v[...]).reshape(rows, width)
        xs = jnp.where(part == 0, pltpu.roll(x, rows - 1, 0), -pltpu.roll(x, 1, 0))
        both = jnp.concatenate([x, xs], axis=1)
        hi = both.astype(BF16)
        parts += [hi, (both - hi.astype(F32)).astype(BF16)]
    woven = dot(jnp.concatenate(parts, axis=0), weave).astype(BF16)
    wide = jnp.concatenate([woven[i * rows:(i + 1) * rows] for i in range(4)], axis=1)
    wide = dot(reorder, wide).astype(BF16)
    for i in range(4):
        out[i // 2, i % 2] = wide[:, i * depth:(i + 1) * depth]


def expand(a0, a1, b0, b1):
    bricks, tc, width = a0.shape
    rows = bricks * tc
    return pl.pallas_call(
        expand_kernel,
        out_shape=jax.ShapeDtypeStruct((2, 2, rows, 2 * width), BF16),
        in_specs=[VMEM] * 4,
        out_specs=VMEM,
        compiler_params=PARAMS,
        cost_estimate=FREE,
        name="expand",
    )(a0, a1, b0, b1)


def cut_matrix(where, matrix, messages, room, local=False):
    width, parts, voxels = matrix.shape
    span = voxels // (XL * Z * CORE)
    piece = (width, parts, span)
    shapes = [(2, len(message)) + piece for message in messages] + [(Z,) + piece] * (2 * local)
    count = 2 * sum(map(len, messages)) + 2 * Z * local

    def kernel(place_ref, src, *rest):
        outs, sems = rest[:-1], rest[-1]
        xl, z, c = place_ref[2], place_ref[3], place_ref[4]
        wanted = [
            (s, 1, dc, out.at[dc, k]) for out, message in zip(outs, messages) for k, s in enumerate(message) for dc in range(2)
        ]
        if local:
            wanted += [(s, 0, dc, outs[dc - 2].at[s]) for s in range(Z) for dc in range(2)]
        copies = []
        for i, (s, dxl, dc, out) in enumerate(wanted):
            reader = (c + dc) % CORE
            at = (z + Z + (1 - 2 * reader) * TARGETS[s]) % Z
            first = (((xl + dxl) % XL * Z + at) * CORE + reader) * span
            columns = src.at[:, :, pl.ds(pl.multiple_of(first, span), span)]
            copies.append(pltpu.make_async_copy(columns, out, sems.at[i]))
        for copy in copies:
            copy.start()
        for copy in copies:
            copy.wait()

    return pl.pallas_call(
        kernel,
        in_specs=[SMEM, pl.BlockSpec(memory_space=pltpu.HBM)],
        out_specs=[VMEM] * len(shapes),
        out_shape=[jax.ShapeDtypeStruct(s, BF16) for s in shapes],
        scratch_shapes=[pltpu.SemaphoreType.DMA((count,))],
        compiler_params=pltpu.CompilerParams(vmem_limit_bytes=room * 2**20),
        cost_estimate=FREE,
        name="cut_matrix",
    )(where, matrix)


def flatten_kernel(i, k, own, core, far, cross, out):
    for n, m in enumerate((own.at[i], core.at[i], far.at[0, k], cross.at[k])):
        out[n] = m[...].reshape(out.shape[1:])


def flatten(own, core, far, cross, i, k):
    width, parts, span = own.shape[1:]
    return pl.pallas_call(
        functools.partial(flatten_kernel, i, k),
        out_shape=jax.ShapeDtypeStruct((4, width * parts, span), BF16),
        in_specs=[VMEM] * 4,
        out_specs=VMEM,
        compiler_params=PARAMS,
        cost_estimate=FREE,
        name="flatten",
    )(own, core, far, cross)


def term_kernel(el, ec, flat, *rest):
    dot = functools.partial(jnp.dot, preferred_element_type=F32)
    total = None if len(rest) == 1 else rest[0][...]
    for n, e in enumerate((el.at[0], ec.at[0], el.at[1], ec.at[1])):
        for h in range(2):
            d = dot(e[h], flat[n])
            total = d if total is None else total + d
    rest[-1][...] = total


def term(el, ec, flat, *so_far):
    return pl.pallas_call(
        term_kernel,
        out_shape=jax.ShapeDtypeStruct((el.shape[2], flat.shape[2]), F32),
        in_specs=[VMEM] * (3 + len(so_far)),
        out_specs=VMEM,
        compiler_params=PARAMS,
        cost_estimate=FREE,
        name="term",
    )(el, ec, flat, *so_far)


def finish_kernel(a, b, c, out):
    out[...] = (a[...] + b[...] + c[...]).reshape(out.shape)


def finish(*parts):
    rows, cols = parts[0].shape
    return pl.pallas_call(
        finish_kernel,
        out_shape=jax.ShapeDtypeStruct((rows // BR_DEV, BR_DEV, cols), F32),
        in_specs=[VMEM] * 3,
        out_specs=VMEM,
        compiler_params=PARAMS,
        cost_estimate=FREE,
        name="finish",
    )(*parts)


def on_device(residuals, system_matrix, offsets, patch_ids):
    xh, y, xl, z, c = place()
    where = jnp.stack([xh, y, xl, z, c]).astype(jnp.int32)
    rows, frames, parts, width = residuals.shape
    tc = frames * parts
    raw = residuals.reshape(rows, tc, width)
    pieces = [shift(raw, dy=-1), shift(raw, dy=2), shift(raw, dy=1)]
    (far,) = cut_matrix(where, system_matrix, MESSAGES[:1], 56)
    fars = [across(far)]
    matrix, pieces[0] = lax.optimization_barrier((system_matrix, pieces[0]))
    *far, own, core = cut_matrix(where, matrix, MESSAGES[1:], 48, local=True)
    sent = add_rows(where, offsets, patch_ids, [raw] + pieces)
    (same, plus, minus, other), fars[0], core = lax.optimization_barrier((sent, fars[0], core))
    rest = [shift(plus, dx=1), shift(minus, dx=-1), shift(other, dx=2)]
    core = shift(core, dc=1)
    cross = shift(fars[0][1], dc=1)
    flats = [flatten(own, core, fars[0], cross, s, s) for s in MESSAGES[0]]
    far[0], flats, rest = lax.optimization_barrier((far[0], flats, rest))
    fars.append(across(far[0]))
    from_left, from_right, across_two = rest
    el = expand(same, across_two, from_left, from_right)
    far[1], el = lax.optimization_barrier((far[1], el))
    fars.append(across(far[1]))
    ec = shift(el, dc=1)

    sums = [None, None]
    for s in range(Z):
        if s >= 2:
            fars[s - 1], total = lax.optimization_barrier((fars[s - 1], total))
            sums[1 - s % 2] = shift(total, dz=2 * (s % 2) - 1, mirror=True)
            cross = shift(fars[s - 1][1], dc=1)
            flats.append(flatten(own, core, fars[s - 1], cross, s, 0))
        if s == Z - 1:
            total = term(el, ec, flats[s])
            break
        total = term(el, ec, flats[s], *sums[s % 2:s % 2 + 1] if s > 1 else ())
        if s == 0:
            flats[1], total = lax.optimization_barrier((flats[1], total))
            sums[0] = shift(total, dz=1, mirror=True)
        if 1 <= s < Z - 3:
            late, total = lax.optimization_barrier((far[s + 1], total))
            fars.append(across(late))
    volume = finish(total, *sums)
    return volume.reshape(frames, parts, BR_DEV, -1)


def across(far):
    return shift(far, dx=1, mirror=True)


def solution(mesh):
    in_specs = (P("grp", None, None, "freq"), P("freq", None, None), P(), P())
    out_specs = P(None, None, "grp", "freq")
    return jax.shard_map(
        on_device, mesh=mesh, in_specs=in_specs, out_specs=out_specs, check_vma=False
    )
```

time: 430 us -> 89.9 us (0.21)
  waiting for transfers between devices: 304 us -> 45.3 us
  other arithmetic: 47.6 us -> 0 us
  matrix products: 37.7 us -> 0 us
  starting transfers between devices: 0.22 us -> 24.5 us
  local copies, waits for them, and re-layouts: 23.8 us -> 2.1 us
  Pallas kernels: 0 us -> 17.6 us
  between operations: 13.4 us -> 0.31 us
    reduce_scatter x1 -> x0, waiting for transfers between devices: 194 us -> none  [on_device(): lax.psum_scatter(terms, 'freq', scatter_dimension=3, tiled=True)]
    all_gather x1 -> x0, waiting for transfers between devices: 110 us -> none  [on_device(): gathered = lax.all_gather(slab_terms, 'grp', axis=0, tiled=True)]
    ppermute x0 -> x29, waiting for transfers between devices: none -> 45.3 us  [shift(): return lax.ppermute(array, ('grp', 'freq'), pairs)]
    dot_general x2 -> x0, matrix products: 37.7 us -> none  [the longest x1 26.5 us: adjoint_block(): product = jnp.dot(rows, flat, preferred_element_type=jnp.float32)]
    ppermute x0 -> x29, starting transfers between devices: none -> 24.5 us  [shift(): return lax.ppermute(array, ('grp', 'freq'), pairs)]
    another operation x1 -> x0, other arithmetic: 18.4 us -> none  [adjoint_block(): return jnp.stack([real_part, imag_part], axis=2)]
    add x2 -> x0, other arithmetic: 17.8 us -> none  [the longest x1 17.8 us: adjoint_block(): real_part = product[:, :, 0, 0] + product[:, :, 1, 1]]
    pallas_call x0 -> x21, Pallas kernels: none -> 17.6 us  [the longest x2 8.52 us: cut_matrix(): pl.pallas_call(kernel, in_specs=[SMEM, pl.BlockSpec(memory_space=pltpu.HB...]
  transfers between devices with their start and end apart: 2 -> 29, of which waited for: 2 -> 21; matrix products, arithmetic and copies ran while one was open for 0% -> 2% of each run, Pallas kernels for 0% -> 15%
where the time goes in v1:
time: 89.9 us; the launch traced here: 89.8 us
  waiting for transfers between devices  45.3 us (50%)
  starting transfers between devices  24.5 us (27%)
  Pallas kernels  17.6 us (20%)
  local copies, waits for them, and re-layouts  2.1 us (2%)
    ppermute x29, waiting for transfers between devices, shift(): return lax.ppermute(array, ('grp', 'freq'), pairs)  45.3 us
    ppermute x29, starting transfers between devices, shift(): return lax.ppermute(array, ('grp', 'freq'), pairs)  24.5 us
    pallas_call x2, Pallas kernels, cut_matrix(): pl.pallas_call(kernel, in_specs=[SMEM, pl.BlockSpec(memory_space=pltpu.HB...  8.52 us
    pallas_call x8, Pallas kernels, term(): pl.pallas_call(term_kernel, out_shape=jax.ShapeDtypeStruct((el.shape[2],...  5.6 us
  transfers between devices with their start and end apart: 29, of which 21 were waited for; matrix products, arithmetic and copies ran while one was open for 2% of the time, Pallas kernels for 15%

profile of v1, /device:TPU:24, one launch (start us, length us, event | category | flops | bytes accessed | tf_op | source)
XLA Modules:
  0.0 89.8 jit_solution(15797451245094721930)
XLA Ops:
  0.6 3.1 %cut_matrix.3 = bf16[2,2,128,2,512]{4,3,2,1,0:T(2,128)(2,1)} custom-call(s32[5]{0:T(128)} %stack.23.place_ref, bf16[128,2,16384]{2,1,0:T(2,128)(2,1)} %src.2), custom_call_target="tpu_custom_call" | custom-call | flops 1000 | bytes 1000 | tf_op jit(solution)/shard_map/cut_matrix/pallas_call | solution.py:145
  3.7 1.6 %collective-permute-start.3 = (bf16[2,2,128,2,512]{4,3,2,1,0:T(2,128)(2,1)}, bf16[2,2,128,2,512]{4,3,2,1,0:T(2,128)(2,1)S(1)}, u32[]{:S(2)}, u32[]{:S(2)}) collective-permute-start(bf16[2,2,128,2,512]{4,3,2,1,0:T(2,128)(2,1)} %cut_matrix.3), channel_id=1, source_target_pairs={{0,16},{1,145},{2,18},{3,147},{4,20},{5,149},{6,22},{7,151},{8,24}... | collective-permute-start | bytes 3145736 | tf_op jit(solution)/shard_map/ppermute | solution.py:36
  7.3 1.8 %collective-permute-start.2 = (bf16[8,64,128]{2,1,0:T(8,128)(2,1)S(1)}, bf16[8,64,128]{2,1,0:T(8,128)(2,1)S(1)}, u32[]{:S(2)}, u32[]{:S(2)}) collective-permute-start(bf16[8,64,128]{2,1,0:T(8,128)(2,1)S(1)} %bitcast.23), channel_id=1, source_target_pairs={{0,32},{1,33},{2,34},{3,35},{4,36},{5,37},{6,38},{7,39},{8,40},{9,... | collective-permute-start | bytes 393224 | tf_op jit(solution)/shard_map/ppermute | solution.py:36
  9.1 6.4 %collective-permute-done.r1 = bf16[8,64,128]{2,1,0:T(8,128)(2,1)S(1)} collective-permute-done((bf16[8,64,128]{2,1,0:T(8,128)(2,1)S(1)}, bf16[8,64,128]{2,1,0:T(8,128)(2,1)S(1)}, u32[]{:S(2)}, u32[]{:S(2)}) %collective-permute-start) | collective-permute-done | bytes 131104 | tf_op jit(solution)/shard_map/ppermute | solution.py:36
  15.5 5.5 %cut_matrix.2 = (bf16[2,1,128,2,512]{4,3,2,1,0:T(2,128)(2,1)S(1)}, bf16[2,1,128,2,512]{4,3,2,1,0:T(2,128)(2,1)S(1)}, bf16[2,1,128,2,512]{4,3,2,1,0:T(2,128)(2,1)...) custom-call(s32[5]{0:T(128)S(1)} %copy-done.1, ...), custom_call_target="tpu_custom_call" | custom-call | flops 1000 | bytes 1000 | tf_op jit(solution)/shard_map/cut_matrix/pallas_call | solution.py:145
  23.1 3.2 %collective-permute-start.7 = (f32[4,64,128]{2,1,0:T(8,128)S(1)}, f32[4,64,128]{2,1,0:T(8,128)S(1)}, u32[]{:S(2)}, u32[]{:S(2)}) collective-permute-start(f32[4,64,128]{2,1,0:T(8,128)S(1)} %get-tuple-element.69), channel_id=1, source_target_pairs={{0,144},{1,145},{2,146},{3,147},{4,148},{5,149},{6,150},{7,151},{8... | collective-permute-start | bytes 393224 | tf_op jit(solution)/shard_map/ppermute | solution.py:36
  27.3 2.5 %collective-permute-done.6.b0 = f32[4,64,128]{2,1,0:T(8,128)S(1)} collective-permute-done((f32[4,64,128]{2,1,0:T(8,128)S(1)}, f32[4,64,128]{2,1,0:T(8,128)S(1)}, u32[]{:S(2)}, u32[]{:S(2)}) %collective-permute-start.6) | collective-permute-done | bytes 131104 | tf_op jit(solution)/shard_map/ppermute | solution.py:36
  29.8 2.1 %collective-permute-done.7.b1 = f32[4,64,128]{2,1,0:T(8,128)S(1)} collective-permute-done((f32[4,64,128]{2,1,0:T(8,128)S(1)}, f32[4,64,128]{2,1,0:T(8,128)S(1)}, u32[]{:S(2)}, u32[]{:S(2)}) %collective-permute-start.7) | collective-permute-done | bytes 131104 | tf_op jit(solution)/shard_map/ppermute | solution.py:36
  36.1 2.0 %collective-permute-start.14 = (f32[256,512]{1,0:T(8,128)S(1)}, f32[256,512]{1,0:T(8,128)S(1)}, u32[]{:S(2)}, u32[]{:S(2)}) collective-permute-start(f32[256,512]{1,0:T(8,128)S(1)} %term.8), channel_id=1, source_target_pairs={{0,2},{1,15},{2,4},{3,1},{4,6},{5,3},{6,8},{7,5},{8,10},{9,7},{10,... | collective-permute-start | bytes 1572872 | tf_op jit(solution)/shard_map/ppermute | solution.py:36
  39.5 4.5 %collective-permute-done.12.far = bf16[2,1,128,2,512]{4,3,2,1,0:T(2,128)(2,1)S(1)} collective-permute-done((bf16[2,1,128,2,512]{4,3,2,1,0:T(2,128)(2,1)S(1)}, bf16[2,1,128,2,512]{4,3,2,1,0:T(2,128)(2,1)S(1)}, u32[]{:S(2)}, u32[]{:S(2)}) %collective-permute-start.12) | collective-permute-done | bytes 524320 | tf_op jit(solution)/shard_map/ppermute | solution.py:36
  44.2 1.4 %collective-permute-start.13 = (bf16[1,128,2,512]{3,2,1,0:T(2,128)(2,1)S(1)}, bf16[1,128,2,512]{3,2,1,0:T(2,128)(2,1)S(1)}, u32[]{:S(2)}, u32[]{:S(2)}) collective-permute-start(bf16[1,128,2,512]{3,2,1,0:T(2,128)(2,1)S(1)} %slice_bitcast_fusion.6), channel_id=1, source_target_pairs={{0,1},{1,0},{2,3},{3,2},{4,5},{5,4},{6,7},{7,6},{8,9},{9,8},{10,11... | collective-permute-start | bytes 786440 | tf_op jit(solution)/shard_map/ppermute | solution.py:36
  45.6 4.8 %collective-permute-start.16 = (f32[256,512]{1,0:T(8,128)S(1)}, f32[256,512]{1,0:T(8,128)S(1)}, u32[]{:S(2)}, u32[]{:S(2)}) collective-permute-start(f32[256,512]{1,0:T(8,128)S(1)} %term.9), channel_id=1, source_target_pairs={{0,14},{1,3},{2,0},{3,5},{4,2},{5,7},{6,4},{7,9},{8,6},{9,11},{10,... | collective-permute-start | bytes 1572872 | tf_op jit(solution)/shard_map/ppermute | solution.py:36
  53.2 4.6 %collective-permute-done.16.rest_0_ = f32[256,512]{1,0:T(8,128)S(1)} collective-permute-done((f32[256,512]{1,0:T(8,128)S(1)}, f32[256,512]{1,0:T(8,128)S(1)}, u32[]{:S(2)}, u32[]{:S(2)}) %collective-permute-start.16) | collective-permute-done | bytes 524320 | tf_op jit(solution)/shard_map/ppermute | solution.py:36
  58.5 2.3 %collective-permute-done.10.far = bf16[2,1,128,2,512]{4,3,2,1,0:T(2,128)(2,1)S(1)} collective-permute-done((bf16[2,1,128,2,512]{4,3,2,1,0:T(2,128)(2,1)S(1)}, bf16[2,1,128,2,512]{4,3,2,1,0:T(2,128)(2,1)S(1)}, u32[]{:S(2)}, u32[]{:S(2)}) %collective-permute-start.10) | collective-permute-done | bytes 524320 | tf_op jit(solution)/shard_map/ppermute | solution.py:36
  61.1 1.5 %collective-permute-start.23 = (f32[256,512]{1,0:T(8,128)S(1)}, f32[256,512]{1,0:T(8,128)S(1)}, u32[]{:S(2)}, u32[]{:S(2)}) collective-permute-start(f32[256,512]{1,0:T(8,128)S(1)} %term.11), channel_id=1, source_target_pairs={{0,14},{1,3},{2,0},{3,5},{4,2},{5,7},{6,4},{7,9},{8,6},{9,11},{10,... | collective-permute-start | bytes 1572872 | tf_op jit(solution)/shard_map/ppermute | solution.py:36
  63.7 2.7 %collective-permute-done.21.far = bf16[2,1,128,2,512]{4,3,2,1,0:T(2,128)(2,1)S(1)} collective-permute-done((bf16[2,1,128,2,512]{4,3,2,1,0:T(2,128)(2,1)S(1)}, bf16[2,1,128,2,512]{4,3,2,1,0:T(2,128)(2,1)S(1)}, u32[]{:S(2)}, u32[]{:S(2)}) %collective-permute-start.21) | collective-permute-done | bytes 524320 | tf_op jit(solution)/shard_map/ppermute | solution.py:36
  66.9 1.3 %collective-permute-done.22.cross = bf16[1,128,2,512]{3,2,1,0:T(2,128)(2,1)S(1)} collective-permute-done((bf16[1,128,2,512]{3,2,1,0:T(2,128)(2,1)S(1)}, bf16[1,128,2,512]{3,2,1,0:T(2,128)(2,1)S(1)}, u32[]{:S(2)}, u32[]{:S(2)}) %collective-permute-start.22) | collective-permute-done | bytes 262176 | tf_op jit(solution)/shard_map/ppermute | solution.py:36
  68.4 2.5 %collective-permute-done.23.rest_0_ = f32[256,512]{1,0:T(8,128)S(1)} collective-permute-done((f32[256,512]{1,0:T(8,128)S(1)}, f32[256,512]{1,0:T(8,128)S(1)}, u32[]{:S(2)}, u32[]{:S(2)}) %collective-permute-start.23) | collective-permute-done | bytes 524320 | tf_op jit(solution)/shard_map/ppermute | solution.py:36
  71.5 1.4 %collective-permute-done.20.far = bf16[2,1,128,2,512]{4,3,2,1,0:T(2,128)(2,1)S(1)} collective-permute-done((bf16[2,1,128,2,512]{4,3,2,1,0:T(2,128)(2,1)S(1)}, bf16[2,1,128,2,512]{4,3,2,1,0:T(2,128)(2,1)S(1)}, u32[]{:S(2)}, u32[]{:S(2)}) %collective-permute-start.20) | collective-permute-done | bytes 524320 | tf_op jit(solution)/shard_map/ppermute | solution.py:36
  73.2 1.9 %collective-permute-start.28 = (f32[256,512]{1,0:T(8,128)S(1)}, f32[256,512]{1,0:T(8,128)S(1)}, u32[]{:S(2)}, u32[]{:S(2)}) collective-permute-start(f32[256,512]{1,0:T(8,128)S(1)} %term.13), channel_id=1, source_target_pairs={{0,14},{1,3},{2,0},{3,5},{4,2},{5,7},{6,4},{7,9},{8,6},{9,11},{10,... | collective-permute-start | bytes 1572872 | tf_op jit(solution)/shard_map/ppermute | solution.py:36
  75.2 1.9 %collective-permute-done.25.rest_0_ = f32[256,512]{1,0:T(8,128)S(1)} collective-permute-done((f32[256,512]{1,0:T(8,128)S(1)}, f32[256,512]{1,0:T(8,128)S(1)}, u32[]{:S(2)}, u32[]{:S(2)}) %collective-permute-start.25) | collective-permute-done | bytes 524320 | tf_op jit(solution)/shard_map/ppermute | solution.py:36
  79.5 1.5 %collective-permute-done.26.cross = bf16[1,128,2,512]{3,2,1,0:T(2,128)(2,1)S(1)} collective-permute-done((bf16[1,128,2,512]{3,2,1,0:T(2,128)(2,1)S(1)}, bf16[1,128,2,512]{3,2,1,0:T(2,128)(2,1)S(1)}, u32[]{:S(2)}, u32[]{:S(2)}) %collective-permute-start.26) | collective-permute-done | bytes 262176 | tf_op jit(solution)/shard_map/ppermute | solution.py:36
  81.8 4.0 %collective-permute-done.28.c = f32[256,512]{1,0:T(8,128)S(1)} collective-permute-done((f32[256,512]{1,0:T(8,128)S(1)}, f32[256,512]{1,0:T(8,128)S(1)}, u32[]{:S(2)}, u32[]{:S(2)}) %collective-permute-start.28) | collective-permute-done | bytes 524320 | tf_op jit(solution)/shard_map/ppermute | solution.py:36
  85.9 3.1 %collective-permute-done.27.b = f32[256,512]{1,0:T(8,128)S(1)} collective-permute-done((f32[256,512]{1,0:T(8,128)S(1)}, f32[256,512]{1,0:T(8,128)S(1)}, u32[]{:S(2)}, u32[]{:S(2)}) %collective-permute-start.27) | collective-permute-done | bytes 524320 | tf_op jit(solution)/shard_map/ppermute | solution.py:36
  (71 shorter events, 22.0 us)
Async XLA Ops:
  3.7 18.4 %collective-permute-start.3 = (bf16[2,2,128,2,512]{4,3,2,1,0:T(2,128)(2,1)}, bf16[2,2,128,2,512]{4,3,2,1,0:T(2,128)(2,1)S(1)}, u32[]{:S(2)}, u32[]{:S(2)}) collective-permute-start(bf16[2,2,128,2,512]{4,3,2,1,0:T(2,128)(2,1)} %cut_matrix.3), channel_id=1, source_target_pairs={{0,16},{1,145},{2,18},{3,147},{4,20},{5,149},{6,22},{7,151},{8,24}... | collective-permute-start | bytes 3145736 | tf_op jit(solution)/shard_map/ppermute | solution.py:36
  5.3 10.2 %collective-permute-start = (bf16[8,64,128]{2,1,0:T(8,128)(2,1)S(1)}, bf16[8,64,128]{2,1,0:T(8,128)(2,1)S(1)}, u32[]{:S(2)}, u32[]{:S(2)}) collective-permute-start(bf16[8,64,128]{2,1,0:T(8,128)(2,1)S(1)} %bitcast.21), channel_id=1, source_target_pairs={{0,96},{1,97},{2,98},{3,99},{4,100},{5,101},{6,102},{7,103},{8,104... | collective-permute-start | bytes 393224 | tf_op jit(solution)/shard_map/ppermute | solution.py:36
  6.0 15.0 %collective-permute-start.1 = (bf16[8,64,128]{2,1,0:T(8,128)(2,1)S(1)}, bf16[8,64,128]{2,1,0:T(8,128)(2,1)S(1)}, u32[]{:S(2)}, u32[]{:S(2)}) collective-permute-start(bf16[8,64,128]{2,1,0:T(8,128)(2,1)S(1)} %bitcast.22), channel_id=1, source_target_pairs={{0,64},{1,65},{2,66},{3,67},{4,68},{5,69},{6,70},{7,71},{8,72},{9,... | collective-permute-start | bytes 393224 | tf_op jit(solution)/shard_map/ppermute | solution.py:36
  7.3 13.7 %collective-permute-start.2 = (bf16[8,64,128]{2,1,0:T(8,128)(2,1)S(1)}, bf16[8,64,128]{2,1,0:T(8,128)(2,1)S(1)}, u32[]{:S(2)}, u32[]{:S(2)}) collective-permute-start(bf16[8,64,128]{2,1,0:T(8,128)(2,1)S(1)} %bitcast.23), channel_id=1, source_target_pairs={{0,32},{1,33},{2,34},{3,35},{4,36},{5,37},{6,38},{7,39},{8,40},{9,... | collective-permute-start | bytes 393224 | tf_op jit(solution)/shard_map/ppermute | solution.py:36
  22.1 5.0 %collective-permute-start.4 = (bf16[8,128,2,512]{3,2,1,0:T(2,128)(2,1)}, bf16[8,128,2,512]{3,2,1,0:T(2,128)(2,1)S(1)}, u32[]{:S(2)}, u32[]{:S(2)}) collective-permute-start(bf16[8,128,2,512]{3,2,1,0:T(2,128)(2,1)} %get-tuple-element.66), channel_id=1, source_target_pairs={{0,1},{1,0},{2,3},{3,2},{4,5},{5,4},{6,7},{7,6},{8,9},{9,8},{10,11... | collective-permute-start | bytes 6291464 | tf_op jit(solution)/shard_map/ppermute | solution.py:36
  22.5 4.5 %collective-permute-start.5 = (bf16[2,128,2,512]{3,2,1,0:T(2,128)(2,1)S(1)}, bf16[2,128,2,512]{3,2,1,0:T(2,128)(2,1)S(1)}, u32[]{:S(2)}, u32[]{:S(2)}) collective-permute-start(bf16[2,128,2,512]{3,2,1,0:T(2,128)(2,1)S(1)} %slice_bitcast_fusion), channel_id=1, source_target_pairs={{0,1},{1,0},{2,3},{3,2},{4,5},{5,4},{6,7},{7,6},{8,9},{9,8},{10,11... | collective-permute-start | bytes 1572872 | tf_op jit(solution)/shard_map/ppermute | solution.py:36
  23.1 6.7 %collective-permute-start.6 = (f32[4,64,128]{2,1,0:T(8,128)S(1)}, f32[4,64,128]{2,1,0:T(8,128)S(1)}, u32[]{:S(2)}, u32[]{:S(2)}) collective-permute-start(f32[4,64,128]{2,1,0:T(8,128)S(1)} %get-tuple-element.68), channel_id=1, source_target_pairs={{0,16},{1,17},{2,18},{3,19},{4,20},{5,21},{6,22},{7,23},{8,24},{9,... | collective-permute-start | bytes 393224 | tf_op jit(solution)/shard_map/ppermute | solution.py:36
  23.1 8.8 %collective-permute-start.7 = (f32[4,64,128]{2,1,0:T(8,128)S(1)}, f32[4,64,128]{2,1,0:T(8,128)S(1)}, u32[]{:S(2)}, u32[]{:S(2)}) collective-permute-start(f32[4,64,128]{2,1,0:T(8,128)S(1)} %get-tuple-element.69), channel_id=1, source_target_pairs={{0,144},{1,145},{2,146},{3,147},{4,148},{5,149},{6,150},{7,151},{8... | collective-permute-start | bytes 393224 | tf_op jit(solution)/shard_map/ppermute | solution.py:36
  26.4 6.5 %collective-permute-start.8 = (f32[4,64,128]{2,1,0:T(8,128)S(1)}, f32[4,64,128]{2,1,0:T(8,128)S(1)}, u32[]{:S(2)}, u32[]{:S(2)}) collective-permute-start(f32[4,64,128]{2,1,0:T(8,128)S(1)} %get-tuple-element.70), channel_id=1, source_target_pairs={{0,128},{1,129},{2,130},{3,131},{4,132},{5,133},{6,134},{7,135},{8... | collective-permute-start | bytes 393224 | tf_op jit(solution)/shard_map/ppermute | solution.py:36
  33.4 2.0 %collective-permute-start.9 = (bf16[2,2,256,256]{3,2,1,0:T(8,128)(2,1)S(1)}, bf16[2,2,256,256]{3,2,1,0:T(8,128)(2,1)S(1)}, u32[]{:S(2)}, u32[]{:S(2)}) collective-permute-start(bf16[2,2,256,256]{3,2,1,0:T(8,128)(2,1)S(1)} %expand.1.el), channel_id=1, source_target_pairs={{0,1},{1,0},{2,3},{3,2},{4,5},{5,4},{6,7},{7,6},{8,9},{9,8},{10,11... | collective-permute-start | bytes 1572872 | tf_op jit(solution)/shard_map/ppermute | solution.py:36
  33.5 10.5 %collective-permute-start.12 = (bf16[2,1,128,2,512]{4,3,2,1,0:T(2,128)(2,1)S(1)}, bf16[2,1,128,2,512]{4,3,2,1,0:T(2,128)(2,1)S(1)}, u32[]{:S(2)}, u32[]{:S(2)}) collective-permute-start(bf16[2,1,128,2,512]{4,3,2,1,0:T(2,128)(2,1)S(1)} %get-tuple-element.84), channel_id=1, source_target_pairs={{0,16},{1,145},{2,18},{3,147},{4,20},{5,149},{6,22},{7,151},{8,24}... | collective-permute-start | bytes 1572872 | tf_op jit(solution)/shard_map/ppermute | solution.py:36
  36.1 14.4 %collective-permute-start.14 = (f32[256,512]{1,0:T(8,128)S(1)}, f32[256,512]{1,0:T(8,128)S(1)}, u32[]{:S(2)}, u32[]{:S(2)}) collective-permute-start(f32[256,512]{1,0:T(8,128)S(1)} %term.8), channel_id=1, source_target_pairs={{0,2},{1,15},{2,4},{3,1},{4,6},{5,3},{6,8},{7,5},{8,10},{9,7},{10,... | collective-permute-start | bytes 1572872 | tf_op jit(solution)/shard_map/ppermute | solution.py:36
  38.1 13.1 %collective-permute-start.11 = (bf16[2,1,128,2,512]{4,3,2,1,0:T(2,128)(2,1)S(1)}, bf16[2,1,128,2,512]{4,3,2,1,0:T(2,128)(2,1)S(1)}, u32[]{:S(2)}, u32[]{:S(2)}) collective-permute-start(bf16[2,1,128,2,512]{4,3,2,1,0:T(2,128)(2,1)S(1)} %get-tuple-element.82), channel_id=1, source_target_pairs={{0,16},{1,145},{2,18},{3,147},{4,20},{5,149},{6,22},{7,151},{8,24}... | collective-permute-start | bytes 1572872 | tf_op jit(solution)/shard_map/ppermute | solution.py:36
  44.2 6.2 %collective-permute-start.13 = (bf16[1,128,2,512]{3,2,1,0:T(2,128)(2,1)S(1)}, bf16[1,128,2,512]{3,2,1,0:T(2,128)(2,1)S(1)}, u32[]{:S(2)}, u32[]{:S(2)}) collective-permute-start(bf16[1,128,2,512]{3,2,1,0:T(2,128)(2,1)S(1)} %slice_bitcast_fusion.6), channel_id=1, source_target_pairs={{0,1},{1,0},{2,3},{3,2},{4,5},{5,4},{6,7},{7,6},{8,9},{9,8},{10,11... | collective-permute-start | bytes 786440 | tf_op jit(solution)/shard_map/ppermute | solution.py:36
  45.6 12.2 %collective-permute-start.16 = (f32[256,512]{1,0:T(8,128)S(1)}, f32[256,512]{1,0:T(8,128)S(1)}, u32[]{:S(2)}, u32[]{:S(2)}) collective-permute-start(f32[256,512]{1,0:T(8,128)S(1)} %term.9), channel_id=1, source_target_pairs={{0,14},{1,3},{2,0},{3,5},{4,2},{5,7},{6,4},{7,9},{8,6},{9,11},{10,... | collective-permute-start | bytes 1572872 | tf_op jit(solution)/shard_map/ppermute | solution.py:36
  50.4 10.4 %collective-permute-start.10 = (bf16[2,1,128,2,512]{4,3,2,1,0:T(2,128)(2,1)S(1)}, bf16[2,1,128,2,512]{4,3,2,1,0:T(2,128)(2,1)S(1)}, u32[]{:S(2)}, u32[]{:S(2)}) collective-permute-start(bf16[2,1,128,2,512]{4,3,2,1,0:T(2,128)(2,1)S(1)} %get-tuple-element.80), channel_id=1, source_target_pairs={{0,16},{1,145},{2,18},{3,147},{4,20},{5,149},{6,22},{7,151},{8,24}... | collective-permute-start | bytes 1572872 | tf_op jit(solution)/shard_map/ppermute | solution.py:36
  51.6 11.4 %collective-permute-start.18 = (f32[256,512]{1,0:T(8,128)S(1)}, f32[256,512]{1,0:T(8,128)S(1)}, u32[]{:S(2)}, u32[]{:S(2)}) collective-permute-start(f32[256,512]{1,0:T(8,128)S(1)} %term.10), channel_id=1, source_target_pairs={{0,2},{1,15},{2,4},{3,1},{4,6},{5,3},{6,8},{7,5},{8,10},{9,7},{10,... | collective-permute-start | bytes 1572872 | tf_op jit(solution)/shard_map/ppermute | solution.py:36
  51.9 14.5 %collective-permute-start.21 = (bf16[2,1,128,2,512]{4,3,2,1,0:T(2,128)(2,1)S(1)}, bf16[2,1,128,2,512]{4,3,2,1,0:T(2,128)(2,1)S(1)}, u32[]{:S(2)}, u32[]{:S(2)}) collective-permute-start(bf16[2,1,128,2,512]{4,3,2,1,0:T(2,128)(2,1)S(1)} %get-tuple-element.96), channel_id=1, source_target_pairs={{0,16},{1,145},{2,18},{3,147},{4,20},{5,149},{6,22},{7,151},{8,24}... | collective-permute-start | bytes 1572872 | tf_op jit(solution)/shard_map/ppermute | solution.py:36
  61.1 9.7 %collective-permute-start.23 = (f32[256,512]{1,0:T(8,128)S(1)}, f32[256,512]{1,0:T(8,128)S(1)}, u32[]{:S(2)}, u32[]{:S(2)}) collective-permute-start(f32[256,512]{1,0:T(8,128)S(1)} %term.11), channel_id=1, source_target_pairs={{0,14},{1,3},{2,0},{3,5},{4,2},{5,7},{6,4},{7,9},{8,6},{9,11},{10,... | collective-permute-start | bytes 1572872 | tf_op jit(solution)/shard_map/ppermute | solution.py:36
  62.6 10.4 %collective-permute-start.20 = (bf16[2,1,128,2,512]{4,3,2,1,0:T(2,128)(2,1)S(1)}, bf16[2,1,128,2,512]{4,3,2,1,0:T(2,128)(2,1)S(1)}, u32[]{:S(2)}, u32[]{:S(2)}) collective-permute-start(bf16[2,1,128,2,512]{4,3,2,1,0:T(2,128)(2,1)S(1)} %get-tuple-element.95), channel_id=1, source_target_pairs={{0,16},{1,145},{2,18},{3,147},{4,20},{5,149},{6,22},{7,151},{8,24}... | collective-permute-start | bytes 1572872 | tf_op jit(solution)/shard_map/ppermute | solution.py:36
  66.7 10.5 %collective-permute-start.25 = (f32[256,512]{1,0:T(8,128)S(1)}, f32[256,512]{1,0:T(8,128)S(1)}, u32[]{:S(2)}, u32[]{:S(2)}) collective-permute-start(f32[256,512]{1,0:T(8,128)S(1)} %term.12), channel_id=1, source_target_pairs={{0,2},{1,15},{2,4},{3,1},{4,6},{5,3},{6,8},{7,5},{8,10},{9,7},{10,... | collective-permute-start | bytes 1572872 | tf_op jit(solution)/shard_map/ppermute | solution.py:36
  66.8 11.8 %collective-permute-start.19 = (bf16[2,1,128,2,512]{4,3,2,1,0:T(2,128)(2,1)S(1)}, bf16[2,1,128,2,512]{4,3,2,1,0:T(2,128)(2,1)S(1)}, u32[]{:S(2)}, u32[]{:S(2)}) collective-permute-start(bf16[2,1,128,2,512]{4,3,2,1,0:T(2,128)(2,1)S(1)} %get-tuple-element.94), channel_id=1, source_target_pairs={{0,16},{1,145},{2,18},{3,147},{4,20},{5,149},{6,22},{7,151},{8,24}... | collective-permute-start | bytes 1572872 | tf_op jit(solution)/shard_map/ppermute | solution.py:36
  73.2 12.7 %collective-permute-start.28 = (f32[256,512]{1,0:T(8,128)S(1)}, f32[256,512]{1,0:T(8,128)S(1)}, u32[]{:S(2)}, u32[]{:S(2)}) collective-permute-start(f32[256,512]{1,0:T(8,128)S(1)} %term.13), channel_id=1, source_target_pairs={{0,14},{1,3},{2,0},{3,5},{4,2},{5,7},{6,4},{7,9},{8,6},{9,11},{10,... | collective-permute-start | bytes 1572872 | tf_op jit(solution)/shard_map/ppermute | solution.py:36
  78.6 10.4 %collective-permute-start.27 = (f32[256,512]{1,0:T(8,128)S(1)}, f32[256,512]{1,0:T(8,128)S(1)}, u32[]{:S(2)}, u32[]{:S(2)}) collective-permute-start(f32[256,512]{1,0:T(8,128)S(1)} %term.14), channel_id=1, source_target_pairs={{0,2},{1,15},{2,4},{3,1},{4,6},{5,3},{6,8},{7,5},{8,10},{9,7},{10,... | collective-permute-start | bytes 1572872 | tf_op jit(solution)/shard_map/ppermute | solution.py:36
  (9 other events, 59.5 us)

commit v2 on v1

--- a/solution.py
+++ b/solution.py
@@ -12,6 +12,7 @@
 BR_DEV = 4
 TARGETS = (4, -3, 3, -2, 2, -1, 1, 0)
 MESSAGES = ((0, 1), (2,), (3,), (4,), (5,), (6,), (7,))
+PACE = (1, 2, 3)
 FREE = pl.CostEstimate(flops=1000, bytes_accessed=1000, transcendentals=0)
 PARAMS = pltpu.CompilerParams(vmem_limit_bytes=24 * 2**20)
 SMEM = pl.BlockSpec(memory_space=pltpu.SMEM)
@@ -115,7 +116,7 @@
     )(a0, a1, b0, b1)
 
 
-def cut_matrix(where, matrix, messages, room, local=False):
+def cut_matrix(where, matrix, messages, local=False):
     width, parts, voxels = matrix.shape
     span = voxels // (XL * Z * CORE)
     piece = (width, parts, span)
@@ -148,10 +149,10 @@
         out_specs=[VMEM] * len(shapes),
         out_shape=[jax.ShapeDtypeStruct(s, BF16) for s in shapes],
         scratch_shapes=[pltpu.SemaphoreType.DMA((count,))],
-        compiler_params=pltpu.CompilerParams(vmem_limit_bytes=room * 2**20),
+        compiler_params=PARAMS,
         cost_estimate=FREE,
         name="cut_matrix",
-    )(where, matrix)
+    )(where, pltpu.with_memory_space_constraint(matrix, pltpu.HBM))
 
 
 def flatten_kernel(i, k, own, core, far, cross, out):
@@ -218,22 +219,22 @@
     tc = frames * parts
     raw = residuals.reshape(rows, tc, width)
     pieces = [shift(raw, dy=-1), shift(raw, dy=2), shift(raw, dy=1)]
-    (far,) = cut_matrix(where, system_matrix, MESSAGES[:1], 56)
+    (far,) = cut_matrix(where, system_matrix, MESSAGES[:1])
     fars = [across(far)]
     matrix, pieces[0] = lax.optimization_barrier((system_matrix, pieces[0]))
-    *far, own, core = cut_matrix(where, matrix, MESSAGES[1:], 48, local=True)
+    *far, own, core = cut_matrix(where, matrix, MESSAGES[1:], local=True)
     sent = add_rows(where, offsets, patch_ids, [raw] + pieces)
     (same, plus, minus, other), fars[0], core = lax.optimization_barrier((sent, fars[0], core))
     rest = [shift(plus, dx=1), shift(minus, dx=-1), shift(other, dx=2)]
     core = shift(core, dc=1)
     cross = shift(fars[0][1], dc=1)
     flats = [flatten(own, core, fars[0], cross, s, s) for s in MESSAGES[0]]
-    far[0], flats, rest = lax.optimization_barrier((far[0], flats, rest))
-    fars.append(across(far[0]))
+    for i in range(3):
+        far[i], rest[i] = lax.optimization_barrier((far[i], rest[i]))
+        fars.append(across(far[i]))
+    flats, rest = lax.optimization_barrier((flats, rest))
     from_left, from_right, across_two = rest
     el = expand(same, across_two, from_left, from_right)
-    far[1], el = lax.optimization_barrier((far[1], el))
-    fars.append(across(far[1]))
     ec = shift(el, dc=1)
 
     sums = [None, None]
@@ -247,12 +248,12 @@
             total = term(el, ec, flats[s])
             break
         total = term(el, ec, flats[s], *sums[s % 2:s % 2 + 1] if s > 1 else ())
+        if s in PACE:
+            late, total = lax.optimization_barrier((far[len(fars) - 1], total))
+            fars.append(across(late))
         if s == 0:
             flats[1], total = lax.optimization_barrier((flats[1], total))
             sums[0] = shift(total, dz=1, mirror=True)
-        if 1 <= s < Z - 3:
-            late, total = lax.optimization_barrier((far[s + 1], total))
-            fars.append(across(late))
     volume = finish(total, *sums)
     return volume.reshape(frames, parts, BR_DEV, -1)
 

time: 89.9 us -> 87.1 us (0.969)
  Pallas kernels: 17.6 us -> 15 us
  waiting for transfers between devices: 45.3 us -> 47.9 us
  starting transfers between devices: 24.5 us -> 22.3 us
    pallas_call x2, Pallas kernels: 8.52 us -> 5.91 us  [cut_matrix(): pl.pallas_call(kernel, in_specs=[SMEM, pl.BlockSpec(memory_space=pltpu.HB...]
    ppermute x29, waiting for transfers between devices: 45.3 us -> 47.9 us  [shift(): return lax.ppermute(array, ('grp', 'freq'), pairs)]
    ppermute x29, starting transfers between devices: 24.5 us -> 22.3 us  [shift(): return lax.ppermute(array, ('grp', 'freq'), pairs)]
  transfers between devices with their start and end apart: 29 -> 29, of which waited for: 21 -> 20; matrix products, arithmetic and copies ran while one was open for 2% -> 2% of each run, Pallas kernels for 15% -> 13%
where the time goes in v2:
time: 87.1 us; the launch traced here: 87 us
  waiting for transfers between devices  47.9 us (55%)
  starting transfers between devices  22.3 us (26%)
  Pallas kernels  15 us (17%)
  local copies, waits for them, and re-layouts  1.55 us (2%)
    ppermute x29, waiting for transfers between devices, shift(): return lax.ppermute(array, ('grp', 'freq'), pairs)  47.9 us
    ppermute x29, starting transfers between devices, shift(): return lax.ppermute(array, ('grp', 'freq'), pairs)  22.3 us
    pallas_call x2, Pallas kernels, cut_matrix(): pl.pallas_call(kernel, in_specs=[SMEM, pl.BlockSpec(memory_space=pltpu.HB...  5.91 us
    pallas_call x8, Pallas kernels, term(): pl.pallas_call(term_kernel, out_shape=jax.ShapeDtypeStruct((el.shape[2],...  5.6 us
  transfers between devices with their start and end apart: 29, of which 20 were waited for; matrix products, arithmetic and copies ran while one was open for 2% of the time, Pallas kernels for 13%

profile of v2, /device:TPU:24, one launch (start us, length us, event | category | flops | bytes accessed | tf_op | source)
XLA Modules:
  0.0 87.0 jit_solution(14916077791356361853)
XLA Ops:
  0.1 1.8 %cut_matrix.2 = bf16[2,2,128,2,512]{4,3,2,1,0:T(2,128)(2,1)S(1)} custom-call(s32[5]{0:T(128)S(1)} %stack.23.place_ref, bf16[128,2,16384]{2,1,0:T(2,128)(2,1)} %src.2), custom_call_target="tpu_custom_call" | custom-call | flops 1000 | bytes 1000 | tf_op jit(solution)/shard_map/cut_matrix/pallas_call | solution.py:146
  1.9 1.6 %collective-permute-start.3 = (bf16[2,2,128,2,512]{4,3,2,1,0:T(2,128)(2,1)S(1)}, bf16[2,2,128,2,512]{4,3,2,1,0:T(2,128)(2,1)S(1)}, u32[]{:S(2)}, u32[]{:S(2)}) collective-permute-start(bf16[2,2,128,2,512]{4,3,2,1,0:T(2,128)(2,1)S(1)} %cut_matrix.2), channel_id=1, source_target_pairs={{0,16},{1,145},{2,18},{3,147},{4,20},{5,149},{6,22},{7,151},{8,24}... | collective-permute-start | bytes 3145736 | tf_op jit(solution)/shard_map/ppermute | solution.py:37
  4.2 1.3 %collective-permute-start.1 = (bf16[8,64,128]{2,1,0:T(8,128)(2,1)S(1)}, bf16[8,64,128]{2,1,0:T(8,128)(2,1)S(1)}, u32[]{:S(2)}, u32[]{:S(2)}) collective-permute-start(bf16[8,64,128]{2,1,0:T(8,128)(2,1)S(1)} %bitcast.22), channel_id=1, source_target_pairs={{0,64},{1,65},{2,66},{3,67},{4,68},{5,69},{6,70},{7,71},{8,72},{9,... | collective-permute-start | bytes 393224 | tf_op jit(solution)/shard_map/ppermute | solution.py:37
  5.5 1.8 %collective-permute-start.2 = (bf16[8,64,128]{2,1,0:T(8,128)(2,1)S(1)}, bf16[8,64,128]{2,1,0:T(8,128)(2,1)S(1)}, u32[]{:S(2)}, u32[]{:S(2)}) collective-permute-start(bf16[8,64,128]{2,1,0:T(8,128)(2,1)S(1)} %bitcast.23), channel_id=1, source_target_pairs={{0,32},{1,33},{2,34},{3,35},{4,36},{5,37},{6,38},{7,39},{8,40},{9,... | collective-permute-start | bytes 393224 | tf_op jit(solution)/shard_map/ppermute | solution.py:37
  7.3 6.4 %collective-permute-done.r1 = bf16[8,64,128]{2,1,0:T(8,128)(2,1)S(1)} collective-permute-done((bf16[8,64,128]{2,1,0:T(8,128)(2,1)S(1)}, bf16[8,64,128]{2,1,0:T(8,128)(2,1)S(1)}, u32[]{:S(2)}, u32[]{:S(2)}) %collective-permute-start) | collective-permute-done | bytes 131104 | tf_op jit(solution)/shard_map/ppermute | solution.py:37
  13.7 4.1 %cut_matrix.3 = (bf16[2,1,128,2,512]{4,3,2,1,0:T(2,128)(2,1)S(1)}, bf16[2,1,128,2,512]{4,3,2,1,0:T(2,128)(2,1)S(1)}, bf16[2,1,128,2,512]{4,3,2,1,0:T(2,128)(2,1)...) custom-call(s32[5]{0:T(128)S(1)} %stack.23.place_ref, ...), custom_call_target="tpu_custom_call" | custom-call | flops 1000 | bytes 1000 | tf_op jit(solution)/shard_map/cut_matrix/pallas_call | solution.py:146
  22.8 5.0 %collective-permute-done.8.a1 = f32[4,64,128]{2,1,0:T(8,128)S(1)} collective-permute-done((f32[4,64,128]{2,1,0:T(8,128)S(1)}, f32[4,64,128]{2,1,0:T(8,128)S(1)}, u32[]{:S(2)}, u32[]{:S(2)}) %collective-permute-start.8) | collective-permute-done | bytes 131104 | tf_op jit(solution)/shard_map/ppermute | solution.py:37
  27.9 1.8 %collective-permute-done.6.b0 = f32[4,64,128]{2,1,0:T(8,128)S(1)} collective-permute-done((f32[4,64,128]{2,1,0:T(8,128)S(1)}, f32[4,64,128]{2,1,0:T(8,128)S(1)}, u32[]{:S(2)}, u32[]{:S(2)}) %collective-permute-start.6) | collective-permute-done | bytes 131104 | tf_op jit(solution)/shard_map/ppermute | solution.py:37
  30.9 1.8 %collective-permute-done.9.ec = bf16[2,2,256,256]{3,2,1,0:T(8,128)(2,1)S(1)} collective-permute-done((bf16[2,2,256,256]{3,2,1,0:T(8,128)(2,1)S(1)}, bf16[2,2,256,256]{3,2,1,0:T(8,128)(2,1)S(1)}, u32[]{:S(2)}, u32[]{:S(2)}) %collective-permute-start.9) | collective-permute-done | bytes 524320 | tf_op jit(solution)/shard_map/ppermute | solution.py:37
  33.4 2.0 %collective-permute-start.13 = (f32[256,512]{1,0:T(8,128)S(1)}, f32[256,512]{1,0:T(8,128)S(1)}, u32[]{:S(2)}, u32[]{:S(2)}) collective-permute-start(f32[256,512]{1,0:T(8,128)S(1)} %term.8), channel_id=1, source_target_pairs={{0,2},{1,15},{2,4},{3,1},{4,6},{5,3},{6,8},{7,5},{8,10},{9,7},{10,... | collective-permute-start | bytes 1572872 | tf_op jit(solution)/shard_map/ppermute | solution.py:37
  36.1 5.2 %collective-permute-done.11.far = bf16[2,1,128,2,512]{4,3,2,1,0:T(2,128)(2,1)S(1)} collective-permute-done((bf16[2,1,128,2,512]{4,3,2,1,0:T(2,128)(2,1)S(1)}, bf16[2,1,128,2,512]{4,3,2,1,0:T(2,128)(2,1)S(1)}, u32[]{:S(2)}, u32[]{:S(2)}) %collective-permute-start.11) | collective-permute-done | bytes 524320 | tf_op jit(solution)/shard_map/ppermute | solution.py:37
  41.7 5.9 %collective-permute-start.15 = (f32[256,512]{1,0:T(8,128)S(1)}, f32[256,512]{1,0:T(8,128)S(1)}, u32[]{:S(2)}, u32[]{:S(2)}) collective-permute-start(f32[256,512]{1,0:T(8,128)S(1)} %term.9), channel_id=1, source_target_pairs={{0,14},{1,3},{2,0},{3,5},{4,2},{5,7},{6,4},{7,9},{8,6},{9,11},{10,... | collective-permute-start | bytes 1572872 | tf_op jit(solution)/shard_map/ppermute | solution.py:37
  50.4 4.6 %collective-permute-done.15.rest_0_ = f32[256,512]{1,0:T(8,128)S(1)} collective-permute-done((f32[256,512]{1,0:T(8,128)S(1)}, f32[256,512]{1,0:T(8,128)S(1)}, u32[]{:S(2)}, u32[]{:S(2)}) %collective-permute-start.15) | collective-permute-done | bytes 524320 | tf_op jit(solution)/shard_map/ppermute | solution.py:37
  55.7 2.3 %collective-permute-done.19.far = bf16[2,1,128,2,512]{4,3,2,1,0:T(2,128)(2,1)S(1)} collective-permute-done((bf16[2,1,128,2,512]{4,3,2,1,0:T(2,128)(2,1)S(1)}, bf16[2,1,128,2,512]{4,3,2,1,0:T(2,128)(2,1)S(1)}, u32[]{:S(2)}, u32[]{:S(2)}) %collective-permute-start.19) | collective-permute-done | bytes 524320 | tf_op jit(solution)/shard_map/ppermute | solution.py:37
  58.3 1.5 %collective-permute-start.23 = (f32[256,512]{1,0:T(8,128)S(1)}, f32[256,512]{1,0:T(8,128)S(1)}, u32[]{:S(2)}, u32[]{:S(2)}) collective-permute-start(f32[256,512]{1,0:T(8,128)S(1)} %term.11), channel_id=1, source_target_pairs={{0,14},{1,3},{2,0},{3,5},{4,2},{5,7},{6,4},{7,9},{8,6},{9,11},{10,... | collective-permute-start | bytes 1572872 | tf_op jit(solution)/shard_map/ppermute | solution.py:37
  60.9 2.7 %collective-permute-done.18.far = bf16[2,1,128,2,512]{4,3,2,1,0:T(2,128)(2,1)S(1)} collective-permute-done((bf16[2,1,128,2,512]{4,3,2,1,0:T(2,128)(2,1)S(1)}, bf16[2,1,128,2,512]{4,3,2,1,0:T(2,128)(2,1)S(1)}, u32[]{:S(2)}, u32[]{:S(2)}) %collective-permute-start.18) | collective-permute-done | bytes 524320 | tf_op jit(solution)/shard_map/ppermute | solution.py:37
  64.1 1.3 %collective-permute-done.22.cross = bf16[1,128,2,512]{3,2,1,0:T(2,128)(2,1)S(1)} collective-permute-done((bf16[1,128,2,512]{3,2,1,0:T(2,128)(2,1)S(1)}, bf16[1,128,2,512]{3,2,1,0:T(2,128)(2,1)S(1)}, u32[]{:S(2)}, u32[]{:S(2)}) %collective-permute-start.22) | collective-permute-done | bytes 262176 | tf_op jit(solution)/shard_map/ppermute | solution.py:37
  65.6 2.5 %collective-permute-done.23.rest_0_ = f32[256,512]{1,0:T(8,128)S(1)} collective-permute-done((f32[256,512]{1,0:T(8,128)S(1)}, f32[256,512]{1,0:T(8,128)S(1)}, u32[]{:S(2)}, u32[]{:S(2)}) %collective-permute-start.23) | collective-permute-done | bytes 524320 | tf_op jit(solution)/shard_map/ppermute | solution.py:37
  68.8 1.4 %collective-permute-done.17.far = bf16[2,1,128,2,512]{4,3,2,1,0:T(2,128)(2,1)S(1)} collective-permute-done((bf16[2,1,128,2,512]{4,3,2,1,0:T(2,128)(2,1)S(1)}, bf16[2,1,128,2,512]{4,3,2,1,0:T(2,128)(2,1)S(1)}, u32[]{:S(2)}, u32[]{:S(2)}) %collective-permute-start.17) | collective-permute-done | bytes 524320 | tf_op jit(solution)/shard_map/ppermute | solution.py:37
  70.4 1.9 %collective-permute-start.28 = (f32[256,512]{1,0:T(8,128)S(1)}, f32[256,512]{1,0:T(8,128)S(1)}, u32[]{:S(2)}, u32[]{:S(2)}) collective-permute-start(f32[256,512]{1,0:T(8,128)S(1)} %term.13), channel_id=1, source_target_pairs={{0,14},{1,3},{2,0},{3,5},{4,2},{5,7},{6,4},{7,9},{8,6},{9,11},{10,... | collective-permute-start | bytes 1572872 | tf_op jit(solution)/shard_map/ppermute | solution.py:37
  72.4 1.9 %collective-permute-done.25.rest_0_ = f32[256,512]{1,0:T(8,128)S(1)} collective-permute-done((f32[256,512]{1,0:T(8,128)S(1)}, f32[256,512]{1,0:T(8,128)S(1)}, u32[]{:S(2)}, u32[]{:S(2)}) %collective-permute-start.25) | collective-permute-done | bytes 524320 | tf_op jit(solution)/shard_map/ppermute | solution.py:37
  76.7 1.5 %collective-permute-done.26.cross = bf16[1,128,2,512]{3,2,1,0:T(2,128)(2,1)S(1)} collective-permute-done((bf16[1,128,2,512]{3,2,1,0:T(2,128)(2,1)S(1)}, bf16[1,128,2,512]{3,2,1,0:T(2,128)(2,1)S(1)}, u32[]{:S(2)}, u32[]{:S(2)}) %collective-permute-start.26) | collective-permute-done | bytes 262176 | tf_op jit(solution)/shard_map/ppermute | solution.py:37
  79.1 4.0 %collective-permute-done.28.c = f32[256,512]{1,0:T(8,128)S(1)} collective-permute-done((f32[256,512]{1,0:T(8,128)S(1)}, f32[256,512]{1,0:T(8,128)S(1)}, u32[]{:S(2)}, u32[]{:S(2)}) %collective-permute-start.28) | collective-permute-done | bytes 524320 | tf_op jit(solution)/shard_map/ppermute | solution.py:37
  83.1 3.1 %collective-permute-done.27.b = f32[256,512]{1,0:T(8,128)S(1)} collective-permute-done((f32[256,512]{1,0:T(8,128)S(1)}, f32[256,512]{1,0:T(8,128)S(1)}, u32[]{:S(2)}, u32[]{:S(2)}) %collective-permute-start.27) | collective-permute-done | bytes 524320 | tf_op jit(solution)/shard_map/ppermute | solution.py:37
  (69 shorter events, 19.3 us)
Async XLA Ops:
  1.9 17.0 %collective-permute-start.3 = (bf16[2,2,128,2,512]{4,3,2,1,0:T(2,128)(2,1)S(1)}, bf16[2,2,128,2,512]{4,3,2,1,0:T(2,128)(2,1)S(1)}, u32[]{:S(2)}, u32[]{:S(2)}) collective-permute-start(bf16[2,2,128,2,512]{4,3,2,1,0:T(2,128)(2,1)S(1)} %cut_matrix.2), channel_id=1, source_target_pairs={{0,16},{1,145},{2,18},{3,147},{4,20},{5,149},{6,22},{7,151},{8,24}... | collective-permute-start | bytes 3145736 | tf_op jit(solution)/shard_map/ppermute | solution.py:37
  3.5 10.2 %collective-permute-start = (bf16[8,64,128]{2,1,0:T(8,128)(2,1)S(1)}, bf16[8,64,128]{2,1,0:T(8,128)(2,1)S(1)}, u32[]{:S(2)}, u32[]{:S(2)}) collective-permute-start(bf16[8,64,128]{2,1,0:T(8,128)(2,1)S(1)} %bitcast.21), channel_id=1, source_target_pairs={{0,96},{1,97},{2,98},{3,99},{4,100},{5,101},{6,102},{7,103},{8,104... | collective-permute-start | bytes 393224 | tf_op jit(solution)/shard_map/ppermute | solution.py:37
  4.2 13.6 %collective-permute-start.1 = (bf16[8,64,128]{2,1,0:T(8,128)(2,1)S(1)}, bf16[8,64,128]{2,1,0:T(8,128)(2,1)S(1)}, u32[]{:S(2)}, u32[]{:S(2)}) collective-permute-start(bf16[8,64,128]{2,1,0:T(8,128)(2,1)S(1)} %bitcast.22), channel_id=1, source_target_pairs={{0,64},{1,65},{2,66},{3,67},{4,68},{5,69},{6,70},{7,71},{8,72},{9,... | collective-permute-start | bytes 393224 | tf_op jit(solution)/shard_map/ppermute | solution.py:37
  5.5 12.3 %collective-permute-start.2 = (bf16[8,64,128]{2,1,0:T(8,128)(2,1)S(1)}, bf16[8,64,128]{2,1,0:T(8,128)(2,1)S(1)}, u32[]{:S(2)}, u32[]{:S(2)}) collective-permute-start(bf16[8,64,128]{2,1,0:T(8,128)(2,1)S(1)} %bitcast.23), channel_id=1, source_target_pairs={{0,32},{1,33},{2,34},{3,35},{4,36},{5,37},{6,38},{7,39},{8,40},{9,... | collective-permute-start | bytes 393224 | tf_op jit(solution)/shard_map/ppermute | solution.py:37
  18.9 10.9 %collective-permute-start.4 = (bf16[8,128,2,512]{3,2,1,0:T(2,128)(2,1)S(1)}, bf16[8,128,2,512]{3,2,1,0:T(2,128)(2,1)S(1)}, u32[]{:S(2)}, u32[]{:S(2)}) collective-permute-start(bf16[8,128,2,512]{3,2,1,0:T(2,128)(2,1)S(1)} %get-tuple-element.65), channel_id=1, source_target_pairs={{0,1},{1,0},{2,3},{3,2},{4,5},{5,4},{6,7},{7,6},{8,9},{9,8},{10,11... | collective-permute-start | bytes 6291464 | tf_op jit(solution)/shard_map/ppermute | solution.py:37
  19.4 10.4 %collective-permute-start.5 = (bf16[2,128,2,512]{3,2,1,0:T(2,128)(2,1)S(1)}, bf16[2,128,2,512]{3,2,1,0:T(2,128)(2,1)S(1)}, u32[]{:S(2)}, u32[]{:S(2)}) collective-permute-start(bf16[2,128,2,512]{3,2,1,0:T(2,128)(2,1)S(1)} %slice_bitcast_fusion), channel_id=1, source_target_pairs={{0,1},{1,0},{2,3},{3,2},{4,5},{5,4},{6,7},{7,6},{8,9},{9,8},{10,11... | collective-permute-start | bytes 1572872 | tf_op jit(solution)/shard_map/ppermute | solution.py:37
  20.0 7.9 %collective-permute-start.8 = (f32[4,64,128]{2,1,0:T(8,128)S(1)}, f32[4,64,128]{2,1,0:T(8,128)S(1)}, u32[]{:S(2)}, u32[]{:S(2)}) collective-permute-start(f32[4,64,128]{2,1,0:T(8,128)S(1)} %get-tuple-element.74), channel_id=1, source_target_pairs={{0,128},{1,129},{2,130},{3,131},{4,132},{5,133},{6,134},{7,135},{8... | collective-permute-start | bytes 393224 | tf_op jit(solution)/shard_map/ppermute | solution.py:37
  20.8 7.2 %collective-permute-start.7 = (f32[4,64,128]{2,1,0:T(8,128)S(1)}, f32[4,64,128]{2,1,0:T(8,128)S(1)}, u32[]{:S(2)}, u32[]{:S(2)}) collective-permute-start(f32[4,64,128]{2,1,0:T(8,128)S(1)} %get-tuple-element.71), channel_id=1, source_target_pairs={{0,144},{1,145},{2,146},{3,147},{4,148},{5,149},{6,150},{7,151},{8... | collective-permute-start | bytes 393224 | tf_op jit(solution)/shard_map/ppermute | solution.py:37
  22.0 7.7 %collective-permute-start.6 = (f32[4,64,128]{2,1,0:T(8,128)S(1)}, f32[4,64,128]{2,1,0:T(8,128)S(1)}, u32[]{:S(2)}, u32[]{:S(2)}) collective-permute-start(f32[4,64,128]{2,1,0:T(8,128)S(1)} %get-tuple-element.68), channel_id=1, source_target_pairs={{0,16},{1,17},{2,18},{3,19},{4,20},{5,21},{6,22},{7,23},{8,24},{9,... | collective-permute-start | bytes 393224 | tf_op jit(solution)/shard_map/ppermute | solution.py:37
  30.7 2.0 %collective-permute-start.9 = (bf16[2,2,256,256]{3,2,1,0:T(8,128)(2,1)S(1)}, bf16[2,2,256,256]{3,2,1,0:T(8,128)(2,1)S(1)}, u32[]{:S(2)}, u32[]{:S(2)}) collective-permute-start(bf16[2,2,256,256]{3,2,1,0:T(8,128)(2,1)S(1)} %expand.1.el), channel_id=1, source_target_pairs={{0,1},{1,0},{2,3},{3,2},{4,5},{5,4},{6,7},{7,6},{8,9},{9,8},{10,11... | collective-permute-start | bytes 1572872 | tf_op jit(solution)/shard_map/ppermute | solution.py:37
  30.8 10.5 %collective-permute-start.11 = (bf16[2,1,128,2,512]{4,3,2,1,0:T(2,128)(2,1)S(1)}, bf16[2,1,128,2,512]{4,3,2,1,0:T(2,128)(2,1)S(1)}, u32[]{:S(2)}, u32[]{:S(2)}) collective-permute-start(bf16[2,1,128,2,512]{4,3,2,1,0:T(2,128)(2,1)S(1)} %get-tuple-element.82), channel_id=1, source_target_pairs={{0,16},{1,145},{2,18},{3,147},{4,20},{5,149},{6,22},{7,151},{8,24}... | collective-permute-start | bytes 1572872 | tf_op jit(solution)/shard_map/ppermute | solution.py:37
  33.4 14.4 %collective-permute-start.13 = (f32[256,512]{1,0:T(8,128)S(1)}, f32[256,512]{1,0:T(8,128)S(1)}, u32[]{:S(2)}, u32[]{:S(2)}) collective-permute-start(f32[256,512]{1,0:T(8,128)S(1)} %term.8), channel_id=1, source_target_pairs={{0,2},{1,15},{2,4},{3,1},{4,6},{5,3},{6,8},{7,5},{8,10},{9,7},{10,... | collective-permute-start | bytes 1572872 | tf_op jit(solution)/shard_map/ppermute | solution.py:37
  35.4 13.1 %collective-permute-start.10 = (bf16[2,1,128,2,512]{4,3,2,1,0:T(2,128)(2,1)S(1)}, bf16[2,1,128,2,512]{4,3,2,1,0:T(2,128)(2,1)S(1)}, u32[]{:S(2)}, u32[]{:S(2)}) collective-permute-start(bf16[2,1,128,2,512]{4,3,2,1,0:T(2,128)(2,1)S(1)} %get-tuple-element.80), channel_id=1, source_target_pairs={{0,16},{1,145},{2,18},{3,147},{4,20},{5,149},{6,22},{7,151},{8,24}... | collective-permute-start | bytes 1572872 | tf_op jit(solution)/shard_map/ppermute | solution.py:37
  41.4 6.2 %collective-permute-start.12 = (bf16[1,128,2,512]{3,2,1,0:T(2,128)(2,1)S(1)}, bf16[1,128,2,512]{3,2,1,0:T(2,128)(2,1)S(1)}, u32[]{:S(2)}, u32[]{:S(2)}) collective-permute-start(bf16[1,128,2,512]{3,2,1,0:T(2,128)(2,1)S(1)} %slice_bitcast_fusion.6), channel_id=1, source_target_pairs={{0,1},{1,0},{2,3},{3,2},{4,5},{5,4},{6,7},{7,6},{8,9},{9,8},{10,11... | collective-permute-start | bytes 786440 | tf_op jit(solution)/shard_map/ppermute | solution.py:37
  41.7 13.3 %collective-permute-start.15 = (f32[256,512]{1,0:T(8,128)S(1)}, f32[256,512]{1,0:T(8,128)S(1)}, u32[]{:S(2)}, u32[]{:S(2)}) collective-permute-start(f32[256,512]{1,0:T(8,128)S(1)} %term.9), channel_id=1, source_target_pairs={{0,14},{1,3},{2,0},{3,5},{4,2},{5,7},{6,4},{7,9},{8,6},{9,11},{10,... | collective-permute-start | bytes 1572872 | tf_op jit(solution)/shard_map/ppermute | solution.py:37
  47.6 10.4 %collective-permute-start.19 = (bf16[2,1,128,2,512]{4,3,2,1,0:T(2,128)(2,1)S(1)}, bf16[2,1,128,2,512]{4,3,2,1,0:T(2,128)(2,1)S(1)}, u32[]{:S(2)}, u32[]{:S(2)}) collective-permute-start(bf16[2,1,128,2,512]{4,3,2,1,0:T(2,128)(2,1)S(1)} %get-tuple-element.96), channel_id=1, source_target_pairs={{0,16},{1,145},{2,18},{3,147},{4,20},{5,149},{6,22},{7,151},{8,24}... | collective-permute-start | bytes 1572872 | tf_op jit(solution)/shard_map/ppermute | solution.py:37
  48.8 11.4 %collective-permute-start.21 = (f32[256,512]{1,0:T(8,128)S(1)}, f32[256,512]{1,0:T(8,128)S(1)}, u32[]{:S(2)}, u32[]{:S(2)}) collective-permute-start(f32[256,512]{1,0:T(8,128)S(1)} %term.10), channel_id=1, source_target_pairs={{0,2},{1,15},{2,4},{3,1},{4,6},{5,3},{6,8},{7,5},{8,10},{9,7},{10,... | collective-permute-start | bytes 1572872 | tf_op jit(solution)/shard_map/ppermute | solution.py:37
  49.1 14.5 %collective-permute-start.18 = (bf16[2,1,128,2,512]{4,3,2,1,0:T(2,128)(2,1)S(1)}, bf16[2,1,128,2,512]{4,3,2,1,0:T(2,128)(2,1)S(1)}, u32[]{:S(2)}, u32[]{:S(2)}) collective-permute-start(bf16[2,1,128,2,512]{4,3,2,1,0:T(2,128)(2,1)S(1)} %get-tuple-element.95), channel_id=1, source_target_pairs={{0,16},{1,145},{2,18},{3,147},{4,20},{5,149},{6,22},{7,151},{8,24}... | collective-permute-start | bytes 1572872 | tf_op jit(solution)/shard_map/ppermute | solution.py:37
  58.3 9.7 %collective-permute-start.23 = (f32[256,512]{1,0:T(8,128)S(1)}, f32[256,512]{1,0:T(8,128)S(1)}, u32[]{:S(2)}, u32[]{:S(2)}) collective-permute-start(f32[256,512]{1,0:T(8,128)S(1)} %term.11), channel_id=1, source_target_pairs={{0,14},{1,3},{2,0},{3,5},{4,2},{5,7},{6,4},{7,9},{8,6},{9,11},{10,... | collective-permute-start | bytes 1572872 | tf_op jit(solution)/shard_map/ppermute | solution.py:37
  59.8 10.4 %collective-permute-start.17 = (bf16[2,1,128,2,512]{4,3,2,1,0:T(2,128)(2,1)S(1)}, bf16[2,1,128,2,512]{4,3,2,1,0:T(2,128)(2,1)S(1)}, u32[]{:S(2)}, u32[]{:S(2)}) collective-permute-start(bf16[2,1,128,2,512]{4,3,2,1,0:T(2,128)(2,1)S(1)} %get-tuple-element.94), channel_id=1, source_target_pairs={{0,16},{1,145},{2,18},{3,147},{4,20},{5,149},{6,22},{7,151},{8,24}... | collective-permute-start | bytes 1572872 | tf_op jit(solution)/shard_map/ppermute | solution.py:37
  63.9 10.5 %collective-permute-start.25 = (f32[256,512]{1,0:T(8,128)S(1)}, f32[256,512]{1,0:T(8,128)S(1)}, u32[]{:S(2)}, u32[]{:S(2)}) collective-permute-start(f32[256,512]{1,0:T(8,128)S(1)} %term.12), channel_id=1, source_target_pairs={{0,2},{1,15},{2,4},{3,1},{4,6},{5,3},{6,8},{7,5},{8,10},{9,7},{10,... | collective-permute-start | bytes 1572872 | tf_op jit(solution)/shard_map/ppermute | solution.py:37
  64.0 11.8 %collective-permute-start.16 = (bf16[2,1,128,2,512]{4,3,2,1,0:T(2,128)(2,1)S(1)}, bf16[2,1,128,2,512]{4,3,2,1,0:T(2,128)(2,1)S(1)}, u32[]{:S(2)}, u32[]{:S(2)}) collective-permute-start(bf16[2,1,128,2,512]{4,3,2,1,0:T(2,128)(2,1)S(1)} %get-tuple-element.93), channel_id=1, source_target_pairs={{0,16},{1,145},{2,18},{3,147},{4,20},{5,149},{6,22},{7,151},{8,24}... | collective-permute-start | bytes 1572872 | tf_op jit(solution)/shard_map/ppermute | solution.py:37
  70.4 12.7 %collective-permute-start.28 = (f32[256,512]{1,0:T(8,128)S(1)}, f32[256,512]{1,0:T(8,128)S(1)}, u32[]{:S(2)}, u32[]{:S(2)}) collective-permute-start(f32[256,512]{1,0:T(8,128)S(1)} %term.13), channel_id=1, source_target_pairs={{0,14},{1,3},{2,0},{3,5},{4,2},{5,7},{6,4},{7,9},{8,6},{9,11},{10,... | collective-permute-start | bytes 1572872 | tf_op jit(solution)/shard_map/ppermute | solution.py:37
  75.8 10.4 %collective-permute-start.27 = (f32[256,512]{1,0:T(8,128)S(1)}, f32[256,512]{1,0:T(8,128)S(1)}, u32[]{:S(2)}, u32[]{:S(2)}) collective-permute-start(f32[256,512]{1,0:T(8,128)S(1)} %term.14), channel_id=1, source_target_pairs={{0,2},{1,15},{2,4},{3,1},{4,6},{5,3},{6,8},{7,5},{8,10},{9,7},{10,... | collective-permute-start | bytes 1572872 | tf_op jit(solution)/shard_map/ppermute | solution.py:37
  (8 other events, 40.6 us)

commit v3 on v2

--- a/solution.py
+++ b/solution.py
@@ -116,12 +116,12 @@
     )(a0, a1, b0, b1)
 
 
-def cut_matrix(where, matrix, messages, local=False):
+def cut_matrix(where, matrix, messages, local=()):
     width, parts, voxels = matrix.shape
     span = voxels // (XL * Z * CORE)
     piece = (width, parts, span)
-    shapes = [(2, len(message)) + piece for message in messages] + [(Z,) + piece] * (2 * local)
-    count = 2 * sum(map(len, messages)) + 2 * Z * local
+    shapes = [(2, len(message)) + piece for message in messages] + [(len(steps),) + piece for steps, _ in local]
+    count = 2 * sum(map(len, messages)) + sum(len(steps) for steps, _ in local)
 
     def kernel(place_ref, src, *rest):
         outs, sems = rest[:-1], rest[-1]
@@ -129,8 +129,8 @@
         wanted = [
             (s, 1, dc, out.at[dc, k]) for out, message in zip(outs, messages) for k, s in enumerate(message) for dc in range(2)
         ]
-        if local:
-            wanted += [(s, 0, dc, outs[dc - 2].at[s]) for s in range(Z) for dc in range(2)]
+        for out, (steps, dc) in zip(outs[len(messages):], local):
+            wanted += [(s, 0, dc, out.at[i]) for i, s in enumerate(steps)]
         copies = []
         for i, (s, dxl, dc, out) in enumerate(wanted):
             reader = (c + dc) % CORE
@@ -155,22 +155,24 @@
     )(where, pltpu.with_memory_space_constraint(matrix, pltpu.HBM))
 
 
-def flatten_kernel(i, k, own, core, far, cross, out):
-    for n, m in enumerate((own.at[i], core.at[i], far.at[0, k], cross.at[k])):
-        out[n] = m[...].reshape(out.shape[1:])
-
-
-def flatten(own, core, far, cross, i, k):
-    width, parts, span = own.shape[1:]
-    return pl.pallas_call(
-        functools.partial(flatten_kernel, i, k),
+def flatten_kernel(index, *refs):
+    out = refs[-1]
+    for n, (i, ref) in enumerate(zip(index, refs)):
+        out[n] = ref[i].reshape(out.shape[1:])
+
+
+def flatten(*pieces):
+    arrays, index = zip(*pieces)
+    width, parts, span = arrays[0].shape[-3:]
+    return pl.pallas_call(
+        functools.partial(flatten_kernel, index),
         out_shape=jax.ShapeDtypeStruct((4, width * parts, span), BF16),
         in_specs=[VMEM] * 4,
         out_specs=VMEM,
         compiler_params=PARAMS,
         cost_estimate=FREE,
         name="flatten",
-    )(own, core, far, cross)
+    )(*arrays)
 
 
 def term_kernel(el, ec, flat, *rest):
@@ -222,20 +224,24 @@
     (far,) = cut_matrix(where, system_matrix, MESSAGES[:1])
     fars = [across(far)]
     matrix, pieces[0] = lax.optimization_barrier((system_matrix, pieces[0]))
-    *far, own, core = cut_matrix(where, matrix, MESSAGES[1:], local=True)
+    early, late = MESSAGES[0], range(len(MESSAGES[0]), Z)
+    *far, own, core = cut_matrix(where, matrix, MESSAGES[1:2], ((early, 0), (range(Z), 1)))
     sent = add_rows(where, offsets, patch_ids, [raw] + pieces)
     (same, plus, minus, other), fars[0], core = lax.optimization_barrier((sent, fars[0], core))
     rest = [shift(plus, dx=1), shift(minus, dx=-1), shift(other, dx=2)]
     core = shift(core, dc=1)
     cross = shift(fars[0][1], dc=1)
-    flats = [flatten(own, core, fars[0], cross, s, s) for s in MESSAGES[0]]
-    for i in range(3):
-        far[i], rest[i] = lax.optimization_barrier((far[i], rest[i]))
-        fars.append(across(far[i]))
+    flats = [flatten((own, (s,)), (core, (s,)), (fars[0], (0, s)), (cross, (s,))) for s in early]
+    far[0], rest[0] = lax.optimization_barrier((far[0], rest[0]))
+    fars.append(across(far[0]))
     flats, rest = lax.optimization_barrier((flats, rest))
     from_left, from_right, across_two = rest
     el = expand(same, across_two, from_left, from_right)
+    matrix, el = lax.optimization_barrier((matrix, el))
     ec = shift(el, dc=1)
+    *more, own = cut_matrix(where, matrix, MESSAGES[2:], ((late, 0),))
+    far += more
+    fars += [across(f) for f in far[1:3]]
 
     sums = [None, None]
     for s in range(Z):
@@ -243,14 +249,14 @@
             fars[s - 1], total = lax.optimization_barrier((fars[s - 1], total))
             sums[1 - s % 2] = shift(total, dz=2 * (s % 2) - 1, mirror=True)
             cross = shift(fars[s - 1][1], dc=1)
-            flats.append(flatten(own, core, fars[s - 1], cross, s, 0))
+            flats.append(flatten((own, (s - 2,)), (core, (s,)), (fars[s - 1], (0, 0)), (cross, (0,))))
         if s == Z - 1:
             total = term(el, ec, flats[s])
             break
         total = term(el, ec, flats[s], *sums[s % 2:s % 2 + 1] if s > 1 else ())
         if s in PACE:
-            late, total = lax.optimization_barrier((far[len(fars) - 1], total))
-            fars.append(across(late))
+            ahead, total = lax.optimization_barrier((far[len(fars) - 1], total))
+            fars.append(across(ahead))
         if s == 0:
             flats[1], total = lax.optimization_barrier((flats[1], total))
             sums[0] = shift(total, dz=1, mirror=True)

time: 87.1 us -> 86.3 us (level)
  waiting for transfers between devices: 47.9 us -> 40.5 us
  starting transfers between devices: 22.3 us -> 26.9 us
  Pallas kernels: 15 us -> 16.4 us
    ppermute x29, waiting for transfers between devices: 47.9 us -> 40.5 us  [shift(): return lax.ppermute(array, ('grp', 'freq'), pairs)]
    ppermute x29, starting transfers between devices: 22.3 us -> 26.9 us  [shift(): return lax.ppermute(array, ('grp', 'freq'), pairs)]
    pallas_call x2 -> x3, Pallas kernels: 5.91 us -> 7.36 us  [cut_matrix(): pl.pallas_call(kernel, in_specs=[SMEM, pl.BlockSpec(memory_space=pltpu.HB...]
  transfers between devices with their start and end apart: 29 -> 29, of which waited for: 20 -> 24; matrix products, arithmetic and copies ran while one was open for 2% -> 2% of each run, Pallas kernels for 13% -> 15%
where the time goes in v3:
time: 86.3 us; the launch traced here: 85.6 us
  waiting for transfers between devices  40.5 us (47%)
  starting transfers between devices  26.9 us (31%)
  Pallas kernels  16.4 us (19%)
  local copies, waits for them, and re-layouts  1.55 us (2%)
    ppermute x29, waiting for transfers between devices, shift(): return lax.ppermute(array, ('grp', 'freq'), pairs)  40.5 us
    ppermute x29, starting transfers between devices, shift(): return lax.ppermute(array, ('grp', 'freq'), pairs)  26.9 us
    pallas_call x3, Pallas kernels, cut_matrix(): pl.pallas_call(kernel, in_specs=[SMEM, pl.BlockSpec(memory_space=pltpu.HB...  7.36 us
    pallas_call x8, Pallas kernels, term(): pl.pallas_call(term_kernel, out_shape=jax.ShapeDtypeStruct((el.shape[2],...  5.6 us
  transfers between devices with their start and end apart: 29, of which 24 were waited for; matrix products, arithmetic and copies ran while one was open for 2% of the time, Pallas kernels for 15%

profile of v3, /device:TPU:24, one launch (start us, length us, event | category | flops | bytes accessed | tf_op | source)
XLA Modules:
  0.0 85.6 jit_solution(14640032771566246827)
XLA Ops:
  0.1 1.8 %cut_matrix.3 = bf16[2,2,128,2,512]{4,3,2,1,0:T(2,128)(2,1)S(1)} custom-call(s32[5]{0:T(128)S(1)} %stack.23.place_ref, bf16[128,2,16384]{2,1,0:T(2,128)(2,1)} %src.3), custom_call_target="tpu_custom_call" | custom-call | flops 1000 | bytes 1000 | tf_op jit(solution)/shard_map/cut_matrix/pallas_call | solution.py:146
  1.9 1.6 %collective-permute-start.3 = (bf16[2,2,128,2,512]{4,3,2,1,0:T(2,128)(2,1)S(1)}, bf16[2,2,128,2,512]{4,3,2,1,0:T(2,128)(2,1)S(1)}, u32[]{:S(2)}, u32[]{:S(2)}) collective-permute-start(bf16[2,2,128,2,512]{4,3,2,1,0:T(2,128)(2,1)S(1)} %cut_matrix.3), channel_id=1, source_target_pairs={{0,16},{1,145},{2,18},{3,147},{4,20},{5,149},{6,22},{7,151},{8,24}... | collective-permute-start | bytes 3145736 | tf_op jit(solution)/shard_map/ppermute | solution.py:37
  4.2 2.5 %collective-permute-start.2 = (bf16[8,64,128]{2,1,0:T(8,128)(2,1)S(1)}, bf16[8,64,128]{2,1,0:T(8,128)(2,1)S(1)}, u32[]{:S(2)}, u32[]{:S(2)}) collective-permute-start(bf16[8,64,128]{2,1,0:T(8,128)(2,1)S(1)} %bitcast.22), channel_id=1, source_target_pairs={{0,32},{1,33},{2,34},{3,35},{4,36},{5,37},{6,38},{7,39},{8,40},{9,... | collective-permute-start | bytes 393224 | tf_op jit(solution)/shard_map/ppermute | solution.py:37
  6.7 4.2 %collective-permute-done.r1 = bf16[8,64,128]{2,1,0:T(8,128)(2,1)S(1)} collective-permute-done((bf16[8,64,128]{2,1,0:T(8,128)(2,1)S(1)}, bf16[8,64,128]{2,1,0:T(8,128)(2,1)S(1)}, u32[]{:S(2)}, u32[]{:S(2)}) %collective-permute-start) | collective-permute-done | bytes 131104 | tf_op jit(solution)/shard_map/ppermute | solution.py:37
  10.9 2.6 %cut_matrix.4 = (bf16[2,1,128,2,512]{4,3,2,1,0:T(2,128)(2,1)S(1)}, bf16[2,128,2,512]{3,2,1,0:T(2,128)(2,1)S(1)}, bf16[8,128,2,512]{3,2,1,0:T(2,128)(2,1)S(1)}) custom-call(s32[5]{0:T(128)S(1)} %stack.23.place_ref, bf16[128,2,16384]{2,1,0:T(2,128)(2,1)} %src.3), custom_call_target="tpu_custom_call" | custom-call | flops 1000 | bytes 1000 | tf_op jit(solution)/shard_map/cut_matrix/pallas_call | solution.py:146
  14.9 3.1 %collective-permute-done.3.refs_2_ = bf16[2,2,128,2,512]{4,3,2,1,0:T(2,128)(2,1)S(1)} collective-permute-done((bf16[2,2,128,2,512]{4,3,2,1,0:T(2,128)(2,1)S(1)}, bf16[2,2,128,2,512]{4,3,2,1,0:T(2,128)(2,1)S(1)}, u32[]{:S(2)}, u32[]{:S(2)}) %collective-permute-start.3) | collective-permute-done | bytes 1048608 | tf_op jit(solution)/shard_map/ppermute | solution.py:37
  19.2 3.0 %collective-permute-start.7 = (f32[4,64,128]{2,1,0:T(8,128)S(1)}, f32[4,64,128]{2,1,0:T(8,128)S(1)}, u32[]{:S(2)}, u32[]{:S(2)}) collective-permute-start(f32[4,64,128]{2,1,0:T(8,128)S(1)} %get-tuple-element.69), channel_id=1, source_target_pairs={{0,144},{1,145},{2,146},{3,147},{4,148},{5,149},{6,150},{7,151},{8... | collective-permute-start | bytes 393224 | tf_op jit(solution)/shard_map/ppermute | solution.py:37
  22.8 2.9 %collective-permute-done.6.b0 = f32[4,64,128]{2,1,0:T(8,128)S(1)} collective-permute-done((f32[4,64,128]{2,1,0:T(8,128)S(1)}, f32[4,64,128]{2,1,0:T(8,128)S(1)}, u32[]{:S(2)}, u32[]{:S(2)}) %collective-permute-start.6) | collective-permute-done | bytes 131104 | tf_op jit(solution)/shard_map/ppermute | solution.py:37
  25.9 1.8 %collective-permute-done.7.b1 = f32[4,64,128]{2,1,0:T(8,128)S(1)} collective-permute-done((f32[4,64,128]{2,1,0:T(8,128)S(1)}, f32[4,64,128]{2,1,0:T(8,128)S(1)}, u32[]{:S(2)}, u32[]{:S(2)}) %collective-permute-start.7) | collective-permute-done | bytes 131104 | tf_op jit(solution)/shard_map/ppermute | solution.py:37
  32.0 2.0 %collective-permute-start.13 = (f32[256,512]{1,0:T(8,128)S(1)}, f32[256,512]{1,0:T(8,128)S(1)}, u32[]{:S(2)}, u32[]{:S(2)}) collective-permute-start(f32[256,512]{1,0:T(8,128)S(1)} %term.8), channel_id=1, source_target_pairs={{0,2},{1,15},{2,4},{3,1},{4,6},{5,3},{6,8},{7,5},{8,10},{9,7},{10,... | collective-permute-start | bytes 1572872 | tf_op jit(solution)/shard_map/ppermute | solution.py:37
  34.0 3.0 %cut_matrix.5 = (bf16[2,1,128,2,512]{4,3,2,1,0:T(2,128)(2,1)S(1)}, bf16[2,1,128,2,512]{4,3,2,1,0:T(2,128)(2,1)S(1)}, bf16[2,1,128,2,512]{4,3,2,1,0:T(2,128)(2,1)...) custom-call(s32[5]{0:T(128)S(1)} %stack.23.place_ref, ...), custom_call_target="tpu_custom_call" | custom-call | flops 1000 | bytes 1000 | tf_op jit(solution)/shard_map/cut_matrix/pallas_call | solution.py:146
  40.0 4.4 %collective-permute-start.12 = (bf16[1,128,2,512]{3,2,1,0:T(2,128)(2,1)S(1)}, bf16[1,128,2,512]{3,2,1,0:T(2,128)(2,1)S(1)}, u32[]{:S(2)}, u32[]{:S(2)}) collective-permute-start(bf16[1,128,2,512]{3,2,1,0:T(2,128)(2,1)S(1)} %slice_bitcast_fusion.6), channel_id=1, source_target_pairs={{0,1},{1,0},{2,3},{3,2},{4,5},{5,4},{6,7},{7,6},{8,9},{9,8},{10,11... | collective-permute-start | bytes 786440 | tf_op jit(solution)/shard_map/ppermute | solution.py:37
  44.5 1.8 %collective-permute-start.15 = (f32[256,512]{1,0:T(8,128)S(1)}, f32[256,512]{1,0:T(8,128)S(1)}, u32[]{:S(2)}, u32[]{:S(2)}) collective-permute-start(f32[256,512]{1,0:T(8,128)S(1)} %term.9), channel_id=1, source_target_pairs={{0,14},{1,3},{2,0},{3,5},{4,2},{5,7},{6,4},{7,9},{8,6},{9,11},{10,... | collective-permute-start | bytes 1572872 | tf_op jit(solution)/shard_map/ppermute | solution.py:37
  47.6 2.8 %collective-permute-start.14 = (bf16[1,128,2,512]{3,2,1,0:T(2,128)(2,1)S(1)}, bf16[1,128,2,512]{3,2,1,0:T(2,128)(2,1)S(1)}, u32[]{:S(2)}, u32[]{:S(2)}) collective-permute-start(bf16[1,128,2,512]{3,2,1,0:T(2,128)(2,1)S(1)} %slice_bitcast_fusion.5), channel_id=1, source_target_pairs={{0,1},{1,0},{2,3},{3,2},{4,5},{5,4},{6,7},{7,6},{8,9},{9,8},{10,11... | collective-permute-start | bytes 786440 | tf_op jit(solution)/shard_map/ppermute | solution.py:37
  51.7 2.5 %collective-permute-done.15.rest_0_ = f32[256,512]{1,0:T(8,128)S(1)} collective-permute-done((f32[256,512]{1,0:T(8,128)S(1)}, f32[256,512]{1,0:T(8,128)S(1)}, u32[]{:S(2)}, u32[]{:S(2)}) %collective-permute-start.15) | collective-permute-done | bytes 524320 | tf_op jit(solution)/shard_map/ppermute | solution.py:37
  54.9 1.7 %collective-permute-done.19.refs_2_ = bf16[2,1,128,2,512]{4,3,2,1,0:T(2,128)(2,1)S(1)} collective-permute-done((bf16[2,1,128,2,512]{4,3,2,1,0:T(2,128)(2,1)S(1)}, bf16[2,1,128,2,512]{4,3,2,1,0:T(2,128)(2,1)S(1)}, u32[]{:S(2)}, u32[]{:S(2)}) %collective-permute-start.19) | collective-permute-done | bytes 524320 | tf_op jit(solution)/shard_map/ppermute | solution.py:37
  56.9 1.4 %collective-permute-start.23 = (f32[256,512]{1,0:T(8,128)S(1)}, f32[256,512]{1,0:T(8,128)S(1)}, u32[]{:S(2)}, u32[]{:S(2)}) collective-permute-start(f32[256,512]{1,0:T(8,128)S(1)} %term.11), channel_id=1, source_target_pairs={{0,14},{1,3},{2,0},{3,5},{4,2},{5,7},{6,4},{7,9},{8,6},{9,11},{10,... | collective-permute-start | bytes 1572872 | tf_op jit(solution)/shard_map/ppermute | solution.py:37
  58.6 2.2 %collective-permute-done.21.rest_0_ = f32[256,512]{1,0:T(8,128)S(1)} collective-permute-done((f32[256,512]{1,0:T(8,128)S(1)}, f32[256,512]{1,0:T(8,128)S(1)}, u32[]{:S(2)}, u32[]{:S(2)}) %collective-permute-start.21) | collective-permute-done | bytes 524320 | tf_op jit(solution)/shard_map/ppermute | solution.py:37
  64.2 2.5 %collective-permute-done.23.rest_0_ = f32[256,512]{1,0:T(8,128)S(1)} collective-permute-done((f32[256,512]{1,0:T(8,128)S(1)}, f32[256,512]{1,0:T(8,128)S(1)}, u32[]{:S(2)}, u32[]{:S(2)}) %collective-permute-start.23) | collective-permute-done | bytes 524320 | tf_op jit(solution)/shard_map/ppermute | solution.py:37
  70.7 2.4 %collective-permute-done.25.rest_0_ = f32[256,512]{1,0:T(8,128)S(1)} collective-permute-done((f32[256,512]{1,0:T(8,128)S(1)}, f32[256,512]{1,0:T(8,128)S(1)}, u32[]{:S(2)}, u32[]{:S(2)}) %collective-permute-start.25) | collective-permute-done | bytes 524320 | tf_op jit(solution)/shard_map/ppermute | solution.py:37
  74.3 1.6 %collective-permute-start.27 = (f32[256,512]{1,0:T(8,128)S(1)}, f32[256,512]{1,0:T(8,128)S(1)}, u32[]{:S(2)}, u32[]{:S(2)}) collective-permute-start(f32[256,512]{1,0:T(8,128)S(1)} %term.14), channel_id=1, source_target_pairs={{0,2},{1,15},{2,4},{3,1},{4,6},{5,3},{6,8},{7,5},{8,10},{9,7},{10,... | collective-permute-start | bytes 1572872 | tf_op jit(solution)/shard_map/ppermute | solution.py:37
  76.2 1.5 %collective-permute-done.26.refs_3_ = bf16[1,128,2,512]{3,2,1,0:T(2,128)(2,1)S(1)} collective-permute-done((bf16[1,128,2,512]{3,2,1,0:T(2,128)(2,1)S(1)}, bf16[1,128,2,512]{3,2,1,0:T(2,128)(2,1)S(1)}, u32[]{:S(2)}, u32[]{:S(2)}) %collective-permute-start.26) | collective-permute-done | bytes 262176 | tf_op jit(solution)/shard_map/ppermute | solution.py:37
  78.5 3.0 %collective-permute-done.28.c = f32[256,512]{1,0:T(8,128)S(1)} collective-permute-done((f32[256,512]{1,0:T(8,128)S(1)}, f32[256,512]{1,0:T(8,128)S(1)}, u32[]{:S(2)}, u32[]{:S(2)}) %collective-permute-start.28) | collective-permute-done | bytes 524320 | tf_op jit(solution)/shard_map/ppermute | solution.py:37
  81.5 3.2 %collective-permute-done.27.b = f32[256,512]{1,0:T(8,128)S(1)} collective-permute-done((f32[256,512]{1,0:T(8,128)S(1)}, f32[256,512]{1,0:T(8,128)S(1)}, u32[]{:S(2)}, u32[]{:S(2)}) %collective-permute-start.27) | collective-permute-done | bytes 524320 | tf_op jit(solution)/shard_map/ppermute | solution.py:37
  (70 shorter events, 26.1 us)
Async XLA Ops:
  1.9 16.1 %collective-permute-start.3 = (bf16[2,2,128,2,512]{4,3,2,1,0:T(2,128)(2,1)S(1)}, bf16[2,2,128,2,512]{4,3,2,1,0:T(2,128)(2,1)S(1)}, u32[]{:S(2)}, u32[]{:S(2)}) collective-permute-start(bf16[2,2,128,2,512]{4,3,2,1,0:T(2,128)(2,1)S(1)} %cut_matrix.3), channel_id=1, source_target_pairs={{0,16},{1,145},{2,18},{3,147},{4,20},{5,149},{6,22},{7,151},{8,24}... | collective-permute-start | bytes 3145736 | tf_op jit(solution)/shard_map/ppermute | solution.py:37
  3.5 7.4 %collective-permute-start = (bf16[8,64,128]{2,1,0:T(8,128)(2,1)S(1)}, bf16[8,64,128]{2,1,0:T(8,128)(2,1)S(1)}, u32[]{:S(2)}, u32[]{:S(2)}) collective-permute-start(bf16[8,64,128]{2,1,0:T(8,128)(2,1)S(1)} %bitcast.21), channel_id=1, source_target_pairs={{0,96},{1,97},{2,98},{3,99},{4,100},{5,101},{6,102},{7,103},{8,104... | collective-permute-start | bytes 393224 | tf_op jit(solution)/shard_map/ppermute | solution.py:37
  4.2 9.3 %collective-permute-start.2 = (bf16[8,64,128]{2,1,0:T(8,128)(2,1)S(1)}, bf16[8,64,128]{2,1,0:T(8,128)(2,1)S(1)}, u32[]{:S(2)}, u32[]{:S(2)}) collective-permute-start(bf16[8,64,128]{2,1,0:T(8,128)(2,1)S(1)} %bitcast.22), channel_id=1, source_target_pairs={{0,32},{1,33},{2,34},{3,35},{4,36},{5,37},{6,38},{7,39},{8,40},{9,... | collective-permute-start | bytes 393224 | tf_op jit(solution)/shard_map/ppermute | solution.py:37
  6.7 7.2 %collective-permute-start.1 = (bf16[8,64,128]{2,1,0:T(8,128)(2,1)S(1)}, bf16[8,64,128]{2,1,0:T(8,128)(2,1)S(1)}, u32[]{:S(2)}, u32[]{:S(2)}) collective-permute-start(bf16[8,64,128]{2,1,0:T(8,128)(2,1)S(1)} %bitcast.23), channel_id=1, source_target_pairs={{0,64},{1,65},{2,66},{3,67},{4,68},{5,69},{6,70},{7,71},{8,72},{9,... | collective-permute-start | bytes 393224 | tf_op jit(solution)/shard_map/ppermute | solution.py:37
  18.0 7.7 %collective-permute-start.4 = (bf16[8,128,2,512]{3,2,1,0:T(2,128)(2,1)S(1)}, bf16[8,128,2,512]{3,2,1,0:T(2,128)(2,1)S(1)}, u32[]{:S(2)}, u32[]{:S(2)}) collective-permute-start(bf16[8,128,2,512]{3,2,1,0:T(2,128)(2,1)S(1)} %get-tuple-element.64), channel_id=1, source_target_pairs={{0,1},{1,0},{2,3},{3,2},{4,5},{5,4},{6,7},{7,6},{8,9},{9,8},{10,11... | collective-permute-start | bytes 6291464 | tf_op jit(solution)/shard_map/ppermute | solution.py:37
  18.4 7.3 %collective-permute-start.5 = (bf16[2,128,2,512]{3,2,1,0:T(2,128)(2,1)S(1)}, bf16[2,128,2,512]{3,2,1,0:T(2,128)(2,1)S(1)}, u32[]{:S(2)}, u32[]{:S(2)}) collective-permute-start(bf16[2,128,2,512]{3,2,1,0:T(2,128)(2,1)S(1)} %slice_bitcast_fusion), channel_id=1, source_target_pairs={{0,1},{1,0},{2,3},{3,2},{4,5},{5,4},{6,7},{7,6},{8,9},{9,8},{10,11... | collective-permute-start | bytes 1572872 | tf_op jit(solution)/shard_map/ppermute | solution.py:37
  19.0 6.7 %collective-permute-start.6 = (f32[4,64,128]{2,1,0:T(8,128)S(1)}, f32[4,64,128]{2,1,0:T(8,128)S(1)}, u32[]{:S(2)}, u32[]{:S(2)}) collective-permute-start(f32[4,64,128]{2,1,0:T(8,128)S(1)} %get-tuple-element.67), channel_id=1, source_target_pairs={{0,16},{1,17},{2,18},{3,19},{4,20},{5,21},{6,22},{7,23},{8,24},{9,... | collective-permute-start | bytes 393224 | tf_op jit(solution)/shard_map/ppermute | solution.py:37
  19.2 8.5 %collective-permute-start.7 = (f32[4,64,128]{2,1,0:T(8,128)S(1)}, f32[4,64,128]{2,1,0:T(8,128)S(1)}, u32[]{:S(2)}, u32[]{:S(2)}) collective-permute-start(f32[4,64,128]{2,1,0:T(8,128)S(1)} %get-tuple-element.69), channel_id=1, source_target_pairs={{0,144},{1,145},{2,146},{3,147},{4,148},{5,149},{6,150},{7,151},{8... | collective-permute-start | bytes 393224 | tf_op jit(solution)/shard_map/ppermute | solution.py:37
  22.2 6.5 %collective-permute-start.8 = (f32[4,64,128]{2,1,0:T(8,128)S(1)}, f32[4,64,128]{2,1,0:T(8,128)S(1)}, u32[]{:S(2)}, u32[]{:S(2)}) collective-permute-start(f32[4,64,128]{2,1,0:T(8,128)S(1)} %get-tuple-element.70), channel_id=1, source_target_pairs={{0,128},{1,129},{2,130},{3,131},{4,132},{5,133},{6,134},{7,135},{8... | collective-permute-start | bytes 393224 | tf_op jit(solution)/shard_map/ppermute | solution.py:37
  29.4 10.5 %collective-permute-start.11 = (bf16[2,1,128,2,512]{4,3,2,1,0:T(2,128)(2,1)S(1)}, bf16[2,1,128,2,512]{4,3,2,1,0:T(2,128)(2,1)S(1)}, u32[]{:S(2)}, u32[]{:S(2)}) collective-permute-start(bf16[2,1,128,2,512]{4,3,2,1,0:T(2,128)(2,1)S(1)} %get-tuple-element.80), channel_id=1, source_target_pairs={{0,16},{1,145},{2,18},{3,147},{4,20},{5,149},{6,22},{7,151},{8,24}... | collective-permute-start | bytes 1572872 | tf_op jit(solution)/shard_map/ppermute | solution.py:37
  32.0 14.4 %collective-permute-start.13 = (f32[256,512]{1,0:T(8,128)S(1)}, f32[256,512]{1,0:T(8,128)S(1)}, u32[]{:S(2)}, u32[]{:S(2)}) collective-permute-start(f32[256,512]{1,0:T(8,128)S(1)} %term.8), channel_id=1, source_target_pairs={{0,2},{1,15},{2,4},{3,1},{4,6},{5,3},{6,8},{7,5},{8,10},{9,7},{10,... | collective-permute-start | bytes 1572872 | tf_op jit(solution)/shard_map/ppermute | solution.py:37
  37.0 10.5 %collective-permute-start.10 = (bf16[2,1,128,2,512]{4,3,2,1,0:T(2,128)(2,1)S(1)}, bf16[2,1,128,2,512]{4,3,2,1,0:T(2,128)(2,1)S(1)}, u32[]{:S(2)}, u32[]{:S(2)}) collective-permute-start(bf16[2,1,128,2,512]{4,3,2,1,0:T(2,128)(2,1)S(1)} %get-tuple-element.78), channel_id=1, source_target_pairs={{0,16},{1,145},{2,18},{3,147},{4,20},{5,149},{6,22},{7,151},{8,24}... | collective-permute-start | bytes 1572872 | tf_op jit(solution)/shard_map/ppermute | solution.py:37
  40.0 6.2 %collective-permute-start.12 = (bf16[1,128,2,512]{3,2,1,0:T(2,128)(2,1)S(1)}, bf16[1,128,2,512]{3,2,1,0:T(2,128)(2,1)S(1)}, u32[]{:S(2)}, u32[]{:S(2)}) collective-permute-start(bf16[1,128,2,512]{3,2,1,0:T(2,128)(2,1)S(1)} %slice_bitcast_fusion.6), channel_id=1, source_target_pairs={{0,1},{1,0},{2,3},{3,2},{4,5},{5,4},{6,7},{7,6},{8,9},{9,8},{10,11... | collective-permute-start | bytes 786440 | tf_op jit(solution)/shard_map/ppermute | solution.py:37
  44.5 9.7 %collective-permute-start.15 = (f32[256,512]{1,0:T(8,128)S(1)}, f32[256,512]{1,0:T(8,128)S(1)}, u32[]{:S(2)}, u32[]{:S(2)}) collective-permute-start(f32[256,512]{1,0:T(8,128)S(1)} %term.9), channel_id=1, source_target_pairs={{0,14},{1,3},{2,0},{3,5},{4,2},{5,7},{6,4},{7,9},{8,6},{9,11},{10,... | collective-permute-start | bytes 1572872 | tf_op jit(solution)/shard_map/ppermute | solution.py:37
  46.2 10.4 %collective-permute-start.19 = (bf16[2,1,128,2,512]{4,3,2,1,0:T(2,128)(2,1)S(1)}, bf16[2,1,128,2,512]{4,3,2,1,0:T(2,128)(2,1)S(1)}, u32[]{:S(2)}, u32[]{:S(2)}) collective-permute-start(bf16[2,1,128,2,512]{4,3,2,1,0:T(2,128)(2,1)S(1)} %get-tuple-element.94), channel_id=1, source_target_pairs={{0,16},{1,145},{2,18},{3,147},{4,20},{5,149},{6,22},{7,151},{8,24}... | collective-permute-start | bytes 1572872 | tf_op jit(solution)/shard_map/ppermute | solution.py:37
  47.6 3.9 %collective-permute-start.14 = (bf16[1,128,2,512]{3,2,1,0:T(2,128)(2,1)S(1)}, bf16[1,128,2,512]{3,2,1,0:T(2,128)(2,1)S(1)}, u32[]{:S(2)}, u32[]{:S(2)}) collective-permute-start(bf16[1,128,2,512]{3,2,1,0:T(2,128)(2,1)S(1)} %slice_bitcast_fusion.5), channel_id=1, source_target_pairs={{0,1},{1,0},{2,3},{3,2},{4,5},{5,4},{6,7},{7,6},{8,9},{9,8},{10,11... | collective-permute-start | bytes 786440 | tf_op jit(solution)/shard_map/ppermute | solution.py:37
  50.4 10.4 %collective-permute-start.21 = (f32[256,512]{1,0:T(8,128)S(1)}, f32[256,512]{1,0:T(8,128)S(1)}, u32[]{:S(2)}, u32[]{:S(2)}) collective-permute-start(f32[256,512]{1,0:T(8,128)S(1)} %term.10), channel_id=1, source_target_pairs={{0,2},{1,15},{2,4},{3,1},{4,6},{5,3},{6,8},{7,5},{8,10},{9,7},{10,... | collective-permute-start | bytes 1572872 | tf_op jit(solution)/shard_map/ppermute | solution.py:37
  50.4 11.9 %collective-permute-start.18 = (bf16[2,1,128,2,512]{4,3,2,1,0:T(2,128)(2,1)S(1)}, bf16[2,1,128,2,512]{4,3,2,1,0:T(2,128)(2,1)S(1)}, u32[]{:S(2)}, u32[]{:S(2)}) collective-permute-start(bf16[2,1,128,2,512]{4,3,2,1,0:T(2,128)(2,1)S(1)} %get-tuple-element.93), channel_id=1, source_target_pairs={{0,16},{1,145},{2,18},{3,147},{4,20},{5,149},{6,22},{7,151},{8,24}... | collective-permute-start | bytes 1572872 | tf_op jit(solution)/shard_map/ppermute | solution.py:37
  56.9 9.7 %collective-permute-start.23 = (f32[256,512]{1,0:T(8,128)S(1)}, f32[256,512]{1,0:T(8,128)S(1)}, u32[]{:S(2)}, u32[]{:S(2)}) collective-permute-start(f32[256,512]{1,0:T(8,128)S(1)} %term.11), channel_id=1, source_target_pairs={{0,14},{1,3},{2,0},{3,5},{4,2},{5,7},{6,4},{7,9},{8,6},{9,11},{10,... | collective-permute-start | bytes 1572872 | tf_op jit(solution)/shard_map/ppermute | solution.py:37
  58.3 10.4 %collective-permute-start.17 = (bf16[2,1,128,2,512]{4,3,2,1,0:T(2,128)(2,1)S(1)}, bf16[2,1,128,2,512]{4,3,2,1,0:T(2,128)(2,1)S(1)}, u32[]{:S(2)}, u32[]{:S(2)}) collective-permute-start(bf16[2,1,128,2,512]{4,3,2,1,0:T(2,128)(2,1)S(1)} %get-tuple-element.92), channel_id=1, source_target_pairs={{0,16},{1,145},{2,18},{3,147},{4,20},{5,149},{6,22},{7,151},{8,24}... | collective-permute-start | bytes 1572872 | tf_op jit(solution)/shard_map/ppermute | solution.py:37
  62.5 10.5 %collective-permute-start.25 = (f32[256,512]{1,0:T(8,128)S(1)}, f32[256,512]{1,0:T(8,128)S(1)}, u32[]{:S(2)}, u32[]{:S(2)}) collective-permute-start(f32[256,512]{1,0:T(8,128)S(1)} %term.12), channel_id=1, source_target_pairs={{0,2},{1,15},{2,4},{3,1},{4,6},{5,3},{6,8},{7,5},{8,10},{9,7},{10,... | collective-permute-start | bytes 1572872 | tf_op jit(solution)/shard_map/ppermute | solution.py:37
  62.9 11.5 %collective-permute-start.16 = (bf16[2,1,128,2,512]{4,3,2,1,0:T(2,128)(2,1)S(1)}, bf16[2,1,128,2,512]{4,3,2,1,0:T(2,128)(2,1)S(1)}, u32[]{:S(2)}, u32[]{:S(2)}) collective-permute-start(bf16[2,1,128,2,512]{4,3,2,1,0:T(2,128)(2,1)S(1)} %get-tuple-element.91), channel_id=1, source_target_pairs={{0,16},{1,145},{2,18},{3,147},{4,20},{5,149},{6,22},{7,151},{8,24}... | collective-permute-start | bytes 1572872 | tf_op jit(solution)/shard_map/ppermute | solution.py:37
  69.0 12.5 %collective-permute-start.28 = (f32[256,512]{1,0:T(8,128)S(1)}, f32[256,512]{1,0:T(8,128)S(1)}, u32[]{:S(2)}, u32[]{:S(2)}) collective-permute-start(f32[256,512]{1,0:T(8,128)S(1)} %term.13), channel_id=1, source_target_pairs={{0,14},{1,3},{2,0},{3,5},{4,2},{5,7},{6,4},{7,9},{8,6},{9,11},{10,... | collective-permute-start | bytes 1572872 | tf_op jit(solution)/shard_map/ppermute | solution.py:37
  74.3 10.4 %collective-permute-start.27 = (f32[256,512]{1,0:T(8,128)S(1)}, f32[256,512]{1,0:T(8,128)S(1)}, u32[]{:S(2)}, u32[]{:S(2)}) collective-permute-start(f32[256,512]{1,0:T(8,128)S(1)} %term.14), channel_id=1, source_target_pairs={{0,2},{1,15},{2,4},{3,1},{4,6},{5,3},{6,8},{7,5},{8,10},{9,7},{10,... | collective-permute-start | bytes 1572872 | tf_op jit(solution)/shard_map/ppermute | solution.py:37
  (8 other events, 32.7 us)

commit v4 on v3

--- a/solution.py
+++ b/solution.py
@@ -225,23 +225,24 @@
     fars = [across(far)]
     matrix, pieces[0] = lax.optimization_barrier((system_matrix, pieces[0]))
     early, late = MESSAGES[0], range(len(MESSAGES[0]), Z)
-    *far, own, core = cut_matrix(where, matrix, MESSAGES[1:2], ((early, 0), (range(Z), 1)))
+    *far, own, core = cut_matrix(where, matrix, MESSAGES[1:3], ((early, 0), (range(Z), 1)))
     sent = add_rows(where, offsets, patch_ids, [raw] + pieces)
     (same, plus, minus, other), fars[0], core = lax.optimization_barrier((sent, fars[0], core))
     rest = [shift(plus, dx=1), shift(minus, dx=-1), shift(other, dx=2)]
     core = shift(core, dc=1)
     cross = shift(fars[0][1], dc=1)
     flats = [flatten((own, (s,)), (core, (s,)), (fars[0], (0, s)), (cross, (s,))) for s in early]
-    far[0], rest[0] = lax.optimization_barrier((far[0], rest[0]))
-    fars.append(across(far[0]))
+    for i in range(2):
+        far[i], rest[i] = lax.optimization_barrier((far[i], rest[i]))
+        fars.append(across(far[i]))
     flats, rest = lax.optimization_barrier((flats, rest))
     from_left, from_right, across_two = rest
     el = expand(same, across_two, from_left, from_right)
     matrix, el = lax.optimization_barrier((matrix, el))
     ec = shift(el, dc=1)
-    *more, own = cut_matrix(where, matrix, MESSAGES[2:], ((late, 0),))
+    *more, own = cut_matrix(where, matrix, MESSAGES[3:], ((late, 0),))
     far += more
-    fars += [across(f) for f in far[1:3]]
+    fars.append(across(far[2]))
 
     sums = [None, None]
     for s in range(Z):

time: 86.3 us -> 86.7 us (level)
  waiting for transfers between devices: 40.5 us -> 42.8 us
  starting transfers between devices: 26.9 us -> 24.7 us
    ppermute x29, waiting for transfers between devices: 40.5 us -> 42.8 us  [shift(): return lax.ppermute(array, ('grp', 'freq'), pairs)]
    ppermute x29, starting transfers between devices: 26.9 us -> 24.7 us  [shift(): return lax.ppermute(array, ('grp', 'freq'), pairs)]
  transfers between devices with their start and end apart: 29 -> 29, of which waited for: 24 -> 20; matrix products, arithmetic and copies ran while one was open for 2% -> 2% of each run, Pallas kernels for 15% -> 15%
where the time goes in v4:
time: 86.7 us; the launch traced here: 85.8 us
  waiting for transfers between devices  42.8 us (49%)
  starting transfers between devices  24.7 us (28%)
  Pallas kernels  16.4 us (19%)
  local copies, waits for them, and re-layouts  1.55 us (2%)
    ppermute x29, waiting for transfers between devices, shift(): return lax.ppermute(array, ('grp', 'freq'), pairs)  42.8 us
    ppermute x29, starting transfers between devices, shift(): return lax.ppermute(array, ('grp', 'freq'), pairs)  24.7 us
    pallas_call x3, Pallas kernels, cut_matrix(): pl.pallas_call(kernel, in_specs=[SMEM, pl.BlockSpec(memory_space=pltpu.HB...  7.36 us
    pallas_call x8, Pallas kernels, term(): pl.pallas_call(term_kernel, out_shape=jax.ShapeDtypeStruct((el.shape[2],...  5.61 us
  transfers between devices with their start and end apart: 29, of which 20 were waited for; matrix products, arithmetic and copies ran while one was open for 2% of the time, Pallas kernels for 15%

profile of v4, /device:TPU:24, one launch (start us, length us, event | category | flops | bytes accessed | tf_op | source)
XLA Modules:
  0.0 85.8 jit_solution(8746292224756279206)
XLA Ops:
  0.1 1.8 %cut_matrix.3 = bf16[2,2,128,2,512]{4,3,2,1,0:T(2,128)(2,1)S(1)} custom-call(s32[5]{0:T(128)S(1)} %stack.23.place_ref, bf16[128,2,16384]{2,1,0:T(2,128)(2,1)} %src.3), custom_call_target="tpu_custom_call" | custom-call | flops 1000 | bytes 1000 | tf_op jit(solution)/shard_map/cut_matrix/pallas_call | solution.py:146
  1.9 1.6 %collective-permute-start.3 = (bf16[2,2,128,2,512]{4,3,2,1,0:T(2,128)(2,1)S(1)}, bf16[2,2,128,2,512]{4,3,2,1,0:T(2,128)(2,1)S(1)}, u32[]{:S(2)}, u32[]{:S(2)}) collective-permute-start(bf16[2,2,128,2,512]{4,3,2,1,0:T(2,128)(2,1)S(1)} %cut_matrix.3), channel_id=1, source_target_pairs={{0,16},{1,145},{2,18},{3,147},{4,20},{5,149},{6,22},{7,151},{8,24}... | collective-permute-start | bytes 3145736 | tf_op jit(solution)/shard_map/ppermute | solution.py:37
  4.2 2.5 %collective-permute-start.2 = (bf16[8,64,128]{2,1,0:T(8,128)(2,1)S(1)}, bf16[8,64,128]{2,1,0:T(8,128)(2,1)S(1)}, u32[]{:S(2)}, u32[]{:S(2)}) collective-permute-start(bf16[8,64,128]{2,1,0:T(8,128)(2,1)S(1)} %bitcast.22), channel_id=1, source_target_pairs={{0,32},{1,33},{2,34},{3,35},{4,36},{5,37},{6,38},{7,39},{8,40},{9,... | collective-permute-start | bytes 393224 | tf_op jit(solution)/shard_map/ppermute | solution.py:37
  6.7 4.2 %collective-permute-done.r1 = bf16[8,64,128]{2,1,0:T(8,128)(2,1)S(1)} collective-permute-done((bf16[8,64,128]{2,1,0:T(8,128)(2,1)S(1)}, bf16[8,64,128]{2,1,0:T(8,128)(2,1)S(1)}, u32[]{:S(2)}, u32[]{:S(2)}) %collective-permute-start) | collective-permute-done | bytes 131104 | tf_op jit(solution)/shard_map/ppermute | solution.py:37
  10.9 2.8 %cut_matrix.4 = (bf16[2,1,128,2,512]{4,3,2,1,0:T(2,128)(2,1)S(1)}, bf16[2,1,128,2,512]{4,3,2,1,0:T(2,128)(2,1)S(1)}, bf16[2,128,2,512]{3,2,1,0:T(2,128)(2,1)S(1)}, bf16[8,128,2,512]{3,2,1,0:T(2,128)(2,1)S(1)}) custom-call(s32[5]{0:T(128)S(1)} %stack.23.place_ref, bf16[128,2,16384]{2,1,0:T(2,128)(2,1)} %src.3), custom_call_target="tpu_custom_call" | custom-call | flops 1000 | bytes 1000 | tf_op jit(solution)/shard_map/cut_matrix/pallas_call | solution.py:146
  14.9 3.1 %collective-permute-done.3.refs_2_ = bf16[2,2,128,2,512]{4,3,2,1,0:T(2,128)(2,1)S(1)} collective-permute-done((bf16[2,2,128,2,512]{4,3,2,1,0:T(2,128)(2,1)S(1)}, bf16[2,2,128,2,512]{4,3,2,1,0:T(2,128)(2,1)S(1)}, u32[]{:S(2)}, u32[]{:S(2)}) %collective-permute-start.3) | collective-permute-done | bytes 1048608 | tf_op jit(solution)/shard_map/ppermute | solution.py:37
  19.2 3.0 %collective-permute-start.7 = (f32[4,64,128]{2,1,0:T(8,128)S(1)}, f32[4,64,128]{2,1,0:T(8,128)S(1)}, u32[]{:S(2)}, u32[]{:S(2)}) collective-permute-start(f32[4,64,128]{2,1,0:T(8,128)S(1)} %get-tuple-element.72), channel_id=1, source_target_pairs={{0,144},{1,145},{2,146},{3,147},{4,148},{5,149},{6,150},{7,151},{8... | collective-permute-start | bytes 393224 | tf_op jit(solution)/shard_map/ppermute | solution.py:37
  22.8 2.9 %collective-permute-done.6.b0 = f32[4,64,128]{2,1,0:T(8,128)S(1)} collective-permute-done((f32[4,64,128]{2,1,0:T(8,128)S(1)}, f32[4,64,128]{2,1,0:T(8,128)S(1)}, u32[]{:S(2)}, u32[]{:S(2)}) %collective-permute-start.6) | collective-permute-done | bytes 131104 | tf_op jit(solution)/shard_map/ppermute | solution.py:37
  25.7 2.1 %collective-permute-done.7.b1 = f32[4,64,128]{2,1,0:T(8,128)S(1)} collective-permute-done((f32[4,64,128]{2,1,0:T(8,128)S(1)}, f32[4,64,128]{2,1,0:T(8,128)S(1)}, u32[]{:S(2)}, u32[]{:S(2)}) %collective-permute-start.7) | collective-permute-done | bytes 131104 | tf_op jit(solution)/shard_map/ppermute | solution.py:37
  32.0 2.0 %collective-permute-start.13 = (f32[256,512]{1,0:T(8,128)S(1)}, f32[256,512]{1,0:T(8,128)S(1)}, u32[]{:S(2)}, u32[]{:S(2)}) collective-permute-start(f32[256,512]{1,0:T(8,128)S(1)} %term.8), channel_id=1, source_target_pairs={{0,2},{1,15},{2,4},{3,1},{4,6},{5,3},{6,8},{7,5},{8,10},{9,7},{10,... | collective-permute-start | bytes 1572872 | tf_op jit(solution)/shard_map/ppermute | solution.py:37
  34.7 2.8 %cut_matrix.5 = (bf16[2,1,128,2,512]{4,3,2,1,0:T(2,128)(2,1)S(1)}, bf16[2,1,128,2,512]{4,3,2,1,0:T(2,128)(2,1)S(1)}, bf16[2,1,128,2,512]{4,3,2,1,0:T(2,128)(2,1)...) custom-call(s32[5]{0:T(128)S(1)} %stack.23.place_ref, bf16[128,2,16384]{2,1,0:T(2,128)(2,1)} %src.3), custom_call_target="tpu_custom_call" | custom-call | flops 1000 | bytes 1000 | tf_op jit(solution)/shard_map/cut_matrix/pallas_call | solution.py:146
  38.2 1.7 %collective-permute-done.11.refs_2_ = bf16[2,1,128,2,512]{4,3,2,1,0:T(2,128)(2,1)S(1)} collective-permute-done((bf16[2,1,128,2,512]{4,3,2,1,0:T(2,128)(2,1)S(1)}, bf16[2,1,128,2,512]{4,3,2,1,0:T(2,128)(2,1)S(1)}, u32[]{:S(2)}, u32[]{:S(2)}) %collective-permute-start.11) | collective-permute-done | bytes 524320 | tf_op jit(solution)/shard_map/ppermute | solution.py:37
  40.0 4.4 %collective-permute-start.12 = (bf16[1,128,2,512]{3,2,1,0:T(2,128)(2,1)S(1)}, bf16[1,128,2,512]{3,2,1,0:T(2,128)(2,1)S(1)}, u32[]{:S(2)}, u32[]{:S(2)}) collective-permute-start(bf16[1,128,2,512]{3,2,1,0:T(2,128)(2,1)S(1)} %slice_bitcast_fusion.6), channel_id=1, source_target_pairs={{0,1},{1,0},{2,3},{3,2},{4,5},{5,4},{6,7},{7,6},{8,9},{9,8},{10,11... | collective-permute-start | bytes 786440 | tf_op jit(solution)/shard_map/ppermute | solution.py:37
  44.5 1.8 %collective-permute-start.15 = (f32[256,512]{1,0:T(8,128)S(1)}, f32[256,512]{1,0:T(8,128)S(1)}, u32[]{:S(2)}, u32[]{:S(2)}) collective-permute-start(f32[256,512]{1,0:T(8,128)S(1)} %term.9), channel_id=1, source_target_pairs={{0,14},{1,3},{2,0},{3,5},{4,2},{5,7},{6,4},{7,9},{8,6},{9,11},{10,... | collective-permute-start | bytes 1572872 | tf_op jit(solution)/shard_map/ppermute | solution.py:37
  49.0 7.7 %collective-permute-done.15.rest_0_ = f32[256,512]{1,0:T(8,128)S(1)} collective-permute-done((f32[256,512]{1,0:T(8,128)S(1)}, f32[256,512]{1,0:T(8,128)S(1)}, u32[]{:S(2)}, u32[]{:S(2)}) %collective-permute-start.15) | collective-permute-done | bytes 524320 | tf_op jit(solution)/shard_map/ppermute | solution.py:37
  60.3 1.9 %collective-permute-done.18.refs_2_ = bf16[2,1,128,2,512]{4,3,2,1,0:T(2,128)(2,1)S(1)} collective-permute-done((bf16[2,1,128,2,512]{4,3,2,1,0:T(2,128)(2,1)S(1)}, bf16[2,1,128,2,512]{4,3,2,1,0:T(2,128)(2,1)S(1)}, u32[]{:S(2)}, u32[]{:S(2)}) %collective-permute-start.18) | collective-permute-done | bytes 524320 | tf_op jit(solution)/shard_map/ppermute | solution.py:37
  62.9 1.2 %collective-permute-done.22.refs_3_ = bf16[1,128,2,512]{3,2,1,0:T(2,128)(2,1)S(1)} collective-permute-done((bf16[1,128,2,512]{3,2,1,0:T(2,128)(2,1)S(1)}, bf16[1,128,2,512]{3,2,1,0:T(2,128)(2,1)S(1)}, u32[]{:S(2)}, u32[]{:S(2)}) %collective-permute-start.22) | collective-permute-done | bytes 262176 | tf_op jit(solution)/shard_map/ppermute | solution.py:37
  64.2 4.2 %collective-permute-done.23.rest_0_ = f32[256,512]{1,0:T(8,128)S(1)} collective-permute-done((f32[256,512]{1,0:T(8,128)S(1)}, f32[256,512]{1,0:T(8,128)S(1)}, u32[]{:S(2)}, u32[]{:S(2)}) %collective-permute-start.23) | collective-permute-done | bytes 524320 | tf_op jit(solution)/shard_map/ppermute | solution.py:37
  69.4 1.6 %collective-permute-start.28 = (f32[256,512]{1,0:T(8,128)S(1)}, f32[256,512]{1,0:T(8,128)S(1)}, u32[]{:S(2)}, u32[]{:S(2)}) collective-permute-start(f32[256,512]{1,0:T(8,128)S(1)} %term.13), channel_id=1, source_target_pairs={{0,14},{1,3},{2,0},{3,5},{4,2},{5,7},{6,4},{7,9},{8,6},{9,11},{10,... | collective-permute-start | bytes 1572872 | tf_op jit(solution)/shard_map/ppermute | solution.py:37
  71.1 2.2 %collective-permute-done.25.rest_0_ = f32[256,512]{1,0:T(8,128)S(1)} collective-permute-done((f32[256,512]{1,0:T(8,128)S(1)}, f32[256,512]{1,0:T(8,128)S(1)}, u32[]{:S(2)}, u32[]{:S(2)}) %collective-permute-start.25) | collective-permute-done | bytes 524320 | tf_op jit(solution)/shard_map/ppermute | solution.py:37
  74.4 1.5 %collective-permute-start.27 = (f32[256,512]{1,0:T(8,128)S(1)}, f32[256,512]{1,0:T(8,128)S(1)}, u32[]{:S(2)}, u32[]{:S(2)}) collective-permute-start(f32[256,512]{1,0:T(8,128)S(1)} %term.14), channel_id=1, source_target_pairs={{0,2},{1,15},{2,4},{3,1},{4,6},{5,3},{6,8},{7,5},{8,10},{9,7},{10,... | collective-permute-start | bytes 1572872 | tf_op jit(solution)/shard_map/ppermute | solution.py:37
  76.2 1.5 %collective-permute-done.26.refs_3_ = bf16[1,128,2,512]{3,2,1,0:T(2,128)(2,1)S(1)} collective-permute-done((bf16[1,128,2,512]{3,2,1,0:T(2,128)(2,1)S(1)}, bf16[1,128,2,512]{3,2,1,0:T(2,128)(2,1)S(1)}, u32[]{:S(2)}, u32[]{:S(2)}) %collective-permute-start.26) | collective-permute-done | bytes 262176 | tf_op jit(solution)/shard_map/ppermute | solution.py:37
  78.5 3.0 %collective-permute-done.28.c = f32[256,512]{1,0:T(8,128)S(1)} collective-permute-done((f32[256,512]{1,0:T(8,128)S(1)}, f32[256,512]{1,0:T(8,128)S(1)}, u32[]{:S(2)}, u32[]{:S(2)}) %collective-permute-start.28) | collective-permute-done | bytes 524320 | tf_op jit(solution)/shard_map/ppermute | solution.py:37
  81.5 3.4 %collective-permute-done.27.b = f32[256,512]{1,0:T(8,128)S(1)} collective-permute-done((f32[256,512]{1,0:T(8,128)S(1)}, f32[256,512]{1,0:T(8,128)S(1)}, u32[]{:S(2)}, u32[]{:S(2)}) %collective-permute-start.27) | collective-permute-done | bytes 524320 | tf_op jit(solution)/shard_map/ppermute | solution.py:37
  (70 shorter events, 20.9 us)
Async XLA Ops:
  1.9 16.1 %collective-permute-start.3 = (bf16[2,2,128,2,512]{4,3,2,1,0:T(2,128)(2,1)S(1)}, bf16[2,2,128,2,512]{4,3,2,1,0:T(2,128)(2,1)S(1)}, u32[]{:S(2)}, u32[]{:S(2)}) collective-permute-start(bf16[2,2,128,2,512]{4,3,2,1,0:T(2,128)(2,1)S(1)} %cut_matrix.3), channel_id=1, source_target_pairs={{0,16},{1,145},{2,18},{3,147},{4,20},{5,149},{6,22},{7,151},{8,24}... | collective-permute-start | bytes 3145736 | tf_op jit(solution)/shard_map/ppermute | solution.py:37
  3.5 7.4 %collective-permute-start = (bf16[8,64,128]{2,1,0:T(8,128)(2,1)S(1)}, bf16[8,64,128]{2,1,0:T(8,128)(2,1)S(1)}, u32[]{:S(2)}, u32[]{:S(2)}) collective-permute-start(bf16[8,64,128]{2,1,0:T(8,128)(2,1)S(1)} %bitcast.21), channel_id=1, source_target_pairs={{0,96},{1,97},{2,98},{3,99},{4,100},{5,101},{6,102},{7,103},{8,104... | collective-permute-start | bytes 393224 | tf_op jit(solution)/shard_map/ppermute | solution.py:37
  4.2 9.5 %collective-permute-start.2 = (bf16[8,64,128]{2,1,0:T(8,128)(2,1)S(1)}, bf16[8,64,128]{2,1,0:T(8,128)(2,1)S(1)}, u32[]{:S(2)}, u32[]{:S(2)}) collective-permute-start(bf16[8,64,128]{2,1,0:T(8,128)(2,1)S(1)} %bitcast.22), channel_id=1, source_target_pairs={{0,32},{1,33},{2,34},{3,35},{4,36},{5,37},{6,38},{7,39},{8,40},{9,... | collective-permute-start | bytes 393224 | tf_op jit(solution)/shard_map/ppermute | solution.py:37
  6.7 7.2 %collective-permute-start.1 = (bf16[8,64,128]{2,1,0:T(8,128)(2,1)S(1)}, bf16[8,64,128]{2,1,0:T(8,128)(2,1)S(1)}, u32[]{:S(2)}, u32[]{:S(2)}) collective-permute-start(bf16[8,64,128]{2,1,0:T(8,128)(2,1)S(1)} %bitcast.23), channel_id=1, source_target_pairs={{0,64},{1,65},{2,66},{3,67},{4,68},{5,69},{6,70},{7,71},{8,72},{9,... | collective-permute-start | bytes 393224 | tf_op jit(solution)/shard_map/ppermute | solution.py:37
  18.0 9.7 %collective-permute-start.4 = (bf16[8,128,2,512]{3,2,1,0:T(2,128)(2,1)S(1)}, bf16[8,128,2,512]{3,2,1,0:T(2,128)(2,1)S(1)}, u32[]{:S(2)}, u32[]{:S(2)}) collective-permute-start(bf16[8,128,2,512]{3,2,1,0:T(2,128)(2,1)S(1)} %get-tuple-element.66), channel_id=1, source_target_pairs={{0,1},{1,0},{2,3},{3,2},{4,5},{5,4},{6,7},{7,6},{8,9},{9,8},{10,11... | collective-permute-start | bytes 6291464 | tf_op jit(solution)/shard_map/ppermute | solution.py:37
  18.4 9.4 %collective-permute-start.5 = (bf16[2,128,2,512]{3,2,1,0:T(2,128)(2,1)S(1)}, bf16[2,128,2,512]{3,2,1,0:T(2,128)(2,1)S(1)}, u32[]{:S(2)}, u32[]{:S(2)}) collective-permute-start(bf16[2,128,2,512]{3,2,1,0:T(2,128)(2,1)S(1)} %slice_bitcast_fusion), channel_id=1, source_target_pairs={{0,1},{1,0},{2,3},{3,2},{4,5},{5,4},{6,7},{7,6},{8,9},{9,8},{10,11... | collective-permute-start | bytes 1572872 | tf_op jit(solution)/shard_map/ppermute | solution.py:37
  19.0 6.7 %collective-permute-start.6 = (f32[4,64,128]{2,1,0:T(8,128)S(1)}, f32[4,64,128]{2,1,0:T(8,128)S(1)}, u32[]{:S(2)}, u32[]{:S(2)}) collective-permute-start(f32[4,64,128]{2,1,0:T(8,128)S(1)} %get-tuple-element.69), channel_id=1, source_target_pairs={{0,16},{1,17},{2,18},{3,19},{4,20},{5,21},{6,22},{7,23},{8,24},{9,... | collective-permute-start | bytes 393224 | tf_op jit(solution)/shard_map/ppermute | solution.py:37
  19.2 8.5 %collective-permute-start.7 = (f32[4,64,128]{2,1,0:T(8,128)S(1)}, f32[4,64,128]{2,1,0:T(8,128)S(1)}, u32[]{:S(2)}, u32[]{:S(2)}) collective-permute-start(f32[4,64,128]{2,1,0:T(8,128)S(1)} %get-tuple-element.72), channel_id=1, source_target_pairs={{0,144},{1,145},{2,146},{3,147},{4,148},{5,149},{6,150},{7,151},{8... | collective-permute-start | bytes 393224 | tf_op jit(solution)/shard_map/ppermute | solution.py:37
  22.2 6.5 %collective-permute-start.8 = (f32[4,64,128]{2,1,0:T(8,128)S(1)}, f32[4,64,128]{2,1,0:T(8,128)S(1)}, u32[]{:S(2)}, u32[]{:S(2)}) collective-permute-start(f32[4,64,128]{2,1,0:T(8,128)S(1)} %get-tuple-element.74), channel_id=1, source_target_pairs={{0,128},{1,129},{2,130},{3,131},{4,132},{5,133},{6,134},{7,135},{8... | collective-permute-start | bytes 393224 | tf_op jit(solution)/shard_map/ppermute | solution.py:37
  29.3 2.0 %collective-permute-start.9 = (bf16[2,2,256,256]{3,2,1,0:T(8,128)(2,1)S(1)}, bf16[2,2,256,256]{3,2,1,0:T(8,128)(2,1)S(1)}, u32[]{:S(2)}, u32[]{:S(2)}) collective-permute-start(bf16[2,2,256,256]{3,2,1,0:T(8,128)(2,1)S(1)} %expand.1.el), channel_id=1, source_target_pairs={{0,1},{1,0},{2,3},{3,2},{4,5},{5,4},{6,7},{7,6},{8,9},{9,8},{10,11... | collective-permute-start | bytes 1572872 | tf_op jit(solution)/shard_map/ppermute | solution.py:37
  29.4 10.5 %collective-permute-start.11 = (bf16[2,1,128,2,512]{4,3,2,1,0:T(2,128)(2,1)S(1)}, bf16[2,1,128,2,512]{4,3,2,1,0:T(2,128)(2,1)S(1)}, u32[]{:S(2)}, u32[]{:S(2)}) collective-permute-start(bf16[2,1,128,2,512]{4,3,2,1,0:T(2,128)(2,1)S(1)} %get-tuple-element.84), channel_id=1, source_target_pairs={{0,16},{1,145},{2,18},{3,147},{4,20},{5,149},{6,22},{7,151},{8,24}... | collective-permute-start | bytes 1572872 | tf_op jit(solution)/shard_map/ppermute | solution.py:37
  32.0 14.4 %collective-permute-start.13 = (f32[256,512]{1,0:T(8,128)S(1)}, f32[256,512]{1,0:T(8,128)S(1)}, u32[]{:S(2)}, u32[]{:S(2)}) collective-permute-start(f32[256,512]{1,0:T(8,128)S(1)} %term.8), channel_id=1, source_target_pairs={{0,2},{1,15},{2,4},{3,1},{4,6},{5,3},{6,8},{7,5},{8,10},{9,7},{10,... | collective-permute-start | bytes 1572872 | tf_op jit(solution)/shard_map/ppermute | solution.py:37
  34.0 13.1 %collective-permute-start.10 = (bf16[2,1,128,2,512]{4,3,2,1,0:T(2,128)(2,1)S(1)}, bf16[2,1,128,2,512]{4,3,2,1,0:T(2,128)(2,1)S(1)}, u32[]{:S(2)}, u32[]{:S(2)}) collective-permute-start(bf16[2,1,128,2,512]{4,3,2,1,0:T(2,128)(2,1)S(1)} %get-tuple-element.82), channel_id=1, source_target_pairs={{0,16},{1,145},{2,18},{3,147},{4,20},{5,149},{6,22},{7,151},{8,24}... | collective-permute-start | bytes 1572872 | tf_op jit(solution)/shard_map/ppermute | solution.py:37
  40.0 6.2 %collective-permute-start.12 = (bf16[1,128,2,512]{3,2,1,0:T(2,128)(2,1)S(1)}, bf16[1,128,2,512]{3,2,1,0:T(2,128)(2,1)S(1)}, u32[]{:S(2)}, u32[]{:S(2)}) collective-permute-start(bf16[1,128,2,512]{3,2,1,0:T(2,128)(2,1)S(1)} %slice_bitcast_fusion.6), channel_id=1, source_target_pairs={{0,1},{1,0},{2,3},{3,2},{4,5},{5,4},{6,7},{7,6},{8,9},{9,8},{10,11... | collective-permute-start | bytes 786440 | tf_op jit(solution)/shard_map/ppermute | solution.py:37
  44.5 12.3 %collective-permute-start.15 = (f32[256,512]{1,0:T(8,128)S(1)}, f32[256,512]{1,0:T(8,128)S(1)}, u32[]{:S(2)}, u32[]{:S(2)}) collective-permute-start(f32[256,512]{1,0:T(8,128)S(1)} %term.9), channel_id=1, source_target_pairs={{0,14},{1,3},{2,0},{3,5},{4,2},{5,7},{6,4},{7,9},{8,6},{9,11},{10,... | collective-permute-start | bytes 1572872 | tf_op jit(solution)/shard_map/ppermute | solution.py:37
  46.2 11.2 %collective-permute-start.19 = (bf16[2,1,128,2,512]{4,3,2,1,0:T(2,128)(2,1)S(1)}, bf16[2,1,128,2,512]{4,3,2,1,0:T(2,128)(2,1)S(1)}, u32[]{:S(2)}, u32[]{:S(2)}) collective-permute-start(bf16[2,1,128,2,512]{4,3,2,1,0:T(2,128)(2,1)S(1)} %get-tuple-element.98), channel_id=1, source_target_pairs={{0,16},{1,145},{2,18},{3,147},{4,20},{5,149},{6,22},{7,151},{8,24}... | collective-permute-start | bytes 1572872 | tf_op jit(solution)/shard_map/ppermute | solution.py:37
  47.4 12.2 %collective-permute-start.21 = (f32[256,512]{1,0:T(8,128)S(1)}, f32[256,512]{1,0:T(8,128)S(1)}, u32[]{:S(2)}, u32[]{:S(2)}) collective-permute-start(f32[256,512]{1,0:T(8,128)S(1)} %term.10), channel_id=1, source_target_pairs={{0,2},{1,15},{2,4},{3,1},{4,6},{5,3},{6,8},{7,5},{8,10},{9,7},{10,... | collective-permute-start | bytes 1572872 | tf_op jit(solution)/shard_map/ppermute | solution.py:37
  47.9 14.3 %collective-permute-start.18 = (bf16[2,1,128,2,512]{4,3,2,1,0:T(2,128)(2,1)S(1)}, bf16[2,1,128,2,512]{4,3,2,1,0:T(2,128)(2,1)S(1)}, u32[]{:S(2)}, u32[]{:S(2)}) collective-permute-start(bf16[2,1,128,2,512]{4,3,2,1,0:T(2,128)(2,1)S(1)} %get-tuple-element.97), channel_id=1, source_target_pairs={{0,16},{1,145},{2,18},{3,147},{4,20},{5,149},{6,22},{7,151},{8,24}... | collective-permute-start | bytes 1572872 | tf_op jit(solution)/shard_map/ppermute | solution.py:37
  57.8 10.6 %collective-permute-start.23 = (f32[256,512]{1,0:T(8,128)S(1)}, f32[256,512]{1,0:T(8,128)S(1)}, u32[]{:S(2)}, u32[]{:S(2)}) collective-permute-start(f32[256,512]{1,0:T(8,128)S(1)} %term.11), channel_id=1, source_target_pairs={{0,14},{1,3},{2,0},{3,5},{4,2},{5,7},{6,4},{7,9},{8,6},{9,11},{10,... | collective-permute-start | bytes 1572872 | tf_op jit(solution)/shard_map/ppermute | solution.py:37
  58.4 10.7 %collective-permute-start.17 = (bf16[2,1,128,2,512]{4,3,2,1,0:T(2,128)(2,1)S(1)}, bf16[2,1,128,2,512]{4,3,2,1,0:T(2,128)(2,1)S(1)}, u32[]{:S(2)}, u32[]{:S(2)}) collective-permute-start(bf16[2,1,128,2,512]{4,3,2,1,0:T(2,128)(2,1)S(1)} %get-tuple-element.96), channel_id=1, source_target_pairs={{0,16},{1,145},{2,18},{3,147},{4,20},{5,149},{6,22},{7,151},{8,24}... | collective-permute-start | bytes 1572872 | tf_op jit(solution)/shard_map/ppermute | solution.py:37
  62.5 10.8 %collective-permute-start.25 = (f32[256,512]{1,0:T(8,128)S(1)}, f32[256,512]{1,0:T(8,128)S(1)}, u32[]{:S(2)}, u32[]{:S(2)}) collective-permute-start(f32[256,512]{1,0:T(8,128)S(1)} %term.12), channel_id=1, source_target_pairs={{0,2},{1,15},{2,4},{3,1},{4,6},{5,3},{6,8},{7,5},{8,10},{9,7},{10,... | collective-permute-start | bytes 1572872 | tf_op jit(solution)/shard_map/ppermute | solution.py:37
  62.9 11.5 %collective-permute-start.16 = (bf16[2,1,128,2,512]{4,3,2,1,0:T(2,128)(2,1)S(1)}, bf16[2,1,128,2,512]{4,3,2,1,0:T(2,128)(2,1)S(1)}, u32[]{:S(2)}, u32[]{:S(2)}) collective-permute-start(bf16[2,1,128,2,512]{4,3,2,1,0:T(2,128)(2,1)S(1)} %get-tuple-element.95), channel_id=1, source_target_pairs={{0,16},{1,145},{2,18},{3,147},{4,20},{5,149},{6,22},{7,151},{8,24}... | collective-permute-start | bytes 1572872 | tf_op jit(solution)/shard_map/ppermute | solution.py:37
  69.4 12.1 %collective-permute-start.28 = (f32[256,512]{1,0:T(8,128)S(1)}, f32[256,512]{1,0:T(8,128)S(1)}, u32[]{:S(2)}, u32[]{:S(2)}) collective-permute-start(f32[256,512]{1,0:T(8,128)S(1)} %term.13), channel_id=1, source_target_pairs={{0,14},{1,3},{2,0},{3,5},{4,2},{5,7},{6,4},{7,9},{8,6},{9,11},{10,... | collective-permute-start | bytes 1572872 | tf_op jit(solution)/shard_map/ppermute | solution.py:37
  74.4 10.5 %collective-permute-start.27 = (f32[256,512]{1,0:T(8,128)S(1)}, f32[256,512]{1,0:T(8,128)S(1)}, u32[]{:S(2)}, u32[]{:S(2)}) collective-permute-start(f32[256,512]{1,0:T(8,128)S(1)} %term.14), channel_id=1, source_target_pairs={{0,2},{1,15},{2,4},{3,1},{4,6},{5,3},{6,8},{7,5},{8,10},{9,7},{10,... | collective-permute-start | bytes 1572872 | tf_op jit(solution)/shard_map/ppermute | solution.py:37
  (8 other events, 32.4 us)

commit v5 on v3

--- a/solution.py
+++ b/solution.py
@@ -10,7 +10,7 @@
 XH, Y, XL, Z, CORE = 2, 4, 2, 8, 2
 NX = XH * XL
 BR_DEV = 4
-TARGETS = (4, -3, 3, -2, 2, -1, 1, 0)
+TARGETS = (4, 3, -3, 2, -2, 1, -1, 0)
 MESSAGES = ((0, 1), (2,), (3,), (4,), (5,), (6,), (7,))
 PACE = (1, 2, 3)
 FREE = pl.CostEstimate(flops=1000, bytes_accessed=1000, transcendentals=0)
@@ -175,19 +175,23 @@
     )(*arrays)
 
 
-def term_kernel(el, ec, flat, *rest):
+def term_kernel(at, el, ec, flat, *rest):
     dot = functools.partial(jnp.dot, preferred_element_type=F32)
-    total = None if len(rest) == 1 else rest[0][...]
+    out = rest[-1]
+    total = None
     for n, e in enumerate((el.at[0], ec.at[0], el.at[1], ec.at[1])):
         for h in range(2):
             d = dot(e[h], flat[n])
             total = d if total is None else total + d
-    rest[-1][...] = total
-
-
-def term(el, ec, flat, *so_far):
-    return pl.pallas_call(
-        term_kernel,
+    out[...] = total
+    if len(rest) > 1:
+        columns = pl.ds(at, rest[0].shape[1])
+        out[:, columns] += rest[0][...]
+
+
+def term(el, ec, flat, *so_far, at=0):
+    return pl.pallas_call(
+        functools.partial(term_kernel, at),
         out_shape=jax.ShapeDtypeStruct((el.shape[2], flat.shape[2]), F32),
         in_specs=[VMEM] * (3 + len(so_far)),
         out_specs=VMEM,
@@ -247,19 +251,20 @@
     for s in range(Z):
         if s >= 2:
             fars[s - 1], total = lax.optimization_barrier((fars[s - 1], total))
-            sums[1 - s % 2] = shift(total, dz=2 * (s % 2) - 1, mirror=True)
+            sums[s % 2] = shift(total, dz=1 - 2 * (s % 2), mirror=True)
             cross = shift(fars[s - 1][1], dc=1)
             flats.append(flatten((own, (s - 2,)), (core, (s,)), (fars[s - 1], (0, 0)), (cross, (0,))))
-        if s == Z - 1:
+        if s in (0, Z - 1):
             total = term(el, ec, flats[s])
-            break
-        total = term(el, ec, flats[s], *sums[s % 2:s % 2 + 1] if s > 1 else ())
+        else:
+            total = term(el, ec, flats[s], sums[1 - s % 2], at=total.shape[1] // 2 if s == 2 else 0)
         if s in PACE:
             ahead, total = lax.optimization_barrier((far[len(fars) - 1], total))
             fars.append(across(ahead))
         if s == 0:
             flats[1], total = lax.optimization_barrier((flats[1], total))
-            sums[0] = shift(total, dz=1, mirror=True)
+            half = total.shape[1] // 2
+            sums = [shift(total[:, :half], dz=1, mirror=True), shift(total[:, half:], dz=-1, mirror=True)]
     volume = finish(total, *sums)
     return volume.reshape(frames, parts, BR_DEV, -1)
 

time: 86.3 us -> 95.7 us (1.11)
  waiting for transfers between devices: 40.5 us -> 47.6 us
  starting transfers between devices: 26.9 us -> 29.6 us
    ppermute x29 -> x30, waiting for transfers between devices: 40.5 us -> 47.6 us  [shift(): return lax.ppermute(array, ('grp', 'freq'), pairs)]
    ppermute x29 -> x30, starting transfers between devices: 26.9 us -> 29.6 us  [shift(): return lax.ppermute(array, ('grp', 'freq'), pairs)]
  transfers between devices with their start and end apart: 29 -> 30, of which waited for: 24 -> 16; matrix products, arithmetic and copies ran while one was open for 2% -> 2% of each run, Pallas kernels for 15% -> 14%
where the time goes in v5:
time: 95.7 us; the launch traced here: 95.5 us
  waiting for transfers between devices  47.6 us (50%)
  starting transfers between devices  29.6 us (31%)
  Pallas kernels  16.4 us (17%)
  local copies, waits for them, and re-layouts  1.59 us (2%)
    ppermute x30, waiting for transfers between devices, shift(): return lax.ppermute(array, ('grp', 'freq'), pairs)  47.6 us
    ppermute x30, starting transfers between devices, shift(): return lax.ppermute(array, ('grp', 'freq'), pairs)  29.6 us
    pallas_call x3, Pallas kernels, cut_matrix(): pl.pallas_call(kernel, in_specs=[SMEM, pl.BlockSpec(memory_space=pltpu.HB...  7.36 us
    pallas_call x8, Pallas kernels, term(): pl.pallas_call(functools.partial(term_kernel, at), out_shape=jax.ShapeDty...  5.61 us
  transfers between devices with their start and end apart: 30, of which 16 were waited for; matrix products, arithmetic and copies ran while one was open for 2% of the time, Pallas kernels for 14%

profile of v5, /device:TPU:24, one launch (start us, length us, event | category | flops | bytes accessed | tf_op | source)
XLA Modules:
  0.0 95.5 jit_solution(10796881731356438445)
XLA Ops:
  0.1 1.8 %cut_matrix.3 = bf16[2,2,128,2,512]{4,3,2,1,0:T(2,128)(2,1)S(1)} custom-call(s32[5]{0:T(128)S(1)} %stack.23.place_ref, bf16[128,2,16384]{2,1,0:T(2,128)(2,1)} %src.3), custom_call_target="tpu_custom_call" | custom-call | flops 1000 | bytes 1000 | tf_op jit(solution)/shard_map/cut_matrix/pallas_call | solution.py:146
  1.9 1.6 %collective-permute-start.3 = (bf16[2,2,128,2,512]{4,3,2,1,0:T(2,128)(2,1)S(1)}, bf16[2,2,128,2,512]{4,3,2,1,0:T(2,128)(2,1)S(1)}, u32[]{:S(2)}, u32[]{:S(2)}) collective-permute-start(bf16[2,2,128,2,512]{4,3,2,1,0:T(2,128)(2,1)S(1)} %cut_matrix.3), channel_id=1, source_target_pairs={{0,16},{1,145},{2,18},{3,147},{4,20},{5,149},{6,22},{7,151},{8,24}... | collective-permute-start | bytes 3145736 | tf_op jit(solution)/shard_map/ppermute | solution.py:37
  4.2 2.5 %collective-permute-start.2 = (bf16[8,64,128]{2,1,0:T(8,128)(2,1)S(1)}, bf16[8,64,128]{2,1,0:T(8,128)(2,1)S(1)}, u32[]{:S(2)}, u32[]{:S(2)}) collective-permute-start(bf16[8,64,128]{2,1,0:T(8,128)(2,1)S(1)} %bitcast.22), channel_id=1, source_target_pairs={{0,32},{1,33},{2,34},{3,35},{4,36},{5,37},{6,38},{7,39},{8,40},{9,... | collective-permute-start | bytes 393224 | tf_op jit(solution)/shard_map/ppermute | solution.py:37
  6.7 4.2 %collective-permute-done.r1 = bf16[8,64,128]{2,1,0:T(8,128)(2,1)S(1)} collective-permute-done((bf16[8,64,128]{2,1,0:T(8,128)(2,1)S(1)}, bf16[8,64,128]{2,1,0:T(8,128)(2,1)S(1)}, u32[]{:S(2)}, u32[]{:S(2)}) %collective-permute-start) | collective-permute-done | bytes 131104 | tf_op jit(solution)/shard_map/ppermute | solution.py:37
  10.9 2.6 %cut_matrix.4 = (bf16[2,1,128,2,512]{4,3,2,1,0:T(2,128)(2,1)S(1)}, bf16[2,128,2,512]{3,2,1,0:T(2,128)(2,1)S(1)}, bf16[8,128,2,512]{3,2,1,0:T(2,128)(2,1)S(1)}) custom-call(s32[5]{0:T(128)S(1)} %stack.23.place_ref, bf16[128,2,16384]{2,1,0:T(2,128)(2,1)} %src.3), custom_call_target="tpu_custom_call" | custom-call | flops 1000 | bytes 1000 | tf_op jit(solution)/shard_map/cut_matrix/pallas_call | solution.py:146
  14.9 3.1 %collective-permute-done.3.refs_2_ = bf16[2,2,128,2,512]{4,3,2,1,0:T(2,128)(2,1)S(1)} collective-permute-done((bf16[2,2,128,2,512]{4,3,2,1,0:T(2,128)(2,1)S(1)}, bf16[2,2,128,2,512]{4,3,2,1,0:T(2,128)(2,1)S(1)}, u32[]{:S(2)}, u32[]{:S(2)}) %collective-permute-start.3) | collective-permute-done | bytes 1048608 | tf_op jit(solution)/shard_map/ppermute | solution.py:37
  19.2 3.0 %collective-permute-start.7 = (f32[4,64,128]{2,1,0:T(8,128)S(1)}, f32[4,64,128]{2,1,0:T(8,128)S(1)}, u32[]{:S(2)}, u32[]{:S(2)}) collective-permute-start(f32[4,64,128]{2,1,0:T(8,128)S(1)} %get-tuple-element.69), channel_id=1, source_target_pairs={{0,144},{1,145},{2,146},{3,147},{4,148},{5,149},{6,150},{7,151},{8... | collective-permute-start | bytes 393224 | tf_op jit(solution)/shard_map/ppermute | solution.py:37
  22.8 2.9 %collective-permute-done.6.b0 = f32[4,64,128]{2,1,0:T(8,128)S(1)} collective-permute-done((f32[4,64,128]{2,1,0:T(8,128)S(1)}, f32[4,64,128]{2,1,0:T(8,128)S(1)}, u32[]{:S(2)}, u32[]{:S(2)}) %collective-permute-start.6) | collective-permute-done | bytes 131104 | tf_op jit(solution)/shard_map/ppermute | solution.py:37
  25.9 1.8 %collective-permute-done.7.b1 = f32[4,64,128]{2,1,0:T(8,128)S(1)} collective-permute-done((f32[4,64,128]{2,1,0:T(8,128)S(1)}, f32[4,64,128]{2,1,0:T(8,128)S(1)}, u32[]{:S(2)}, u32[]{:S(2)}) %collective-permute-start.7) | collective-permute-done | bytes 131104 | tf_op jit(solution)/shard_map/ppermute | solution.py:37
  30.2 1.1 %collective-permute-done.9.ec = bf16[2,2,256,256]{3,2,1,0:T(8,128)(2,1)S(1)} collective-permute-done((bf16[2,2,256,256]{3,2,1,0:T(8,128)(2,1)S(1)}, bf16[2,2,256,256]{3,2,1,0:T(8,128)(2,1)S(1)}, u32[]{:S(2)}, u32[]{:S(2)}) %collective-permute-start.9) | collective-permute-done | bytes 524320 | tf_op jit(solution)/shard_map/ppermute | solution.py:37
  32.0 2.0 %collective-permute-start.12 = (f32[256,256]{1,0:T(8,128)S(1)}, f32[256,256]{1,0:T(8,128)S(1)}, u32[]{:S(2)}, u32[]{:S(2)}) collective-permute-start(f32[256,256]{1,0:T(8,128)S(1)} %get-tuple-element.106), channel_id=1, source_target_pairs={{0,2},{1,15},{2,4},{3,1},{4,6},{5,3},{6,8},{7,5},{8,10},{9,7},{10,... | collective-permute-start | bytes 786440 | tf_op jit(solution)/shard_map/ppermute | solution.py:37
  34.0 3.0 %cut_matrix.5 = (bf16[2,1,128,2,512]{4,3,2,1,0:T(2,128)(2,1)S(1)}, bf16[2,1,128,2,512]{4,3,2,1,0:T(2,128)(2,1)S(1)}, bf16[2,1,128,2,512]{4,3,2,1,0:T(2,128)(2,1)...) custom-call(s32[5]{0:T(128)S(1)} %stack.23.place_ref, ...), custom_call_target="tpu_custom_call" | custom-call | flops 1000 | bytes 1000 | tf_op jit(solution)/shard_map/cut_matrix/pallas_call | solution.py:146
  37.8 4.5 %collective-permute-done.12.rest_0_ = f32[256,256]{1,0:T(8,128)S(1)} collective-permute-done((f32[256,256]{1,0:T(8,128)S(1)}, f32[256,256]{1,0:T(8,128)S(1)}, u32[]{:S(2)}, u32[]{:S(2)}) %collective-permute-start.12) | collective-permute-done | bytes 262176 | tf_op jit(solution)/shard_map/ppermute | solution.py:37
  43.2 1.3 %collective-permute-start.13 = (bf16[1,128,2,512]{3,2,1,0:T(2,128)(2,1)S(1)}, bf16[1,128,2,512]{3,2,1,0:T(2,128)(2,1)S(1)}, u32[]{:S(2)}, u32[]{:S(2)}) collective-permute-start(bf16[1,128,2,512]{3,2,1,0:T(2,128)(2,1)S(1)} %slice_bitcast_fusion.6), channel_id=1, source_target_pairs={{0,1},{1,0},{2,3},{3,2},{4,5},{5,4},{6,7},{7,6},{8,9},{9,8},{10,11... | collective-permute-start | bytes 786440 | tf_op jit(solution)/shard_map/ppermute | solution.py:37
  44.5 2.4 %collective-permute-start.14 = (f32[256,256]{1,0:T(8,128)S(1)}, f32[256,256]{1,0:T(8,128)S(1)}, u32[]{:S(2)}, u32[]{:S(2)}) collective-permute-start(f32[256,256]{1,0:T(8,128)S(1)} %get-tuple-element.105), channel_id=1, source_target_pairs={{0,14},{1,3},{2,0},{3,5},{4,2},{5,7},{6,4},{7,9},{8,6},{9,11},{10,... | collective-permute-start | bytes 786440 | tf_op jit(solution)/shard_map/ppermute | solution.py:37
  47.1 6.6 %collective-permute-done.14.rest_0_ = f32[256,256]{1,0:T(8,128)S(1)} collective-permute-done((f32[256,256]{1,0:T(8,128)S(1)}, f32[256,256]{1,0:T(8,128)S(1)}, u32[]{:S(2)}, u32[]{:S(2)}) %collective-permute-start.14) | collective-permute-done | bytes 262176 | tf_op jit(solution)/shard_map/ppermute | solution.py:37
  54.7 3.7 %collective-permute-start.22 = (f32[256,512]{1,0:T(8,128)S(1)}, f32[256,512]{1,0:T(8,128)S(1)}, u32[]{:S(2)}, u32[]{:S(2)}) collective-permute-start(f32[256,512]{1,0:T(8,128)S(1)} %term.10), channel_id=1, source_target_pairs={{0,14},{1,3},{2,0},{3,5},{4,2},{5,7},{6,4},{7,9},{8,6},{9,11},{10,... | collective-permute-start | bytes 1572872 | tf_op jit(solution)/shard_map/ppermute | solution.py:37
  61.2 7.3 %collective-permute-done.22.rest_0_ = f32[256,512]{1,0:T(8,128)S(1)} collective-permute-done((f32[256,512]{1,0:T(8,128)S(1)}, f32[256,512]{1,0:T(8,128)S(1)}, u32[]{:S(2)}, u32[]{:S(2)}) %collective-permute-start.22) | collective-permute-done | bytes 524320 | tf_op jit(solution)/shard_map/ppermute | solution.py:37
  69.6 3.8 %collective-permute-start.26 = (f32[256,512]{1,0:T(8,128)S(1)}, f32[256,512]{1,0:T(8,128)S(1)}, u32[]{:S(2)}, u32[]{:S(2)}) collective-permute-start(f32[256,512]{1,0:T(8,128)S(1)} %term.12), channel_id=1, source_target_pairs={{0,14},{1,3},{2,0},{3,5},{4,2},{5,7},{6,4},{7,9},{8,6},{9,11},{10,... | collective-permute-start | bytes 1572872 | tf_op jit(solution)/shard_map/ppermute | solution.py:37
  75.0 1.2 %collective-permute-done.25.refs_3_ = bf16[1,128,2,512]{3,2,1,0:T(2,128)(2,1)S(1)} collective-permute-done((bf16[1,128,2,512]{3,2,1,0:T(2,128)(2,1)S(1)}, bf16[1,128,2,512]{3,2,1,0:T(2,128)(2,1)S(1)}, u32[]{:S(2)}, u32[]{:S(2)}) %collective-permute-start.25) | collective-permute-done | bytes 262176 | tf_op jit(solution)/shard_map/ppermute | solution.py:37
  76.4 7.1 %collective-permute-done.26.rest_0_ = f32[256,512]{1,0:T(8,128)S(1)} collective-permute-done((f32[256,512]{1,0:T(8,128)S(1)}, f32[256,512]{1,0:T(8,128)S(1)}, u32[]{:S(2)}, u32[]{:S(2)}) %collective-permute-start.26) | collective-permute-done | bytes 524320 | tf_op jit(solution)/shard_map/ppermute | solution.py:37
  84.2 3.8 %collective-permute-start.29 = (f32[256,512]{1,0:T(8,128)S(1)}, f32[256,512]{1,0:T(8,128)S(1)}, u32[]{:S(2)}, u32[]{:S(2)}) collective-permute-start(f32[256,512]{1,0:T(8,128)S(1)} %term.14), channel_id=1, source_target_pairs={{0,14},{1,3},{2,0},{3,5},{4,2},{5,7},{6,4},{7,9},{8,6},{9,11},{10,... | collective-permute-start | bytes 1572872 | tf_op jit(solution)/shard_map/ppermute | solution.py:37
  88.2 1.5 %collective-permute-done.27.refs_3_ = bf16[1,128,2,512]{3,2,1,0:T(2,128)(2,1)S(1)} collective-permute-done((bf16[1,128,2,512]{3,2,1,0:T(2,128)(2,1)S(1)}, bf16[1,128,2,512]{3,2,1,0:T(2,128)(2,1)S(1)}, u32[]{:S(2)}, u32[]{:S(2)}) %collective-permute-start.27) | collective-permute-done | bytes 262176 | tf_op jit(solution)/shard_map/ppermute | solution.py:37
  90.6 4.1 %collective-permute-done.29.c = f32[256,512]{1,0:T(8,128)S(1)} collective-permute-done((f32[256,512]{1,0:T(8,128)S(1)}, f32[256,512]{1,0:T(8,128)S(1)}, u32[]{:S(2)}, u32[]{:S(2)}) %collective-permute-start.29) | collective-permute-done | bytes 524320 | tf_op jit(solution)/shard_map/ppermute | solution.py:37
  (73 shorter events, 18.5 us)
Async XLA Ops:
  1.9 16.1 %collective-permute-start.3 = (bf16[2,2,128,2,512]{4,3,2,1,0:T(2,128)(2,1)S(1)}, bf16[2,2,128,2,512]{4,3,2,1,0:T(2,128)(2,1)S(1)}, u32[]{:S(2)}, u32[]{:S(2)}) collective-permute-start(bf16[2,2,128,2,512]{4,3,2,1,0:T(2,128)(2,1)S(1)} %cut_matrix.3), channel_id=1, source_target_pairs={{0,16},{1,145},{2,18},{3,147},{4,20},{5,149},{6,22},{7,151},{8,24}... | collective-permute-start | bytes 3145736 | tf_op jit(solution)/shard_map/ppermute | solution.py:37
  3.5 7.4 %collective-permute-start = (bf16[8,64,128]{2,1,0:T(8,128)(2,1)S(1)}, bf16[8,64,128]{2,1,0:T(8,128)(2,1)S(1)}, u32[]{:S(2)}, u32[]{:S(2)}) collective-permute-start(bf16[8,64,128]{2,1,0:T(8,128)(2,1)S(1)} %bitcast.21), channel_id=1, source_target_pairs={{0,96},{1,97},{2,98},{3,99},{4,100},{5,101},{6,102},{7,103},{8,104... | collective-permute-start | bytes 393224 | tf_op jit(solution)/shard_map/ppermute | solution.py:37
  4.2 9.3 %collective-permute-start.2 = (bf16[8,64,128]{2,1,0:T(8,128)(2,1)S(1)}, bf16[8,64,128]{2,1,0:T(8,128)(2,1)S(1)}, u32[]{:S(2)}, u32[]{:S(2)}) collective-permute-start(bf16[8,64,128]{2,1,0:T(8,128)(2,1)S(1)} %bitcast.22), channel_id=1, source_target_pairs={{0,32},{1,33},{2,34},{3,35},{4,36},{5,37},{6,38},{7,39},{8,40},{9,... | collective-permute-start | bytes 393224 | tf_op jit(solution)/shard_map/ppermute | solution.py:37
  6.7 7.2 %collective-permute-start.1 = (bf16[8,64,128]{2,1,0:T(8,128)(2,1)S(1)}, bf16[8,64,128]{2,1,0:T(8,128)(2,1)S(1)}, u32[]{:S(2)}, u32[]{:S(2)}) collective-permute-start(bf16[8,64,128]{2,1,0:T(8,128)(2,1)S(1)} %bitcast.23), channel_id=1, source_target_pairs={{0,64},{1,65},{2,66},{3,67},{4,68},{5,69},{6,70},{7,71},{8,72},{9,... | collective-permute-start | bytes 393224 | tf_op jit(solution)/shard_map/ppermute | solution.py:37
  18.0 7.7 %collective-permute-start.4 = (bf16[8,128,2,512]{3,2,1,0:T(2,128)(2,1)S(1)}, bf16[8,128,2,512]{3,2,1,0:T(2,128)(2,1)S(1)}, u32[]{:S(2)}, u32[]{:S(2)}) collective-permute-start(bf16[8,128,2,512]{3,2,1,0:T(2,128)(2,1)S(1)} %get-tuple-element.64), channel_id=1, source_target_pairs={{0,1},{1,0},{2,3},{3,2},{4,5},{5,4},{6,7},{7,6},{8,9},{9,8},{10,11... | collective-permute-start | bytes 6291464 | tf_op jit(solution)/shard_map/ppermute | solution.py:37
  18.4 7.3 %collective-permute-start.5 = (bf16[2,128,2,512]{3,2,1,0:T(2,128)(2,1)S(1)}, bf16[2,128,2,512]{3,2,1,0:T(2,128)(2,1)S(1)}, u32[]{:S(2)}, u32[]{:S(2)}) collective-permute-start(bf16[2,128,2,512]{3,2,1,0:T(2,128)(2,1)S(1)} %slice_bitcast_fusion), channel_id=1, source_target_pairs={{0,1},{1,0},{2,3},{3,2},{4,5},{5,4},{6,7},{7,6},{8,9},{9,8},{10,11... | collective-permute-start | bytes 1572872 | tf_op jit(solution)/shard_map/ppermute | solution.py:37
  19.0 6.7 %collective-permute-start.6 = (f32[4,64,128]{2,1,0:T(8,128)S(1)}, f32[4,64,128]{2,1,0:T(8,128)S(1)}, u32[]{:S(2)}, u32[]{:S(2)}) collective-permute-start(f32[4,64,128]{2,1,0:T(8,128)S(1)} %get-tuple-element.67), channel_id=1, source_target_pairs={{0,16},{1,17},{2,18},{3,19},{4,20},{5,21},{6,22},{7,23},{8,24},{9,... | collective-permute-start | bytes 393224 | tf_op jit(solution)/shard_map/ppermute | solution.py:37
  19.2 8.5 %collective-permute-start.7 = (f32[4,64,128]{2,1,0:T(8,128)S(1)}, f32[4,64,128]{2,1,0:T(8,128)S(1)}, u32[]{:S(2)}, u32[]{:S(2)}) collective-permute-start(f32[4,64,128]{2,1,0:T(8,128)S(1)} %get-tuple-element.69), channel_id=1, source_target_pairs={{0,144},{1,145},{2,146},{3,147},{4,148},{5,149},{6,150},{7,151},{8... | collective-permute-start | bytes 393224 | tf_op jit(solution)/shard_map/ppermute | solution.py:37
  22.2 6.5 %collective-permute-start.8 = (f32[4,64,128]{2,1,0:T(8,128)S(1)}, f32[4,64,128]{2,1,0:T(8,128)S(1)}, u32[]{:S(2)}, u32[]{:S(2)}) collective-permute-start(f32[4,64,128]{2,1,0:T(8,128)S(1)} %get-tuple-element.70), channel_id=1, source_target_pairs={{0,128},{1,129},{2,130},{3,131},{4,132},{5,133},{6,134},{7,135},{8... | collective-permute-start | bytes 393224 | tf_op jit(solution)/shard_map/ppermute | solution.py:37
  29.4 13.6 %collective-permute-start.11 = (bf16[2,1,128,2,512]{4,3,2,1,0:T(2,128)(2,1)S(1)}, bf16[2,1,128,2,512]{4,3,2,1,0:T(2,128)(2,1)S(1)}, u32[]{:S(2)}, u32[]{:S(2)}) collective-permute-start(bf16[2,1,128,2,512]{4,3,2,1,0:T(2,128)(2,1)S(1)} %get-tuple-element.80), channel_id=1, source_target_pairs={{0,16},{1,145},{2,18},{3,147},{4,20},{5,149},{6,22},{7,151},{8,24}... | collective-permute-start | bytes 1572872 | tf_op jit(solution)/shard_map/ppermute | solution.py:37
  32.0 10.3 %collective-permute-start.12 = (f32[256,256]{1,0:T(8,128)S(1)}, f32[256,256]{1,0:T(8,128)S(1)}, u32[]{:S(2)}, u32[]{:S(2)}) collective-permute-start(f32[256,256]{1,0:T(8,128)S(1)} %get-tuple-element.106), channel_id=1, source_target_pairs={{0,2},{1,15},{2,4},{3,1},{4,6},{5,3},{6,8},{7,5},{8,10},{9,7},{10,... | collective-permute-start | bytes 786440 | tf_op jit(solution)/shard_map/ppermute | solution.py:37
  37.0 17.4 %collective-permute-start.10 = (bf16[2,1,128,2,512]{4,3,2,1,0:T(2,128)(2,1)S(1)}, bf16[2,1,128,2,512]{4,3,2,1,0:T(2,128)(2,1)S(1)}, u32[]{:S(2)}, u32[]{:S(2)}) collective-permute-start(bf16[2,1,128,2,512]{4,3,2,1,0:T(2,128)(2,1)S(1)} %get-tuple-element.78), channel_id=1, source_target_pairs={{0,16},{1,145},{2,18},{3,147},{4,20},{5,149},{6,22},{7,151},{8,24}... | collective-permute-start | bytes 1572872 | tf_op jit(solution)/shard_map/ppermute | solution.py:37
  44.5 9.1 %collective-permute-start.14 = (f32[256,256]{1,0:T(8,128)S(1)}, f32[256,256]{1,0:T(8,128)S(1)}, u32[]{:S(2)}, u32[]{:S(2)}) collective-permute-start(f32[256,256]{1,0:T(8,128)S(1)} %get-tuple-element.105), channel_id=1, source_target_pairs={{0,14},{1,3},{2,0},{3,5},{4,2},{5,7},{6,4},{7,9},{8,6},{9,11},{10,... | collective-permute-start | bytes 786440 | tf_op jit(solution)/shard_map/ppermute | solution.py:37
  46.9 11.6 %collective-permute-start.16 = (f32[256,512]{1,0:T(8,128)S(1)}, f32[256,512]{1,0:T(8,128)S(1)}, u32[]{:S(2)}, u32[]{:S(2)}) collective-permute-start(f32[256,512]{1,0:T(8,128)S(1)} %term.9), channel_id=1, source_target_pairs={{0,2},{1,15},{2,4},{3,1},{4,6},{5,3},{6,8},{7,5},{8,10},{9,7},{10,... | collective-permute-start | bytes 1572872 | tf_op jit(solution)/shard_map/ppermute | solution.py:37
  47.0 12.3 %collective-permute-start.20 = (bf16[2,1,128,2,512]{4,3,2,1,0:T(2,128)(2,1)S(1)}, bf16[2,1,128,2,512]{4,3,2,1,0:T(2,128)(2,1)S(1)}, u32[]{:S(2)}, u32[]{:S(2)}) collective-permute-start(bf16[2,1,128,2,512]{4,3,2,1,0:T(2,128)(2,1)S(1)} %get-tuple-element.94), channel_id=1, source_target_pairs={{0,16},{1,145},{2,18},{3,147},{4,20},{5,149},{6,22},{7,151},{8,24}... | collective-permute-start | bytes 1572872 | tf_op jit(solution)/shard_map/ppermute | solution.py:37
  54.7 13.9 %collective-permute-start.22 = (f32[256,512]{1,0:T(8,128)S(1)}, f32[256,512]{1,0:T(8,128)S(1)}, u32[]{:S(2)}, u32[]{:S(2)}) collective-permute-start(f32[256,512]{1,0:T(8,128)S(1)} %term.10), channel_id=1, source_target_pairs={{0,14},{1,3},{2,0},{3,5},{4,2},{5,7},{6,4},{7,9},{8,6},{9,11},{10,... | collective-permute-start | bytes 1572872 | tf_op jit(solution)/shard_map/ppermute | solution.py:37
  58.4 10.8 %collective-permute-start.19 = (bf16[2,1,128,2,512]{4,3,2,1,0:T(2,128)(2,1)S(1)}, bf16[2,1,128,2,512]{4,3,2,1,0:T(2,128)(2,1)S(1)}, u32[]{:S(2)}, u32[]{:S(2)}) collective-permute-start(bf16[2,1,128,2,512]{4,3,2,1,0:T(2,128)(2,1)S(1)} %get-tuple-element.93), channel_id=1, source_target_pairs={{0,16},{1,145},{2,18},{3,147},{4,20},{5,149},{6,22},{7,151},{8,24}... | collective-permute-start | bytes 1572872 | tf_op jit(solution)/shard_map/ppermute | solution.py:37
  59.6 13.9 %collective-permute-start.24 = (f32[256,512]{1,0:T(8,128)S(1)}, f32[256,512]{1,0:T(8,128)S(1)}, u32[]{:S(2)}, u32[]{:S(2)}) collective-permute-start(f32[256,512]{1,0:T(8,128)S(1)} %term.11), channel_id=1, source_target_pairs={{0,2},{1,15},{2,4},{3,1},{4,6},{5,3},{6,8},{7,5},{8,10},{9,7},{10,... | collective-permute-start | bytes 1572872 | tf_op jit(solution)/shard_map/ppermute | solution.py:37
  59.7 14.8 %collective-permute-start.18 = (bf16[2,1,128,2,512]{4,3,2,1,0:T(2,128)(2,1)S(1)}, bf16[2,1,128,2,512]{4,3,2,1,0:T(2,128)(2,1)S(1)}, u32[]{:S(2)}, u32[]{:S(2)}) collective-permute-start(bf16[2,1,128,2,512]{4,3,2,1,0:T(2,128)(2,1)S(1)} %get-tuple-element.92), channel_id=1, source_target_pairs={{0,16},{1,145},{2,18},{3,147},{4,20},{5,149},{6,22},{7,151},{8,24}... | collective-permute-start | bytes 1572872 | tf_op jit(solution)/shard_map/ppermute | solution.py:37
  69.5 3.9 %collective-permute-start.23 = (bf16[1,128,2,512]{3,2,1,0:T(2,128)(2,1)S(1)}, bf16[1,128,2,512]{3,2,1,0:T(2,128)(2,1)S(1)}, u32[]{:S(2)}, u32[]{:S(2)}) collective-permute-start(bf16[1,128,2,512]{3,2,1,0:T(2,128)(2,1)S(1)} %slice_bitcast_fusion.3), channel_id=1, source_target_pairs={{0,1},{1,0},{2,3},{3,2},{4,5},{5,4},{6,7},{7,6},{8,9},{9,8},{10,11... | collective-permute-start | bytes 786440 | tf_op jit(solution)/shard_map/ppermute | solution.py:37
  69.6 13.9 %collective-permute-start.26 = (f32[256,512]{1,0:T(8,128)S(1)}, f32[256,512]{1,0:T(8,128)S(1)}, u32[]{:S(2)}, u32[]{:S(2)}) collective-permute-start(f32[256,512]{1,0:T(8,128)S(1)} %term.12), channel_id=1, source_target_pairs={{0,14},{1,3},{2,0},{3,5},{4,2},{5,7},{6,4},{7,9},{8,6},{9,11},{10,... | collective-permute-start | bytes 1572872 | tf_op jit(solution)/shard_map/ppermute | solution.py:37
  73.3 10.8 %collective-permute-start.17 = (bf16[2,1,128,2,512]{4,3,2,1,0:T(2,128)(2,1)S(1)}, bf16[2,1,128,2,512]{4,3,2,1,0:T(2,128)(2,1)S(1)}, u32[]{:S(2)}, u32[]{:S(2)}) collective-permute-start(bf16[2,1,128,2,512]{4,3,2,1,0:T(2,128)(2,1)S(1)} %get-tuple-element.91), channel_id=1, source_target_pairs={{0,16},{1,145},{2,18},{3,147},{4,20},{5,149},{6,22},{7,151},{8,24}... | collective-permute-start | bytes 1572872 | tf_op jit(solution)/shard_map/ppermute | solution.py:37
  74.7 15.9 %collective-permute-start.28 = (f32[256,512]{1,0:T(8,128)S(1)}, f32[256,512]{1,0:T(8,128)S(1)}, u32[]{:S(2)}, u32[]{:S(2)}) collective-permute-start(f32[256,512]{1,0:T(8,128)S(1)} %term.13), channel_id=1, source_target_pairs={{0,2},{1,15},{2,4},{3,1},{4,6},{5,3},{6,8},{7,5},{8,10},{9,7},{10,... | collective-permute-start | bytes 1572872 | tf_op jit(solution)/shard_map/ppermute | solution.py:37
  84.2 10.5 %collective-permute-start.29 = (f32[256,512]{1,0:T(8,128)S(1)}, f32[256,512]{1,0:T(8,128)S(1)}, u32[]{:S(2)}, u32[]{:S(2)}) collective-permute-start(f32[256,512]{1,0:T(8,128)S(1)} %term.14), channel_id=1, source_target_pairs={{0,14},{1,3},{2,0},{3,5},{4,2},{5,7},{6,4},{7,9},{8,6},{9,11},{10,... | collective-permute-start | bytes 1572872 | tf_op jit(solution)/shard_map/ppermute | solution.py:37
  (9 other events, 38.7 us)

commit v6 on v3

--- a/solution.py
+++ b/solution.py
@@ -253,7 +253,9 @@
         if s == Z - 1:
             total = term(el, ec, flats[s])
             break
-        total = term(el, ec, flats[s], *sums[s % 2:s % 2 + 1] if s > 1 else ())
+        total = term(el, ec, flats[s])
+        if s > 1:
+            total = sums[s % 2] + total
         if s in PACE:
             ahead, total = lax.optimization_barrier((far[len(fars) - 1], total))
             fars.append(across(ahead))

time: 86.3 us -> 87.5 us (1.014)
  no operation moved by 1% of the time
where the time goes in v6:
time: 87.5 us; the launch traced here: 86.7 us
  waiting for transfers between devices  40.8 us (47%)
  starting transfers between devices  27.3 us (31%)
  Pallas kernels  16.4 us (19%)
  local copies, waits for them, and re-layouts  1.55 us (2%)
    ppermute x29, waiting for transfers between devices, shift(): return lax.ppermute(array, ('grp', 'freq'), pairs)  40.8 us
    ppermute x29, starting transfers between devices, shift(): return lax.ppermute(array, ('grp', 'freq'), pairs)  27.3 us
    pallas_call x3, Pallas kernels, cut_matrix(): pl.pallas_call(kernel, in_specs=[SMEM, pl.BlockSpec(memory_space=pltpu.HB...  7.36 us
    pallas_call x8, Pallas kernels, term(): pl.pallas_call(term_kernel, out_shape=jax.ShapeDtypeStruct((el.shape[2],...  5.58 us
  transfers between devices with their start and end apart: 29, of which 24 were waited for; matrix products, arithmetic and copies ran while one was open for 2% of the time, Pallas kernels for 15%

profile of v6, /device:TPU:24, one launch (start us, length us, event | category | flops | bytes accessed | tf_op | source)
XLA Modules:
  0.0 86.7 jit_solution(1480027053702830219)
XLA Ops:
  0.1 1.8 %cut_matrix.3 = bf16[2,2,128,2,512]{4,3,2,1,0:T(2,128)(2,1)S(1)} custom-call(s32[5]{0:T(128)S(1)} %stack.23.place_ref, bf16[128,2,16384]{2,1,0:T(2,128)(2,1)} %src.3), custom_call_target="tpu_custom_call" | custom-call | flops 1000 | bytes 1000 | tf_op jit(solution)/shard_map/cut_matrix/pallas_call | solution.py:146
  1.9 1.6 %collective-permute-start.3 = (bf16[2,2,128,2,512]{4,3,2,1,0:T(2,128)(2,1)S(1)}, bf16[2,2,128,2,512]{4,3,2,1,0:T(2,128)(2,1)S(1)}, u32[]{:S(2)}, u32[]{:S(2)}) collective-permute-start(bf16[2,2,128,2,512]{4,3,2,1,0:T(2,128)(2,1)S(1)} %cut_matrix.3), channel_id=1, source_target_pairs={{0,16},{1,145},{2,18},{3,147},{4,20},{5,149},{6,22},{7,151},{8,24}... | collective-permute-start | bytes 3145736 | tf_op jit(solution)/shard_map/ppermute | solution.py:37
  4.2 2.5 %collective-permute-start.2 = (bf16[8,64,128]{2,1,0:T(8,128)(2,1)S(1)}, bf16[8,64,128]{2,1,0:T(8,128)(2,1)S(1)}, u32[]{:S(2)}, u32[]{:S(2)}) collective-permute-start(bf16[8,64,128]{2,1,0:T(8,128)(2,1)S(1)} %bitcast.22), channel_id=1, source_target_pairs={{0,32},{1,33},{2,34},{3,35},{4,36},{5,37},{6,38},{7,39},{8,40},{9,... | collective-permute-start | bytes 393224 | tf_op jit(solution)/shard_map/ppermute | solution.py:37
  6.7 4.2 %collective-permute-done.r1 = bf16[8,64,128]{2,1,0:T(8,128)(2,1)S(1)} collective-permute-done((bf16[8,64,128]{2,1,0:T(8,128)(2,1)S(1)}, bf16[8,64,128]{2,1,0:T(8,128)(2,1)S(1)}, u32[]{:S(2)}, u32[]{:S(2)}) %collective-permute-start) | collective-permute-done | bytes 131104 | tf_op jit(solution)/shard_map/ppermute | solution.py:37
  10.9 2.6 %cut_matrix.4 = (bf16[2,1,128,2,512]{4,3,2,1,0:T(2,128)(2,1)S(1)}, bf16[2,128,2,512]{3,2,1,0:T(2,128)(2,1)S(1)}, bf16[8,128,2,512]{3,2,1,0:T(2,128)(2,1)S(1)}) custom-call(s32[5]{0:T(128)S(1)} %stack.23.place_ref, bf16[128,2,16384]{2,1,0:T(2,128)(2,1)} %src.3), custom_call_target="tpu_custom_call" | custom-call | flops 1000 | bytes 1000 | tf_op jit(solution)/shard_map/cut_matrix/pallas_call | solution.py:146
  14.9 3.1 %collective-permute-done.3.refs_2_ = bf16[2,2,128,2,512]{4,3,2,1,0:T(2,128)(2,1)S(1)} collective-permute-done((bf16[2,2,128,2,512]{4,3,2,1,0:T(2,128)(2,1)S(1)}, bf16[2,2,128,2,512]{4,3,2,1,0:T(2,128)(2,1)S(1)}, u32[]{:S(2)}, u32[]{:S(2)}) %collective-permute-start.3) | collective-permute-done | bytes 1048608 | tf_op jit(solution)/shard_map/ppermute | solution.py:37
  19.2 3.0 %collective-permute-start.7 = (f32[4,64,128]{2,1,0:T(8,128)S(1)}, f32[4,64,128]{2,1,0:T(8,128)S(1)}, u32[]{:S(2)}, u32[]{:S(2)}) collective-permute-start(f32[4,64,128]{2,1,0:T(8,128)S(1)} %get-tuple-element.69), channel_id=1, source_target_pairs={{0,144},{1,145},{2,146},{3,147},{4,148},{5,149},{6,150},{7,151},{8... | collective-permute-start | bytes 393224 | tf_op jit(solution)/shard_map/ppermute | solution.py:37
  22.8 2.9 %collective-permute-done.6.b0 = f32[4,64,128]{2,1,0:T(8,128)S(1)} collective-permute-done((f32[4,64,128]{2,1,0:T(8,128)S(1)}, f32[4,64,128]{2,1,0:T(8,128)S(1)}, u32[]{:S(2)}, u32[]{:S(2)}) %collective-permute-start.6) | collective-permute-done | bytes 131104 | tf_op jit(solution)/shard_map/ppermute | solution.py:37
  25.9 1.8 %collective-permute-done.7.b1 = f32[4,64,128]{2,1,0:T(8,128)S(1)} collective-permute-done((f32[4,64,128]{2,1,0:T(8,128)S(1)}, f32[4,64,128]{2,1,0:T(8,128)S(1)}, u32[]{:S(2)}, u32[]{:S(2)}) %collective-permute-start.7) | collective-permute-done | bytes 131104 | tf_op jit(solution)/shard_map/ppermute | solution.py:37
  32.0 2.0 %collective-permute-start.13 = (f32[256,512]{1,0:T(8,128)S(1)}, f32[256,512]{1,0:T(8,128)S(1)}, u32[]{:S(2)}, u32[]{:S(2)}) collective-permute-start(f32[256,512]{1,0:T(8,128)S(1)} %term.8), channel_id=1, source_target_pairs={{0,2},{1,15},{2,4},{3,1},{4,6},{5,3},{6,8},{7,5},{8,10},{9,7},{10,... | collective-permute-start | bytes 1572872 | tf_op jit(solution)/shard_map/ppermute | solution.py:37
  34.0 3.0 %cut_matrix.5 = (bf16[2,1,128,2,512]{4,3,2,1,0:T(2,128)(2,1)S(1)}, bf16[2,1,128,2,512]{4,3,2,1,0:T(2,128)(2,1)S(1)}, bf16[2,1,128,2,512]{4,3,2,1,0:T(2,128)(2,1)...) custom-call(s32[5]{0:T(128)S(1)} %stack.23.place_ref, ...), custom_call_target="tpu_custom_call" | custom-call | flops 1000 | bytes 1000 | tf_op jit(solution)/shard_map/cut_matrix/pallas_call | solution.py:146
  40.0 4.4 %collective-permute-start.14 = (bf16[1,128,2,512]{3,2,1,0:T(2,128)(2,1)S(1)}, bf16[1,128,2,512]{3,2,1,0:T(2,128)(2,1)S(1)}, u32[]{:S(2)}, u32[]{:S(2)}) collective-permute-start(bf16[1,128,2,512]{3,2,1,0:T(2,128)(2,1)S(1)} %slice_bitcast_fusion.6), channel_id=1, source_target_pairs={{0,1},{1,0},{2,3},{3,2},{4,5},{5,4},{6,7},{7,6},{8,9},{9,8},{10,11... | collective-permute-start | bytes 786440 | tf_op jit(solution)/shard_map/ppermute | solution.py:37
  44.5 1.8 %collective-permute-start.11 = (f32[256,512]{1,0:T(8,128)S(1)}, f32[256,512]{1,0:T(8,128)S(1)}, u32[]{:S(2)}, u32[]{:S(2)}) collective-permute-start(f32[256,512]{1,0:T(8,128)S(1)} %term.9), channel_id=1, source_target_pairs={{0,14},{1,3},{2,0},{3,5},{4,2},{5,7},{6,4},{7,9},{8,6},{9,11},{10,... | collective-permute-start | bytes 1572872 | tf_op jit(solution)/shard_map/ppermute | solution.py:37
  47.6 2.8 %collective-permute-start.15 = (bf16[1,128,2,512]{3,2,1,0:T(2,128)(2,1)S(1)}, bf16[1,128,2,512]{3,2,1,0:T(2,128)(2,1)S(1)}, u32[]{:S(2)}, u32[]{:S(2)}) collective-permute-start(bf16[1,128,2,512]{3,2,1,0:T(2,128)(2,1)S(1)} %slice_bitcast_fusion.5), channel_id=1, source_target_pairs={{0,1},{1,0},{2,3},{3,2},{4,5},{5,4},{6,7},{7,6},{8,9},{9,8},{10,11... | collective-permute-start | bytes 786440 | tf_op jit(solution)/shard_map/ppermute | solution.py:37
  52.4 1.8 %collective-permute-done.11 = f32[256,512]{1,0:T(8,128)S(1)} collective-permute-done((f32[256,512]{1,0:T(8,128)S(1)}, f32[256,512]{1,0:T(8,128)S(1)}, u32[]{:S(2)}, u32[]{:S(2)}) %collective-permute-start.11) | collective-permute-done | bytes 524320 | tf_op jit(solution)/shard_map/ppermute | solution.py:37
  54.3 2.4 %collective-permute-done.19.refs_2_ = bf16[2,1,128,2,512]{4,3,2,1,0:T(2,128)(2,1)S(1)} collective-permute-done((bf16[2,1,128,2,512]{4,3,2,1,0:T(2,128)(2,1)S(1)}, bf16[2,1,128,2,512]{4,3,2,1,0:T(2,128)(2,1)S(1)}, u32[]{:S(2)}, u32[]{:S(2)}) %collective-permute-start.19) | collective-permute-done | bytes 524320 | tf_op jit(solution)/shard_map/ppermute | solution.py:37
  64.9 1.8 %collective-permute-done.23 = f32[256,512]{1,0:T(8,128)S(1)} collective-permute-done((f32[256,512]{1,0:T(8,128)S(1)}, f32[256,512]{1,0:T(8,128)S(1)}, u32[]{:S(2)}, u32[]{:S(2)}) %collective-permute-start.23) | collective-permute-done | bytes 524320 | tf_op jit(solution)/shard_map/ppermute | solution.py:37
  66.8 1.7 %collective-permute-done.22.refs_2_ = bf16[2,1,128,2,512]{4,3,2,1,0:T(2,128)(2,1)S(1)} collective-permute-done((bf16[2,1,128,2,512]{4,3,2,1,0:T(2,128)(2,1)S(1)}, bf16[2,1,128,2,512]{4,3,2,1,0:T(2,128)(2,1)S(1)}, u32[]{:S(2)}, u32[]{:S(2)}) %collective-permute-start.22) | collective-permute-done | bytes 524320 | tf_op jit(solution)/shard_map/ppermute | solution.py:37
  68.7 1.5 %collective-permute-done.25.refs_3_ = bf16[1,128,2,512]{3,2,1,0:T(2,128)(2,1)S(1)} collective-permute-done((bf16[1,128,2,512]{3,2,1,0:T(2,128)(2,1)S(1)}, bf16[1,128,2,512]{3,2,1,0:T(2,128)(2,1)S(1)}, u32[]{:S(2)}, u32[]{:S(2)}) %collective-permute-start.25) | collective-permute-done | bytes 262176 | tf_op jit(solution)/shard_map/ppermute | solution.py:37
  70.3 1.7 %collective-permute-start.28 = (f32[256,512]{1,0:T(8,128)S(1)}, f32[256,512]{1,0:T(8,128)S(1)}, u32[]{:S(2)}, u32[]{:S(2)}) collective-permute-start(f32[256,512]{1,0:T(8,128)S(1)} %add.18), channel_id=1, source_target_pairs={{0,14},{1,3},{2,0},{3,5},{4,2},{5,7},{6,4},{7,9},{8,6},{9,11},{10,... | collective-permute-start | bytes 1572872 | tf_op jit(solution)/shard_map/ppermute | solution.py:37
  74.0 1.9 %collective-permute-start.27 = (f32[256,512]{1,0:T(8,128)S(1)}, f32[256,512]{1,0:T(8,128)S(1)}, u32[]{:S(2)}, u32[]{:S(2)}) collective-permute-start(f32[256,512]{1,0:T(8,128)S(1)} %add.19), channel_id=1, source_target_pairs={{0,2},{1,15},{2,4},{3,1},{4,6},{5,3},{6,8},{7,5},{8,10},{9,7},{10,... | collective-permute-start | bytes 1572872 | tf_op jit(solution)/shard_map/ppermute | solution.py:37
  76.2 1.5 %collective-permute-done.26.refs_3_ = bf16[1,128,2,512]{3,2,1,0:T(2,128)(2,1)S(1)} collective-permute-done((bf16[1,128,2,512]{3,2,1,0:T(2,128)(2,1)S(1)}, bf16[1,128,2,512]{3,2,1,0:T(2,128)(2,1)S(1)}, u32[]{:S(2)}, u32[]{:S(2)}) %collective-permute-start.26) | collective-permute-done | bytes 262176 | tf_op jit(solution)/shard_map/ppermute | solution.py:37
  78.5 5.6 %collective-permute-done.28.c = f32[256,512]{1,0:T(8,128)S(1)} collective-permute-done((f32[256,512]{1,0:T(8,128)S(1)}, f32[256,512]{1,0:T(8,128)S(1)}, u32[]{:S(2)}, u32[]{:S(2)}) %collective-permute-start.28) | collective-permute-done | bytes 524320 | tf_op jit(solution)/shard_map/ppermute | solution.py:37
  84.2 1.6 %collective-permute-done.27.b = f32[256,512]{1,0:T(8,128)S(1)} collective-permute-done((f32[256,512]{1,0:T(8,128)S(1)}, f32[256,512]{1,0:T(8,128)S(1)}, u32[]{:S(2)}, u32[]{:S(2)}) %collective-permute-start.27) | collective-permute-done | bytes 524320 | tf_op jit(solution)/shard_map/ppermute | solution.py:37
  (75 shorter events, 27.7 us)
Async XLA Ops:
  1.9 16.1 %collective-permute-start.3 = (bf16[2,2,128,2,512]{4,3,2,1,0:T(2,128)(2,1)S(1)}, bf16[2,2,128,2,512]{4,3,2,1,0:T(2,128)(2,1)S(1)}, u32[]{:S(2)}, u32[]{:S(2)}) collective-permute-start(bf16[2,2,128,2,512]{4,3,2,1,0:T(2,128)(2,1)S(1)} %cut_matrix.3), channel_id=1, source_target_pairs={{0,16},{1,145},{2,18},{3,147},{4,20},{5,149},{6,22},{7,151},{8,24}... | collective-permute-start | bytes 3145736 | tf_op jit(solution)/shard_map/ppermute | solution.py:37
  3.5 7.4 %collective-permute-start = (bf16[8,64,128]{2,1,0:T(8,128)(2,1)S(1)}, bf16[8,64,128]{2,1,0:T(8,128)(2,1)S(1)}, u32[]{:S(2)}, u32[]{:S(2)}) collective-permute-start(bf16[8,64,128]{2,1,0:T(8,128)(2,1)S(1)} %bitcast.21), channel_id=1, source_target_pairs={{0,96},{1,97},{2,98},{3,99},{4,100},{5,101},{6,102},{7,103},{8,104... | collective-permute-start | bytes 393224 | tf_op jit(solution)/shard_map/ppermute | solution.py:37
  4.2 9.3 %collective-permute-start.2 = (bf16[8,64,128]{2,1,0:T(8,128)(2,1)S(1)}, bf16[8,64,128]{2,1,0:T(8,128)(2,1)S(1)}, u32[]{:S(2)}, u32[]{:S(2)}) collective-permute-start(bf16[8,64,128]{2,1,0:T(8,128)(2,1)S(1)} %bitcast.22), channel_id=1, source_target_pairs={{0,32},{1,33},{2,34},{3,35},{4,36},{5,37},{6,38},{7,39},{8,40},{9,... | collective-permute-start | bytes 393224 | tf_op jit(solution)/shard_map/ppermute | solution.py:37
  6.7 7.2 %collective-permute-start.1 = (bf16[8,64,128]{2,1,0:T(8,128)(2,1)S(1)}, bf16[8,64,128]{2,1,0:T(8,128)(2,1)S(1)}, u32[]{:S(2)}, u32[]{:S(2)}) collective-permute-start(bf16[8,64,128]{2,1,0:T(8,128)(2,1)S(1)} %bitcast.23), channel_id=1, source_target_pairs={{0,64},{1,65},{2,66},{3,67},{4,68},{5,69},{6,70},{7,71},{8,72},{9,... | collective-permute-start | bytes 393224 | tf_op jit(solution)/shard_map/ppermute | solution.py:37
  18.0 7.7 %collective-permute-start.4 = (bf16[8,128,2,512]{3,2,1,0:T(2,128)(2,1)S(1)}, bf16[8,128,2,512]{3,2,1,0:T(2,128)(2,1)S(1)}, u32[]{:S(2)}, u32[]{:S(2)}) collective-permute-start(bf16[8,128,2,512]{3,2,1,0:T(2,128)(2,1)S(1)} %get-tuple-element.64), channel_id=1, source_target_pairs={{0,1},{1,0},{2,3},{3,2},{4,5},{5,4},{6,7},{7,6},{8,9},{9,8},{10,11... | collective-permute-start | bytes 6291464 | tf_op jit(solution)/shard_map/ppermute | solution.py:37
  18.4 7.3 %collective-permute-start.5 = (bf16[2,128,2,512]{3,2,1,0:T(2,128)(2,1)S(1)}, bf16[2,128,2,512]{3,2,1,0:T(2,128)(2,1)S(1)}, u32[]{:S(2)}, u32[]{:S(2)}) collective-permute-start(bf16[2,128,2,512]{3,2,1,0:T(2,128)(2,1)S(1)} %slice_bitcast_fusion), channel_id=1, source_target_pairs={{0,1},{1,0},{2,3},{3,2},{4,5},{5,4},{6,7},{7,6},{8,9},{9,8},{10,11... | collective-permute-start | bytes 1572872 | tf_op jit(solution)/shard_map/ppermute | solution.py:37
  19.0 6.7 %collective-permute-start.6 = (f32[4,64,128]{2,1,0:T(8,128)S(1)}, f32[4,64,128]{2,1,0:T(8,128)S(1)}, u32[]{:S(2)}, u32[]{:S(2)}) collective-permute-start(f32[4,64,128]{2,1,0:T(8,128)S(1)} %get-tuple-element.67), channel_id=1, source_target_pairs={{0,16},{1,17},{2,18},{3,19},{4,20},{5,21},{6,22},{7,23},{8,24},{9,... | collective-permute-start | bytes 393224 | tf_op jit(solution)/shard_map/ppermute | solution.py:37
  19.2 8.5 %collective-permute-start.7 = (f32[4,64,128]{2,1,0:T(8,128)S(1)}, f32[4,64,128]{2,1,0:T(8,128)S(1)}, u32[]{:S(2)}, u32[]{:S(2)}) collective-permute-start(f32[4,64,128]{2,1,0:T(8,128)S(1)} %get-tuple-element.69), channel_id=1, source_target_pairs={{0,144},{1,145},{2,146},{3,147},{4,148},{5,149},{6,150},{7,151},{8... | collective-permute-start | bytes 393224 | tf_op jit(solution)/shard_map/ppermute | solution.py:37
  22.2 6.5 %collective-permute-start.8 = (f32[4,64,128]{2,1,0:T(8,128)S(1)}, f32[4,64,128]{2,1,0:T(8,128)S(1)}, u32[]{:S(2)}, u32[]{:S(2)}) collective-permute-start(f32[4,64,128]{2,1,0:T(8,128)S(1)} %get-tuple-element.70), channel_id=1, source_target_pairs={{0,128},{1,129},{2,130},{3,131},{4,132},{5,133},{6,134},{7,135},{8... | collective-permute-start | bytes 393224 | tf_op jit(solution)/shard_map/ppermute | solution.py:37
  29.4 10.5 %collective-permute-start.10 = (bf16[2,1,128,2,512]{4,3,2,1,0:T(2,128)(2,1)S(1)}, bf16[2,1,128,2,512]{4,3,2,1,0:T(2,128)(2,1)S(1)}, u32[]{:S(2)}, u32[]{:S(2)}) collective-permute-start(bf16[2,1,128,2,512]{4,3,2,1,0:T(2,128)(2,1)S(1)} %get-tuple-element.78), channel_id=1, source_target_pairs={{0,16},{1,145},{2,18},{3,147},{4,20},{5,149},{6,22},{7,151},{8,24}... | collective-permute-start | bytes 1572872 | tf_op jit(solution)/shard_map/ppermute | solution.py:37
  32.0 15.1 %collective-permute-start.13 = (f32[256,512]{1,0:T(8,128)S(1)}, f32[256,512]{1,0:T(8,128)S(1)}, u32[]{:S(2)}, u32[]{:S(2)}) collective-permute-start(f32[256,512]{1,0:T(8,128)S(1)} %term.8), channel_id=1, source_target_pairs={{0,2},{1,15},{2,4},{3,1},{4,6},{5,3},{6,8},{7,5},{8,10},{9,7},{10,... | collective-permute-start | bytes 1572872 | tf_op jit(solution)/shard_map/ppermute | solution.py:37
  37.0 10.5 %collective-permute-start.12 = (bf16[2,1,128,2,512]{4,3,2,1,0:T(2,128)(2,1)S(1)}, bf16[2,1,128,2,512]{4,3,2,1,0:T(2,128)(2,1)S(1)}, u32[]{:S(2)}, u32[]{:S(2)}) collective-permute-start(bf16[2,1,128,2,512]{4,3,2,1,0:T(2,128)(2,1)S(1)} %get-tuple-element.85), channel_id=1, source_target_pairs={{0,16},{1,145},{2,18},{3,147},{4,20},{5,149},{6,22},{7,151},{8,24}... | collective-permute-start | bytes 1572872 | tf_op jit(solution)/shard_map/ppermute | solution.py:37
  40.0 6.2 %collective-permute-start.14 = (bf16[1,128,2,512]{3,2,1,0:T(2,128)(2,1)S(1)}, bf16[1,128,2,512]{3,2,1,0:T(2,128)(2,1)S(1)}, u32[]{:S(2)}, u32[]{:S(2)}) collective-permute-start(bf16[1,128,2,512]{3,2,1,0:T(2,128)(2,1)S(1)} %slice_bitcast_fusion.6), channel_id=1, source_target_pairs={{0,1},{1,0},{2,3},{3,2},{4,5},{5,4},{6,7},{7,6},{8,9},{9,8},{10,11... | collective-permute-start | bytes 786440 | tf_op jit(solution)/shard_map/ppermute | solution.py:37
  44.5 9.7 %collective-permute-start.11 = (f32[256,512]{1,0:T(8,128)S(1)}, f32[256,512]{1,0:T(8,128)S(1)}, u32[]{:S(2)}, u32[]{:S(2)}) collective-permute-start(f32[256,512]{1,0:T(8,128)S(1)} %term.9), channel_id=1, source_target_pairs={{0,14},{1,3},{2,0},{3,5},{4,2},{5,7},{6,4},{7,9},{8,6},{9,11},{10,... | collective-permute-start | bytes 1572872 | tf_op jit(solution)/shard_map/ppermute | solution.py:37
  46.2 10.4 %collective-permute-start.19 = (bf16[2,1,128,2,512]{4,3,2,1,0:T(2,128)(2,1)S(1)}, bf16[2,1,128,2,512]{4,3,2,1,0:T(2,128)(2,1)S(1)}, u32[]{:S(2)}, u32[]{:S(2)}) collective-permute-start(bf16[2,1,128,2,512]{4,3,2,1,0:T(2,128)(2,1)S(1)} %get-tuple-element.94), channel_id=1, source_target_pairs={{0,16},{1,145},{2,18},{3,147},{4,20},{5,149},{6,22},{7,151},{8,24}... | collective-permute-start | bytes 1572872 | tf_op jit(solution)/shard_map/ppermute | solution.py:37
  47.6 3.9 %collective-permute-start.15 = (bf16[1,128,2,512]{3,2,1,0:T(2,128)(2,1)S(1)}, bf16[1,128,2,512]{3,2,1,0:T(2,128)(2,1)S(1)}, u32[]{:S(2)}, u32[]{:S(2)}) collective-permute-start(bf16[1,128,2,512]{3,2,1,0:T(2,128)(2,1)S(1)} %slice_bitcast_fusion.5), channel_id=1, source_target_pairs={{0,1},{1,0},{2,3},{3,2},{4,5},{5,4},{6,7},{7,6},{8,9},{9,8},{10,11... | collective-permute-start | bytes 786440 | tf_op jit(solution)/shard_map/ppermute | solution.py:37
  50.4 10.4 %collective-permute-start.18 = (f32[256,512]{1,0:T(8,128)S(1)}, f32[256,512]{1,0:T(8,128)S(1)}, u32[]{:S(2)}, u32[]{:S(2)}) collective-permute-start(f32[256,512]{1,0:T(8,128)S(1)} %add.15), channel_id=1, source_target_pairs={{0,2},{1,15},{2,4},{3,1},{4,6},{5,3},{6,8},{7,5},{8,10},{9,7},{10,... | collective-permute-start | bytes 1572872 | tf_op jit(solution)/shard_map/ppermute | solution.py:37
  50.4 11.9 %collective-permute-start.17 = (bf16[2,1,128,2,512]{4,3,2,1,0:T(2,128)(2,1)S(1)}, bf16[2,1,128,2,512]{4,3,2,1,0:T(2,128)(2,1)S(1)}, u32[]{:S(2)}, u32[]{:S(2)}) collective-permute-start(bf16[2,1,128,2,512]{4,3,2,1,0:T(2,128)(2,1)S(1)} %get-tuple-element.92), channel_id=1, source_target_pairs={{0,16},{1,145},{2,18},{3,147},{4,20},{5,149},{6,22},{7,151},{8,24}... | collective-permute-start | bytes 1572872 | tf_op jit(solution)/shard_map/ppermute | solution.py:37
  56.9 9.7 %collective-permute-start.23 = (f32[256,512]{1,0:T(8,128)S(1)}, f32[256,512]{1,0:T(8,128)S(1)}, u32[]{:S(2)}, u32[]{:S(2)}) collective-permute-start(f32[256,512]{1,0:T(8,128)S(1)} %add.16), channel_id=1, source_target_pairs={{0,14},{1,3},{2,0},{3,5},{4,2},{5,7},{6,4},{7,9},{8,6},{9,11},{10,... | collective-permute-start | bytes 1572872 | tf_op jit(solution)/shard_map/ppermute | solution.py:37
  58.0 10.4 %collective-permute-start.22 = (bf16[2,1,128,2,512]{4,3,2,1,0:T(2,128)(2,1)S(1)}, bf16[2,1,128,2,512]{4,3,2,1,0:T(2,128)(2,1)S(1)}, u32[]{:S(2)}, u32[]{:S(2)}) collective-permute-start(bf16[2,1,128,2,512]{4,3,2,1,0:T(2,128)(2,1)S(1)} %get-tuple-element.98), channel_id=1, source_target_pairs={{0,16},{1,145},{2,18},{3,147},{4,20},{5,149},{6,22},{7,151},{8,24}... | collective-permute-start | bytes 1572872 | tf_op jit(solution)/shard_map/ppermute | solution.py:37
  62.5 10.5 %collective-permute-start.21 = (f32[256,512]{1,0:T(8,128)S(1)}, f32[256,512]{1,0:T(8,128)S(1)}, u32[]{:S(2)}, u32[]{:S(2)}) collective-permute-start(f32[256,512]{1,0:T(8,128)S(1)} %add.17), channel_id=1, source_target_pairs={{0,2},{1,15},{2,4},{3,1},{4,6},{5,3},{6,8},{7,5},{8,10},{9,7},{10,... | collective-permute-start | bytes 1572872 | tf_op jit(solution)/shard_map/ppermute | solution.py:37
  62.9 11.1 %collective-permute-start.16 = (bf16[2,1,128,2,512]{4,3,2,1,0:T(2,128)(2,1)S(1)}, bf16[2,1,128,2,512]{4,3,2,1,0:T(2,128)(2,1)S(1)}, u32[]{:S(2)}, u32[]{:S(2)}) collective-permute-start(bf16[2,1,128,2,512]{4,3,2,1,0:T(2,128)(2,1)S(1)} %get-tuple-element.91), channel_id=1, source_target_pairs={{0,16},{1,145},{2,18},{3,147},{4,20},{5,149},{6,22},{7,151},{8,24}... | collective-permute-start | bytes 1572872 | tf_op jit(solution)/shard_map/ppermute | solution.py:37
  70.3 13.8 %collective-permute-start.28 = (f32[256,512]{1,0:T(8,128)S(1)}, f32[256,512]{1,0:T(8,128)S(1)}, u32[]{:S(2)}, u32[]{:S(2)}) collective-permute-start(f32[256,512]{1,0:T(8,128)S(1)} %add.18), channel_id=1, source_target_pairs={{0,14},{1,3},{2,0},{3,5},{4,2},{5,7},{6,4},{7,9},{8,6},{9,11},{10,... | collective-permute-start | bytes 1572872 | tf_op jit(solution)/shard_map/ppermute | solution.py:37
  74.0 11.8 %collective-permute-start.27 = (f32[256,512]{1,0:T(8,128)S(1)}, f32[256,512]{1,0:T(8,128)S(1)}, u32[]{:S(2)}, u32[]{:S(2)}) collective-permute-start(f32[256,512]{1,0:T(8,128)S(1)} %add.19), channel_id=1, source_target_pairs={{0,2},{1,15},{2,4},{3,1},{4,6},{5,3},{6,8},{7,5},{8,10},{9,7},{10,... | collective-permute-start | bytes 1572872 | tf_op jit(solution)/shard_map/ppermute | solution.py:37
  (8 other events, 32.7 us)

commit v7 on v4

--- a/solution.py
+++ b/solution.py
@@ -77,8 +77,25 @@
     )(where, offsets, patch_ids, *pieces)
 
 
-def expand_kernel(a0, a1, b0, b1, out):
-    bricks, tc, width = a0.shape
+def sum_kernel(a0, a1, b0, b1, out):
+    out[0] = a0[...] + a1[...]
+    out[1] = b0[...] + b1[...]
+
+
+def sum_rows(a0, a1, b0, b1):
+    return pl.pallas_call(
+        sum_kernel,
+        out_shape=jax.ShapeDtypeStruct((2,) + a0.shape, F32),
+        in_specs=[VMEM] * 4,
+        out_specs=VMEM,
+        compiler_params=PARAMS,
+        cost_estimate=FREE,
+        name="sum_rows",
+    )(a0, a1, b0, b1)
+
+
+def expand_kernel(here, there, out):
+    bricks, tc, width = here.shape[1:]
     rows, depth = bricks * tc, 2 * width
     r = lax.broadcasted_iota(jnp.int32, (rows, rows), 0)
     s = lax.broadcasted_iota(jnp.int32, (rows, rows), 1)
@@ -89,31 +106,31 @@
     part = lax.broadcasted_iota(jnp.int32, (rows, width), 0) % 2
     dot = functools.partial(jnp.dot, preferred_element_type=F32)
     parts = []
-    for u, v in ((a0, a1), (b0, b1)):
-        x = (u[...] + v[...]).reshape(rows, width)
+    for source in (here.at[0], there.at[0], here.at[1], there.at[1]):
+        x = source[...].reshape(rows, width)
         xs = jnp.where(part == 0, pltpu.roll(x, rows - 1, 0), -pltpu.roll(x, 1, 0))
         both = jnp.concatenate([x, xs], axis=1)
         hi = both.astype(BF16)
         parts += [hi, (both - hi.astype(F32)).astype(BF16)]
     woven = dot(jnp.concatenate(parts, axis=0), weave).astype(BF16)
-    wide = jnp.concatenate([woven[i * rows:(i + 1) * rows] for i in range(4)], axis=1)
+    wide = jnp.concatenate([woven[i * rows:(i + 1) * rows] for i in range(8)], axis=1)
     wide = dot(reorder, wide).astype(BF16)
-    for i in range(4):
+    for i in range(8):
         out[i // 2, i % 2] = wide[:, i * depth:(i + 1) * depth]
 
 
-def expand(a0, a1, b0, b1):
-    bricks, tc, width = a0.shape
+def expand(here, there):
+    bricks, tc, width = here.shape[1:]
     rows = bricks * tc
     return pl.pallas_call(
         expand_kernel,
-        out_shape=jax.ShapeDtypeStruct((2, 2, rows, 2 * width), BF16),
-        in_specs=[VMEM] * 4,
+        out_shape=jax.ShapeDtypeStruct((4, 2, rows, 2 * width), BF16),
+        in_specs=[VMEM] * 2,
         out_specs=VMEM,
         compiler_params=PARAMS,
         cost_estimate=FREE,
         name="expand",
-    )(a0, a1, b0, b1)
+    )(here, there)
 
 
 def cut_matrix(where, matrix, messages, local=()):
@@ -175,26 +192,26 @@
     )(*arrays)
 
 
-def term_kernel(el, ec, flat, *rest):
+def term_kernel(rows, flat, *rest):
     dot = functools.partial(jnp.dot, preferred_element_type=F32)
     total = None if len(rest) == 1 else rest[0][...]
-    for n, e in enumerate((el.at[0], ec.at[0], el.at[1], ec.at[1])):
+    for n in range(4):
         for h in range(2):
-            d = dot(e[h], flat[n])
+            d = dot(rows[n, h], flat[n])
             total = d if total is None else total + d
     rest[-1][...] = total
 
 
-def term(el, ec, flat, *so_far):
+def term(rows, flat, *so_far):
     return pl.pallas_call(
         term_kernel,
-        out_shape=jax.ShapeDtypeStruct((el.shape[2], flat.shape[2]), F32),
-        in_specs=[VMEM] * (3 + len(so_far)),
+        out_shape=jax.ShapeDtypeStruct((rows.shape[2], flat.shape[2]), F32),
+        in_specs=[VMEM] * (2 + len(so_far)),
         out_specs=VMEM,
         compiler_params=PARAMS,
         cost_estimate=FREE,
         name="term",
-    )(el, ec, flat, *so_far)
+    )(rows, flat, *so_far)
 
 
 def finish_kernel(a, b, c, out):
@@ -232,14 +249,13 @@
     core = shift(core, dc=1)
     cross = shift(fars[0][1], dc=1)
     flats = [flatten((own, (s,)), (core, (s,)), (fars[0], (0, s)), (cross, (s,))) for s in early]
-    for i in range(2):
-        far[i], rest[i] = lax.optimization_barrier((far[i], rest[i]))
-        fars.append(across(far[i]))
+    far[:2], rest = lax.optimization_barrier((far[:2], rest))
+    fars += [across(far[0]), across(far[1])]
     flats, rest = lax.optimization_barrier((flats, rest))
     from_left, from_right, across_two = rest
-    el = expand(same, across_two, from_left, from_right)
-    matrix, el = lax.optimization_barrier((matrix, el))
-    ec = shift(el, dc=1)
+    here = sum_rows(same, across_two, from_left, from_right)
+    matrix, here = lax.optimization_barrier((matrix, here))
+    rows = expand(here, shift(here, dc=1))
     *more, own = cut_matrix(where, matrix, MESSAGES[3:], ((late, 0),))
     far += more
     fars.append(across(far[2]))
@@ -252,9 +268,9 @@
             cross = shift(fars[s - 1][1], dc=1)
             flats.append(flatten((own, (s - 2,)), (core, (s,)), (fars[s - 1], (0, 0)), (cross, (0,))))
         if s == Z - 1:
-            total = term(el, ec, flats[s])
+            total = term(rows, flats[s])
             break
-        total = term(el, ec, flats[s], *sums[s % 2:s % 2 + 1] if s > 1 else ())
+        total = term(rows, flats[s], *sums[s % 2:s % 2 + 1] if s > 1 else ())
         if s in PACE:
             ahead, total = lax.optimization_barrier((far[len(fars) - 1], total))
             fars.append(across(ahead))

time: 86.7 us -> 88.5 us (1.021)
  starting transfers between devices: 24.7 us -> 28.2 us
  waiting for transfers between devices: 42.8 us -> 40 us
    ppermute x29, starting transfers between devices: 24.7 us -> 28.2 us  [shift(): return lax.ppermute(array, ('grp', 'freq'), pairs)]
    ppermute x29, waiting for transfers between devices: 42.8 us -> 40 us  [shift(): return lax.ppermute(array, ('grp', 'freq'), pairs)]
    pallas_call x9 -> x10, Pallas kernels: 6.22 us -> 6.53 us  [the longest x8 5.61 us: term(): pl.pallas_call(term_kernel, out_shape=jax.ShapeDtypeStruct((rows.shape[2]...]
  transfers between devices with their start and end apart: 29 -> 29, of which waited for: 20 -> 18; matrix products, arithmetic and copies ran while one was open for 2% -> 2% of each run, Pallas kernels for 15% -> 16%
where the time goes in v7:
time: 88.5 us; the launch traced here: 86.7 us
  waiting for transfers between devices  40 us (45%)
  starting transfers between devices  28.2 us (32%)
  Pallas kernels  16.7 us (19%)
  local copies, waits for them, and re-layouts  1.55 us (2%)
    ppermute x29, waiting for transfers between devices, shift(): return lax.ppermute(array, ('grp', 'freq'), pairs)  40 us
    ppermute x29, starting transfers between devices, shift(): return lax.ppermute(array, ('grp', 'freq'), pairs)  28.2 us
    pallas_call x3, Pallas kernels, cut_matrix(): pl.pallas_call(kernel, in_specs=[SMEM, pl.BlockSpec(memory_space=pltpu.HB...  7.36 us
    pallas_call x8, Pallas kernels, term(): pl.pallas_call(term_kernel, out_shape=jax.ShapeDtypeStruct((rows.shape[2]...  5.61 us
  transfers between devices with their start and end apart: 29, of which 18 were waited for; matrix products, arithmetic and copies ran while one was open for 2% of the time, Pallas kernels for 16%

profile of v7, /device:TPU:24, one launch (start us, length us, event | category | flops | bytes accessed | tf_op | source)
XLA Modules:
  0.0 86.7 jit_solution(4055054496860069878)
XLA Ops:
  0.1 1.8 %cut_matrix.3 = bf16[2,2,128,2,512]{4,3,2,1,0:T(2,128)(2,1)S(1)} custom-call(s32[5]{0:T(128)S(1)} %stack.23.place_ref, bf16[128,2,16384]{2,1,0:T(2,128)(2,1)} %src.3), custom_call_target="tpu_custom_call" | custom-call | flops 1000 | bytes 1000 | tf_op jit(solution)/shard_map/cut_matrix/pallas_call | solution.py:163
  1.9 1.6 %collective-permute-start.3 = (bf16[2,2,128,2,512]{4,3,2,1,0:T(2,128)(2,1)S(1)}, bf16[2,2,128,2,512]{4,3,2,1,0:T(2,128)(2,1)S(1)}, u32[]{:S(2)}, u32[]{:S(2)}) collective-permute-start(bf16[2,2,128,2,512]{4,3,2,1,0:T(2,128)(2,1)S(1)} %cut_matrix.3), channel_id=1, source_target_pairs={{0,16},{1,145},{2,18},{3,147},{4,20},{5,149},{6,22},{7,151},{8,24}... | collective-permute-start | bytes 3145736 | tf_op jit(solution)/shard_map/ppermute | solution.py:37
  4.2 2.5 %collective-permute-start.2 = (bf16[8,64,128]{2,1,0:T(8,128)(2,1)S(1)}, bf16[8,64,128]{2,1,0:T(8,128)(2,1)S(1)}, u32[]{:S(2)}, u32[]{:S(2)}) collective-permute-start(bf16[8,64,128]{2,1,0:T(8,128)(2,1)S(1)} %bitcast.22), channel_id=1, source_target_pairs={{0,32},{1,33},{2,34},{3,35},{4,36},{5,37},{6,38},{7,39},{8,40},{9,... | collective-permute-start | bytes 393224 | tf_op jit(solution)/shard_map/ppermute | solution.py:37
  6.7 4.2 %collective-permute-done.r1 = bf16[8,64,128]{2,1,0:T(8,128)(2,1)S(1)} collective-permute-done((bf16[8,64,128]{2,1,0:T(8,128)(2,1)S(1)}, bf16[8,64,128]{2,1,0:T(8,128)(2,1)S(1)}, u32[]{:S(2)}, u32[]{:S(2)}) %collective-permute-start) | collective-permute-done | bytes 131104 | tf_op jit(solution)/shard_map/ppermute | solution.py:37
  10.9 2.8 %cut_matrix.4 = (bf16[2,1,128,2,512]{4,3,2,1,0:T(2,128)(2,1)S(1)}, bf16[2,1,128,2,512]{4,3,2,1,0:T(2,128)(2,1)S(1)}, bf16[2,128,2,512]{3,2,1,0:T(2,128)(2,1)S(1)}, bf16[8,128,2,512]{3,2,1,0:T(2,128)(2,1)S(1)}) custom-call(s32[5]{0:T(128)S(1)} %stack.23.place_ref, bf16[128,2,16384]{2,1,0:T(2,128)(2,1)} %src.3), custom_call_target="tpu_custom_call" | custom-call | flops 1000 | bytes 1000 | tf_op jit(solution)/shard_map/cut_matrix/pallas_call | solution.py:163
  13.9 1.0 %add_rows.1 = (f32[4,64,128]{2,1,0:T(8,128)S(1)}, f32[4,64,128]{2,1,0:T(8,128)S(1)}, f32[4,64,128]{2,1,0:T(8,128)S(1)}, f32[4,64,128]{2,1,0:T(8,128)S(1)}) custom-call(s32[5]{0:T(128)S(1)} %stack.23.place_ref, s32[64]{0:T(128)S(1)} %copy-done.1, s32[64]{0:T(128)S(1)} %copy-done.2, bf16[8,64,128]{2,1,0:T(8,128)(2,1)S(1)} %bitcast.24, ...), custom_call_target="tpu_custom_call" | custom-call | flops 1000 | bytes 1000 | tf_op jit(solution)/shard_map/add_rows/pallas_call | solution.py:68
  14.9 3.1 %collective-permute-done.3.refs_2_ = bf16[2,2,128,2,512]{4,3,2,1,0:T(2,128)(2,1)S(1)} collective-permute-done((bf16[2,2,128,2,512]{4,3,2,1,0:T(2,128)(2,1)S(1)}, bf16[2,2,128,2,512]{4,3,2,1,0:T(2,128)(2,1)S(1)}, u32[]{:S(2)}, u32[]{:S(2)}) %collective-permute-start.3) | collective-permute-done | bytes 1048608 | tf_op jit(solution)/shard_map/ppermute | solution.py:37
  19.2 3.0 %collective-permute-start.7 = (f32[4,64,128]{2,1,0:T(8,128)S(1)}, f32[4,64,128]{2,1,0:T(8,128)S(1)}, u32[]{:S(2)}, u32[]{:S(2)}) collective-permute-start(f32[4,64,128]{2,1,0:T(8,128)S(1)} %get-tuple-element.72), channel_id=1, source_target_pairs={{0,144},{1,145},{2,146},{3,147},{4,148},{5,149},{6,150},{7,151},{8... | collective-permute-start | bytes 393224 | tf_op jit(solution)/shard_map/ppermute | solution.py:37
  22.8 2.9 %collective-permute-done.6.b0 = f32[4,64,128]{2,1,0:T(8,128)S(1)} collective-permute-done((f32[4,64,128]{2,1,0:T(8,128)S(1)}, f32[4,64,128]{2,1,0:T(8,128)S(1)}, u32[]{:S(2)}, u32[]{:S(2)}) %collective-permute-start.6) | collective-permute-done | bytes 131104 | tf_op jit(solution)/shard_map/ppermute | solution.py:37
  25.7 2.1 %collective-permute-done.7.b1 = f32[4,64,128]{2,1,0:T(8,128)S(1)} collective-permute-done((f32[4,64,128]{2,1,0:T(8,128)S(1)}, f32[4,64,128]{2,1,0:T(8,128)S(1)}, u32[]{:S(2)}, u32[]{:S(2)}) %collective-permute-start.7) | collective-permute-done | bytes 131104 | tf_op jit(solution)/shard_map/ppermute | solution.py:37
  29.7 1.2 %collective-permute-start.9 = (f32[2,4,64,128]{3,2,1,0:T(8,128)S(1)}, f32[2,4,64,128]{3,2,1,0:T(8,128)S(1)}, u32[]{:S(2)}, u32[]{:S(2)}) collective-permute-start(f32[2,4,64,128]{3,2,1,0:T(8,128)S(1)} %sum_rows.1.here), channel_id=1, source_target_pairs={{0,1},{1,0},{2,3},{3,2},{4,5},{5,4},{6,7},{7,6},{8,9},{9,8},{10,11... | collective-permute-start | bytes 786440 | tf_op jit(solution)/shard_map/ppermute | solution.py:37
  30.9 1.2 %collective-permute-done.9.there = f32[2,4,64,128]{3,2,1,0:T(8,128)S(1)} collective-permute-done((f32[2,4,64,128]{3,2,1,0:T(8,128)S(1)}, f32[2,4,64,128]{3,2,1,0:T(8,128)S(1)}, u32[]{:S(2)}, u32[]{:S(2)}) %collective-permute-start.9) | collective-permute-done | bytes 262176 | tf_op jit(solution)/shard_map/ppermute | solution.py:37
  33.7 2.0 %collective-permute-start.13 = (f32[256,512]{1,0:T(8,128)S(1)}, f32[256,512]{1,0:T(8,128)S(1)}, u32[]{:S(2)}, u32[]{:S(2)}) collective-permute-start(f32[256,512]{1,0:T(8,128)S(1)} %term.8), channel_id=1, source_target_pairs={{0,2},{1,15},{2,4},{3,1},{4,6},{5,3},{6,8},{7,5},{8,10},{9,7},{10,... | collective-permute-start | bytes 1572872 | tf_op jit(solution)/shard_map/ppermute | solution.py:37
  35.6 2.8 %cut_matrix.5 = (bf16[2,1,128,2,512]{4,3,2,1,0:T(2,128)(2,1)S(1)}, bf16[2,1,128,2,512]{4,3,2,1,0:T(2,128)(2,1)S(1)}, bf16[2,1,128,2,512]{4,3,2,1,0:T(2,128)(2,1)...) custom-call(s32[5]{0:T(128)S(1)} %stack.23.place_ref, bf16[128,2,16384]{2,1,0:T(2,128)(2,1)} %src.3), custom_call_target="tpu_custom_call" | custom-call | flops 1000 | bytes 1000 | tf_op jit(solution)/shard_map/cut_matrix/pallas_call | solution.py:163
  39.3 5.4 %collective-permute-start.12 = (bf16[1,128,2,512]{3,2,1,0:T(2,128)(2,1)S(1)}, bf16[1,128,2,512]{3,2,1,0:T(2,128)(2,1)S(1)}, u32[]{:S(2)}, u32[]{:S(2)}) collective-permute-start(bf16[1,128,2,512]{3,2,1,0:T(2,128)(2,1)S(1)} %slice_bitcast_fusion.6), channel_id=1, source_target_pairs={{0,1},{1,0},{2,3},{3,2},{4,5},{5,4},{6,7},{7,6},{8,9},{9,8},{10,11... | collective-permute-start | bytes 786440 | tf_op jit(solution)/shard_map/ppermute | solution.py:37
  49.4 7.5 %collective-permute-done.15.rest_0_ = f32[256,512]{1,0:T(8,128)S(1)} collective-permute-done((f32[256,512]{1,0:T(8,128)S(1)}, f32[256,512]{1,0:T(8,128)S(1)}, u32[]{:S(2)}, u32[]{:S(2)}) %collective-permute-start.15) | collective-permute-done | bytes 524320 | tf_op jit(solution)/shard_map/ppermute | solution.py:37
  58.1 1.9 %collective-permute-start.17 = (bf16[2,1,128,2,512]{4,3,2,1,0:T(2,128)(2,1)S(1)}, bf16[2,1,128,2,512]{4,3,2,1,0:T(2,128)(2,1)S(1)}, u32[]{:S(2)}, u32[]{:S(2)}) collective-permute-start(bf16[2,1,128,2,512]{4,3,2,1,0:T(2,128)(2,1)S(1)} %get-tuple-element.98), channel_id=1, source_target_pairs={{0,16},{1,145},{2,18},{3,147},{4,20},{5,149},{6,22},{7,151},{8,24}... | collective-permute-start | bytes 1572872 | tf_op jit(solution)/shard_map/ppermute | solution.py:37
  62.0 1.1 %collective-permute-start.25 = (f32[256,512]{1,0:T(8,128)S(1)}, f32[256,512]{1,0:T(8,128)S(1)}, u32[]{:S(2)}, u32[]{:S(2)}) collective-permute-start(f32[256,512]{1,0:T(8,128)S(1)} %term.12), channel_id=1, source_target_pairs={{0,2},{1,15},{2,4},{3,1},{4,6},{5,3},{6,8},{7,5},{8,10},{9,7},{10,... | collective-permute-start | bytes 1572872 | tf_op jit(solution)/shard_map/ppermute | solution.py:37
  63.7 5.4 %collective-permute-done.23.rest_0_ = f32[256,512]{1,0:T(8,128)S(1)} collective-permute-done((f32[256,512]{1,0:T(8,128)S(1)}, f32[256,512]{1,0:T(8,128)S(1)}, u32[]{:S(2)}, u32[]{:S(2)}) %collective-permute-start.23) | collective-permute-done | bytes 524320 | tf_op jit(solution)/shard_map/ppermute | solution.py:37
  72.0 1.4 %collective-permute-done.25.rest_0_ = f32[256,512]{1,0:T(8,128)S(1)} collective-permute-done((f32[256,512]{1,0:T(8,128)S(1)}, f32[256,512]{1,0:T(8,128)S(1)}, u32[]{:S(2)}, u32[]{:S(2)}) %collective-permute-start.25) | collective-permute-done | bytes 524320 | tf_op jit(solution)/shard_map/ppermute | solution.py:37
  74.1 1.9 %collective-permute-start.27 = (f32[256,512]{1,0:T(8,128)S(1)}, f32[256,512]{1,0:T(8,128)S(1)}, u32[]{:S(2)}, u32[]{:S(2)}) collective-permute-start(f32[256,512]{1,0:T(8,128)S(1)} %term.14), channel_id=1, source_target_pairs={{0,2},{1,15},{2,4},{3,1},{4,6},{5,3},{6,8},{7,5},{8,10},{9,7},{10,... | collective-permute-start | bytes 1572872 | tf_op jit(solution)/shard_map/ppermute | solution.py:37
  76.3 1.5 %collective-permute-done.26.refs_3_ = bf16[1,128,2,512]{3,2,1,0:T(2,128)(2,1)S(1)} collective-permute-done((bf16[1,128,2,512]{3,2,1,0:T(2,128)(2,1)S(1)}, bf16[1,128,2,512]{3,2,1,0:T(2,128)(2,1)S(1)}, u32[]{:S(2)}, u32[]{:S(2)}) %collective-permute-start.26) | collective-permute-done | bytes 262176 | tf_op jit(solution)/shard_map/ppermute | solution.py:37
  78.6 4.2 %collective-permute-done.28.c = f32[256,512]{1,0:T(8,128)S(1)} collective-permute-done((f32[256,512]{1,0:T(8,128)S(1)}, f32[256,512]{1,0:T(8,128)S(1)}, u32[]{:S(2)}, u32[]{:S(2)}) %collective-permute-start.28) | collective-permute-done | bytes 524320 | tf_op jit(solution)/shard_map/ppermute | solution.py:37
  82.8 3.0 %collective-permute-done.27.b = f32[256,512]{1,0:T(8,128)S(1)} collective-permute-done((f32[256,512]{1,0:T(8,128)S(1)}, f32[256,512]{1,0:T(8,128)S(1)}, u32[]{:S(2)}, u32[]{:S(2)}) %collective-permute-start.27) | collective-permute-done | bytes 524320 | tf_op jit(solution)/shard_map/ppermute | solution.py:37
  (71 shorter events, 21.2 us)
Async XLA Ops:
  1.9 16.1 %collective-permute-start.3 = (bf16[2,2,128,2,512]{4,3,2,1,0:T(2,128)(2,1)S(1)}, bf16[2,2,128,2,512]{4,3,2,1,0:T(2,128)(2,1)S(1)}, u32[]{:S(2)}, u32[]{:S(2)}) collective-permute-start(bf16[2,2,128,2,512]{4,3,2,1,0:T(2,128)(2,1)S(1)} %cut_matrix.3), channel_id=1, source_target_pairs={{0,16},{1,145},{2,18},{3,147},{4,20},{5,149},{6,22},{7,151},{8,24}... | collective-permute-start | bytes 3145736 | tf_op jit(solution)/shard_map/ppermute | solution.py:37
  3.5 7.4 %collective-permute-start = (bf16[8,64,128]{2,1,0:T(8,128)(2,1)S(1)}, bf16[8,64,128]{2,1,0:T(8,128)(2,1)S(1)}, u32[]{:S(2)}, u32[]{:S(2)}) collective-permute-start(bf16[8,64,128]{2,1,0:T(8,128)(2,1)S(1)} %bitcast.21), channel_id=1, source_target_pairs={{0,96},{1,97},{2,98},{3,99},{4,100},{5,101},{6,102},{7,103},{8,104... | collective-permute-start | bytes 393224 | tf_op jit(solution)/shard_map/ppermute | solution.py:37
  4.2 9.5 %collective-permute-start.2 = (bf16[8,64,128]{2,1,0:T(8,128)(2,1)S(1)}, bf16[8,64,128]{2,1,0:T(8,128)(2,1)S(1)}, u32[]{:S(2)}, u32[]{:S(2)}) collective-permute-start(bf16[8,64,128]{2,1,0:T(8,128)(2,1)S(1)} %bitcast.22), channel_id=1, source_target_pairs={{0,32},{1,33},{2,34},{3,35},{4,36},{5,37},{6,38},{7,39},{8,40},{9,... | collective-permute-start | bytes 393224 | tf_op jit(solution)/shard_map/ppermute | solution.py:37
  6.7 7.2 %collective-permute-start.1 = (bf16[8,64,128]{2,1,0:T(8,128)(2,1)S(1)}, bf16[8,64,128]{2,1,0:T(8,128)(2,1)S(1)}, u32[]{:S(2)}, u32[]{:S(2)}) collective-permute-start(bf16[8,64,128]{2,1,0:T(8,128)(2,1)S(1)} %bitcast.23), channel_id=1, source_target_pairs={{0,64},{1,65},{2,66},{3,67},{4,68},{5,69},{6,70},{7,71},{8,72},{9,... | collective-permute-start | bytes 393224 | tf_op jit(solution)/shard_map/ppermute | solution.py:37
  18.0 11.4 %collective-permute-start.4 = (bf16[8,128,2,512]{3,2,1,0:T(2,128)(2,1)S(1)}, bf16[8,128,2,512]{3,2,1,0:T(2,128)(2,1)S(1)}, u32[]{:S(2)}, u32[]{:S(2)}) collective-permute-start(bf16[8,128,2,512]{3,2,1,0:T(2,128)(2,1)S(1)} %get-tuple-element.67), channel_id=1, source_target_pairs={{0,1},{1,0},{2,3},{3,2},{4,5},{5,4},{6,7},{7,6},{8,9},{9,8},{10,11... | collective-permute-start | bytes 6291464 | tf_op jit(solution)/shard_map/ppermute | solution.py:37
  18.4 11.0 %collective-permute-start.5 = (bf16[2,128,2,512]{3,2,1,0:T(2,128)(2,1)S(1)}, bf16[2,128,2,512]{3,2,1,0:T(2,128)(2,1)S(1)}, u32[]{:S(2)}, u32[]{:S(2)}) collective-permute-start(bf16[2,128,2,512]{3,2,1,0:T(2,128)(2,1)S(1)} %slice_bitcast_fusion), channel_id=1, source_target_pairs={{0,1},{1,0},{2,3},{3,2},{4,5},{5,4},{6,7},{7,6},{8,9},{9,8},{10,11... | collective-permute-start | bytes 1572872 | tf_op jit(solution)/shard_map/ppermute | solution.py:37
  19.0 6.7 %collective-permute-start.6 = (f32[4,64,128]{2,1,0:T(8,128)S(1)}, f32[4,64,128]{2,1,0:T(8,128)S(1)}, u32[]{:S(2)}, u32[]{:S(2)}) collective-permute-start(f32[4,64,128]{2,1,0:T(8,128)S(1)} %get-tuple-element.71), channel_id=1, source_target_pairs={{0,16},{1,17},{2,18},{3,19},{4,20},{5,21},{6,22},{7,23},{8,24},{9,... | collective-permute-start | bytes 393224 | tf_op jit(solution)/shard_map/ppermute | solution.py:37
  19.2 8.5 %collective-permute-start.7 = (f32[4,64,128]{2,1,0:T(8,128)S(1)}, f32[4,64,128]{2,1,0:T(8,128)S(1)}, u32[]{:S(2)}, u32[]{:S(2)}) collective-permute-start(f32[4,64,128]{2,1,0:T(8,128)S(1)} %get-tuple-element.72), channel_id=1, source_target_pairs={{0,144},{1,145},{2,146},{3,147},{4,148},{5,149},{6,150},{7,151},{8... | collective-permute-start | bytes 393224 | tf_op jit(solution)/shard_map/ppermute | solution.py:37
  22.2 6.5 %collective-permute-start.8 = (f32[4,64,128]{2,1,0:T(8,128)S(1)}, f32[4,64,128]{2,1,0:T(8,128)S(1)}, u32[]{:S(2)}, u32[]{:S(2)}) collective-permute-start(f32[4,64,128]{2,1,0:T(8,128)S(1)} %get-tuple-element.73), channel_id=1, source_target_pairs={{0,128},{1,129},{2,130},{3,131},{4,132},{5,133},{6,134},{7,135},{8... | collective-permute-start | bytes 393224 | tf_op jit(solution)/shard_map/ppermute | solution.py:37
  28.7 10.5 %collective-permute-start.11 = (bf16[2,1,128,2,512]{4,3,2,1,0:T(2,128)(2,1)S(1)}, bf16[2,1,128,2,512]{4,3,2,1,0:T(2,128)(2,1)S(1)}, u32[]{:S(2)}, u32[]{:S(2)}) collective-permute-start(bf16[2,1,128,2,512]{4,3,2,1,0:T(2,128)(2,1)S(1)} %get-tuple-element.86), channel_id=1, source_target_pairs={{0,16},{1,145},{2,18},{3,147},{4,20},{5,149},{6,22},{7,151},{8,24}... | collective-permute-start | bytes 1572872 | tf_op jit(solution)/shard_map/ppermute | solution.py:37
  29.7 2.4 %collective-permute-start.9 = (f32[2,4,64,128]{3,2,1,0:T(8,128)S(1)}, f32[2,4,64,128]{3,2,1,0:T(8,128)S(1)}, u32[]{:S(2)}, u32[]{:S(2)}) collective-permute-start(f32[2,4,64,128]{3,2,1,0:T(8,128)S(1)} %sum_rows.1.here), channel_id=1, source_target_pairs={{0,1},{1,0},{2,3},{3,2},{4,5},{5,4},{6,7},{7,6},{8,9},{9,8},{10,11... | collective-permute-start | bytes 786440 | tf_op jit(solution)/shard_map/ppermute | solution.py:37
  33.7 13.1 %collective-permute-start.13 = (f32[256,512]{1,0:T(8,128)S(1)}, f32[256,512]{1,0:T(8,128)S(1)}, u32[]{:S(2)}, u32[]{:S(2)}) collective-permute-start(f32[256,512]{1,0:T(8,128)S(1)} %term.8), channel_id=1, source_target_pairs={{0,2},{1,15},{2,4},{3,1},{4,6},{5,3},{6,8},{7,5},{8,10},{9,7},{10,... | collective-permute-start | bytes 1572872 | tf_op jit(solution)/shard_map/ppermute | solution.py:37
  35.6 11.8 %collective-permute-start.10 = (bf16[2,1,128,2,512]{4,3,2,1,0:T(2,128)(2,1)S(1)}, bf16[2,1,128,2,512]{4,3,2,1,0:T(2,128)(2,1)S(1)}, u32[]{:S(2)}, u32[]{:S(2)}) collective-permute-start(bf16[2,1,128,2,512]{4,3,2,1,0:T(2,128)(2,1)S(1)} %get-tuple-element.84), channel_id=1, source_target_pairs={{0,16},{1,145},{2,18},{3,147},{4,20},{5,149},{6,22},{7,151},{8,24}... | collective-permute-start | bytes 1572872 | tf_op jit(solution)/shard_map/ppermute | solution.py:37
  39.3 7.1 %collective-permute-start.12 = (bf16[1,128,2,512]{3,2,1,0:T(2,128)(2,1)S(1)}, bf16[1,128,2,512]{3,2,1,0:T(2,128)(2,1)S(1)}, u32[]{:S(2)}, u32[]{:S(2)}) collective-permute-start(bf16[1,128,2,512]{3,2,1,0:T(2,128)(2,1)S(1)} %slice_bitcast_fusion.6), channel_id=1, source_target_pairs={{0,1},{1,0},{2,3},{3,2},{4,5},{5,4},{6,7},{7,6},{8,9},{9,8},{10,11... | collective-permute-start | bytes 786440 | tf_op jit(solution)/shard_map/ppermute | solution.py:37
  44.7 12.2 %collective-permute-start.15 = (f32[256,512]{1,0:T(8,128)S(1)}, f32[256,512]{1,0:T(8,128)S(1)}, u32[]{:S(2)}, u32[]{:S(2)}) collective-permute-start(f32[256,512]{1,0:T(8,128)S(1)} %term.9), channel_id=1, source_target_pairs={{0,14},{1,3},{2,0},{3,5},{4,2},{5,7},{6,4},{7,9},{8,6},{9,11},{10,... | collective-permute-start | bytes 1572872 | tf_op jit(solution)/shard_map/ppermute | solution.py:37
  45.7 11.9 %collective-permute-start.19 = (bf16[2,1,128,2,512]{4,3,2,1,0:T(2,128)(2,1)S(1)}, bf16[2,1,128,2,512]{4,3,2,1,0:T(2,128)(2,1)S(1)}, u32[]{:S(2)}, u32[]{:S(2)}) collective-permute-start(bf16[2,1,128,2,512]{4,3,2,1,0:T(2,128)(2,1)S(1)} %get-tuple-element.100), channel_id=1, source_target_pairs={{0,16},{1,145},{2,18},{3,147},{4,20},{5,149},{6,22},{7,151},{8,24}... | collective-permute-start | bytes 1572872 | tf_op jit(solution)/shard_map/ppermute | solution.py:37
  48.0 12.2 %collective-permute-start.21 = (f32[256,512]{1,0:T(8,128)S(1)}, f32[256,512]{1,0:T(8,128)S(1)}, u32[]{:S(2)}, u32[]{:S(2)}) collective-permute-start(f32[256,512]{1,0:T(8,128)S(1)} %term.10), channel_id=1, source_target_pairs={{0,2},{1,15},{2,4},{3,1},{4,6},{5,3},{6,8},{7,5},{8,10},{9,7},{10,... | collective-permute-start | bytes 1572872 | tf_op jit(solution)/shard_map/ppermute | solution.py:37
  48.5 13.3 %collective-permute-start.18 = (bf16[2,1,128,2,512]{4,3,2,1,0:T(2,128)(2,1)S(1)}, bf16[2,1,128,2,512]{4,3,2,1,0:T(2,128)(2,1)S(1)}, u32[]{:S(2)}, u32[]{:S(2)}) collective-permute-start(bf16[2,1,128,2,512]{4,3,2,1,0:T(2,128)(2,1)S(1)} %get-tuple-element.99), channel_id=1, source_target_pairs={{0,16},{1,145},{2,18},{3,147},{4,20},{5,149},{6,22},{7,151},{8,24}... | collective-permute-start | bytes 1572872 | tf_op jit(solution)/shard_map/ppermute | solution.py:37
  57.9 11.2 %collective-permute-start.23 = (f32[256,512]{1,0:T(8,128)S(1)}, f32[256,512]{1,0:T(8,128)S(1)}, u32[]{:S(2)}, u32[]{:S(2)}) collective-permute-start(f32[256,512]{1,0:T(8,128)S(1)} %term.11), channel_id=1, source_target_pairs={{0,14},{1,3},{2,0},{3,5},{4,2},{5,7},{6,4},{7,9},{8,6},{9,11},{10,... | collective-permute-start | bytes 1572872 | tf_op jit(solution)/shard_map/ppermute | solution.py:37
  58.1 11.7 %collective-permute-start.17 = (bf16[2,1,128,2,512]{4,3,2,1,0:T(2,128)(2,1)S(1)}, bf16[2,1,128,2,512]{4,3,2,1,0:T(2,128)(2,1)S(1)}, u32[]{:S(2)}, u32[]{:S(2)}) collective-permute-start(bf16[2,1,128,2,512]{4,3,2,1,0:T(2,128)(2,1)S(1)} %get-tuple-element.98), channel_id=1, source_target_pairs={{0,16},{1,145},{2,18},{3,147},{4,20},{5,149},{6,22},{7,151},{8,24}... | collective-permute-start | bytes 1572872 | tf_op jit(solution)/shard_map/ppermute | solution.py:37
  62.0 11.4 %collective-permute-start.25 = (f32[256,512]{1,0:T(8,128)S(1)}, f32[256,512]{1,0:T(8,128)S(1)}, u32[]{:S(2)}, u32[]{:S(2)}) collective-permute-start(f32[256,512]{1,0:T(8,128)S(1)} %term.12), channel_id=1, source_target_pairs={{0,2},{1,15},{2,4},{3,1},{4,6},{5,3},{6,8},{7,5},{8,10},{9,7},{10,... | collective-permute-start | bytes 1572872 | tf_op jit(solution)/shard_map/ppermute | solution.py:37
  63.1 11.0 %collective-permute-start.16 = (bf16[2,1,128,2,512]{4,3,2,1,0:T(2,128)(2,1)S(1)}, bf16[2,1,128,2,512]{4,3,2,1,0:T(2,128)(2,1)S(1)}, u32[]{:S(2)}, u32[]{:S(2)}) collective-permute-start(bf16[2,1,128,2,512]{4,3,2,1,0:T(2,128)(2,1)S(1)} %get-tuple-element.97), channel_id=1, source_target_pairs={{0,16},{1,145},{2,18},{3,147},{4,20},{5,149},{6,22},{7,151},{8,24}... | collective-permute-start | bytes 1572872 | tf_op jit(solution)/shard_map/ppermute | solution.py:37
  70.3 12.5 %collective-permute-start.28 = (f32[256,512]{1,0:T(8,128)S(1)}, f32[256,512]{1,0:T(8,128)S(1)}, u32[]{:S(2)}, u32[]{:S(2)}) collective-permute-start(f32[256,512]{1,0:T(8,128)S(1)} %term.13), channel_id=1, source_target_pairs={{0,14},{1,3},{2,0},{3,5},{4,2},{5,7},{6,4},{7,9},{8,6},{9,11},{10,... | collective-permute-start | bytes 1572872 | tf_op jit(solution)/shard_map/ppermute | solution.py:37
  74.1 11.7 %collective-permute-start.27 = (f32[256,512]{1,0:T(8,128)S(1)}, f32[256,512]{1,0:T(8,128)S(1)}, u32[]{:S(2)}, u32[]{:S(2)}) collective-permute-start(f32[256,512]{1,0:T(8,128)S(1)} %term.14), channel_id=1, source_target_pairs={{0,2},{1,15},{2,4},{3,1},{4,6},{5,3},{6,8},{7,5},{8,10},{9,7},{10,... | collective-permute-start | bytes 1572872 | tf_op jit(solution)/shard_map/ppermute | solution.py:37
  (8 other events, 33.2 us)

commit v8 on v3

--- a/solution.py
+++ b/solution.py
@@ -232,7 +232,7 @@
     core = shift(core, dc=1)
     cross = shift(fars[0][1], dc=1)
     flats = [flatten((own, (s,)), (core, (s,)), (fars[0], (0, s)), (cross, (s,))) for s in early]
-    far[0], rest[0] = lax.optimization_barrier((far[0], rest[0]))
+    far[0], rest[2] = lax.optimization_barrier((far[0], rest[2]))
     fars.append(across(far[0]))
     flats, rest = lax.optimization_barrier((flats, rest))
     from_left, from_right, across_two = rest

time: 86.3 us -> 86.3 us (level)
  transfers between devices with their start and end apart: 29 -> 29, of which waited for: 24 -> 22; matrix products, arithmetic and copies ran while one was open for 2% -> 2% of each run, Pallas kernels for 15% -> 15%
where the time goes in v8:
time: 86.3 us; the launch traced here: 85.7 us
  waiting for transfers between devices  40.4 us (47%)
  starting transfers between devices  27.1 us (31%)
  Pallas kernels  16.4 us (19%)
  local copies, waits for them, and re-layouts  1.55 us (2%)
    ppermute x29, waiting for transfers between devices, shift(): return lax.ppermute(array, ('grp', 'freq'), pairs)  40.4 us
    ppermute x29, starting transfers between devices, shift(): return lax.ppermute(array, ('grp', 'freq'), pairs)  27.1 us
    pallas_call x3, Pallas kernels, cut_matrix(): pl.pallas_call(kernel, in_specs=[SMEM, pl.BlockSpec(memory_space=pltpu.HB...  7.36 us
    pallas_call x8, Pallas kernels, term(): pl.pallas_call(term_kernel, out_shape=jax.ShapeDtypeStruct((el.shape[2],...  5.6 us
  transfers between devices with their start and end apart: 29, of which 22 were waited for; matrix products, arithmetic and copies ran while one was open for 2% of the time, Pallas kernels for 15%

profile of v8, /device:TPU:24, one launch (start us, length us, event | category | flops | bytes accessed | tf_op | source)
XLA Modules:
  0.0 85.7 jit_solution(10413517122423902416)
XLA Ops:
  0.1 1.8 %cut_matrix.3 = bf16[2,2,128,2,512]{4,3,2,1,0:T(2,128)(2,1)S(1)} custom-call(s32[5]{0:T(128)S(1)} %stack.23.place_ref, bf16[128,2,16384]{2,1,0:T(2,128)(2,1)} %src.3), custom_call_target="tpu_custom_call" | custom-call | flops 1000 | bytes 1000 | tf_op jit(solution)/shard_map/cut_matrix/pallas_call | solution.py:146
  1.9 1.6 %collective-permute-start.3 = (bf16[2,2,128,2,512]{4,3,2,1,0:T(2,128)(2,1)S(1)}, bf16[2,2,128,2,512]{4,3,2,1,0:T(2,128)(2,1)S(1)}, u32[]{:S(2)}, u32[]{:S(2)}) collective-permute-start(bf16[2,2,128,2,512]{4,3,2,1,0:T(2,128)(2,1)S(1)} %cut_matrix.3), channel_id=1, source_target_pairs={{0,16},{1,145},{2,18},{3,147},{4,20},{5,149},{6,22},{7,151},{8,24}... | collective-permute-start | bytes 3145736 | tf_op jit(solution)/shard_map/ppermute | solution.py:37
  4.2 2.5 %collective-permute-start.2 = (bf16[8,64,128]{2,1,0:T(8,128)(2,1)S(1)}, bf16[8,64,128]{2,1,0:T(8,128)(2,1)S(1)}, u32[]{:S(2)}, u32[]{:S(2)}) collective-permute-start(bf16[8,64,128]{2,1,0:T(8,128)(2,1)S(1)} %bitcast.22), channel_id=1, source_target_pairs={{0,32},{1,33},{2,34},{3,35},{4,36},{5,37},{6,38},{7,39},{8,40},{9,... | collective-permute-start | bytes 393224 | tf_op jit(solution)/shard_map/ppermute | solution.py:37
  6.7 4.2 %collective-permute-done.r1 = bf16[8,64,128]{2,1,0:T(8,128)(2,1)S(1)} collective-permute-done((bf16[8,64,128]{2,1,0:T(8,128)(2,1)S(1)}, bf16[8,64,128]{2,1,0:T(8,128)(2,1)S(1)}, u32[]{:S(2)}, u32[]{:S(2)}) %collective-permute-start) | collective-permute-done | bytes 131104 | tf_op jit(solution)/shard_map/ppermute | solution.py:37
  10.9 2.6 %cut_matrix.4 = (bf16[2,1,128,2,512]{4,3,2,1,0:T(2,128)(2,1)S(1)}, bf16[2,128,2,512]{3,2,1,0:T(2,128)(2,1)S(1)}, bf16[8,128,2,512]{3,2,1,0:T(2,128)(2,1)S(1)}) custom-call(s32[5]{0:T(128)S(1)} %stack.23.place_ref, bf16[128,2,16384]{2,1,0:T(2,128)(2,1)} %src.3), custom_call_target="tpu_custom_call" | custom-call | flops 1000 | bytes 1000 | tf_op jit(solution)/shard_map/cut_matrix/pallas_call | solution.py:146
  14.9 3.1 %collective-permute-done.3.refs_2_ = bf16[2,2,128,2,512]{4,3,2,1,0:T(2,128)(2,1)S(1)} collective-permute-done((bf16[2,2,128,2,512]{4,3,2,1,0:T(2,128)(2,1)S(1)}, bf16[2,2,128,2,512]{4,3,2,1,0:T(2,128)(2,1)S(1)}, u32[]{:S(2)}, u32[]{:S(2)}) %collective-permute-start.3) | collective-permute-done | bytes 1048608 | tf_op jit(solution)/shard_map/ppermute | solution.py:37
  19.0 1.8 %collective-permute-start.8 = (f32[4,64,128]{2,1,0:T(8,128)S(1)}, f32[4,64,128]{2,1,0:T(8,128)S(1)}, u32[]{:S(2)}, u32[]{:S(2)}) collective-permute-start(f32[4,64,128]{2,1,0:T(8,128)S(1)} %get-tuple-element.69), channel_id=1, source_target_pairs={{0,128},{1,129},{2,130},{3,131},{4,132},{5,133},{6,134},{7,135},{8... | collective-permute-start | bytes 393224 | tf_op jit(solution)/shard_map/ppermute | solution.py:37
  21.4 2.6 %collective-permute-start.7 = (f32[4,64,128]{2,1,0:T(8,128)S(1)}, f32[4,64,128]{2,1,0:T(8,128)S(1)}, u32[]{:S(2)}, u32[]{:S(2)}) collective-permute-start(f32[4,64,128]{2,1,0:T(8,128)S(1)} %get-tuple-element.67), channel_id=1, source_target_pairs={{0,144},{1,145},{2,146},{3,147},{4,148},{5,149},{6,150},{7,151},{8... | collective-permute-start | bytes 393224 | tf_op jit(solution)/shard_map/ppermute | solution.py:37
  24.0 2.8 %collective-permute-done.8.a1 = f32[4,64,128]{2,1,0:T(8,128)S(1)} collective-permute-done((f32[4,64,128]{2,1,0:T(8,128)S(1)}, f32[4,64,128]{2,1,0:T(8,128)S(1)}, u32[]{:S(2)}, u32[]{:S(2)}) %collective-permute-start.8) | collective-permute-done | bytes 131104 | tf_op jit(solution)/shard_map/ppermute | solution.py:37
  27.1 1.7 %collective-permute-done.6.b0 = f32[4,64,128]{2,1,0:T(8,128)S(1)} collective-permute-done((f32[4,64,128]{2,1,0:T(8,128)S(1)}, f32[4,64,128]{2,1,0:T(8,128)S(1)}, u32[]{:S(2)}, u32[]{:S(2)}) %collective-permute-start.6) | collective-permute-done | bytes 131104 | tf_op jit(solution)/shard_map/ppermute | solution.py:37
  32.1 2.0 %collective-permute-start.13 = (f32[256,512]{1,0:T(8,128)S(1)}, f32[256,512]{1,0:T(8,128)S(1)}, u32[]{:S(2)}, u32[]{:S(2)}) collective-permute-start(f32[256,512]{1,0:T(8,128)S(1)} %term.8), channel_id=1, source_target_pairs={{0,2},{1,15},{2,4},{3,1},{4,6},{5,3},{6,8},{7,5},{8,10},{9,7},{10,... | collective-permute-start | bytes 1572872 | tf_op jit(solution)/shard_map/ppermute | solution.py:37
  34.1 3.0 %cut_matrix.5 = (bf16[2,1,128,2,512]{4,3,2,1,0:T(2,128)(2,1)S(1)}, bf16[2,1,128,2,512]{4,3,2,1,0:T(2,128)(2,1)S(1)}, bf16[2,1,128,2,512]{4,3,2,1,0:T(2,128)(2,1)...) custom-call(s32[5]{0:T(128)S(1)} %stack.23.place_ref, ...), custom_call_target="tpu_custom_call" | custom-call | flops 1000 | bytes 1000 | tf_op jit(solution)/shard_map/cut_matrix/pallas_call | solution.py:146
  38.2 1.8 %collective-permute-done.11.refs_2_ = bf16[2,1,128,2,512]{4,3,2,1,0:T(2,128)(2,1)S(1)} collective-permute-done((bf16[2,1,128,2,512]{4,3,2,1,0:T(2,128)(2,1)S(1)}, bf16[2,1,128,2,512]{4,3,2,1,0:T(2,128)(2,1)S(1)}, u32[]{:S(2)}, u32[]{:S(2)}) %collective-permute-start.11) | collective-permute-done | bytes 524320 | tf_op jit(solution)/shard_map/ppermute | solution.py:37
  40.1 3.6 %collective-permute-start.12 = (bf16[1,128,2,512]{3,2,1,0:T(2,128)(2,1)S(1)}, bf16[1,128,2,512]{3,2,1,0:T(2,128)(2,1)S(1)}, u32[]{:S(2)}, u32[]{:S(2)}) collective-permute-start(bf16[1,128,2,512]{3,2,1,0:T(2,128)(2,1)S(1)} %slice_bitcast_fusion.6), channel_id=1, source_target_pairs={{0,1},{1,0},{2,3},{3,2},{4,5},{5,4},{6,7},{7,6},{8,9},{9,8},{10,11... | collective-permute-start | bytes 786440 | tf_op jit(solution)/shard_map/ppermute | solution.py:37
  43.7 2.6 %collective-permute-start.15 = (f32[256,512]{1,0:T(8,128)S(1)}, f32[256,512]{1,0:T(8,128)S(1)}, u32[]{:S(2)}, u32[]{:S(2)}) collective-permute-start(f32[256,512]{1,0:T(8,128)S(1)} %term.9), channel_id=1, source_target_pairs={{0,14},{1,3},{2,0},{3,5},{4,2},{5,7},{6,4},{7,9},{8,6},{9,11},{10,... | collective-permute-start | bytes 1572872 | tf_op jit(solution)/shard_map/ppermute | solution.py:37
  47.7 1.9 %collective-permute-start.14 = (bf16[1,128,2,512]{3,2,1,0:T(2,128)(2,1)S(1)}, bf16[1,128,2,512]{3,2,1,0:T(2,128)(2,1)S(1)}, u32[]{:S(2)}, u32[]{:S(2)}) collective-permute-start(bf16[1,128,2,512]{3,2,1,0:T(2,128)(2,1)S(1)} %slice_bitcast_fusion.5), channel_id=1, source_target_pairs={{0,1},{1,0},{2,3},{3,2},{4,5},{5,4},{6,7},{7,6},{8,9},{9,8},{10,11... | collective-permute-start | bytes 786440 | tf_op jit(solution)/shard_map/ppermute | solution.py:37
  50.9 2.8 %collective-permute-done.15.rest_0_ = f32[256,512]{1,0:T(8,128)S(1)} collective-permute-done((f32[256,512]{1,0:T(8,128)S(1)}, f32[256,512]{1,0:T(8,128)S(1)}, u32[]{:S(2)}, u32[]{:S(2)}) %collective-permute-start.15) | collective-permute-done | bytes 524320 | tf_op jit(solution)/shard_map/ppermute | solution.py:37
  54.4 2.4 %collective-permute-done.19.refs_2_ = bf16[2,1,128,2,512]{4,3,2,1,0:T(2,128)(2,1)S(1)} collective-permute-done((bf16[2,1,128,2,512]{4,3,2,1,0:T(2,128)(2,1)S(1)}, bf16[2,1,128,2,512]{4,3,2,1,0:T(2,128)(2,1)S(1)}, u32[]{:S(2)}, u32[]{:S(2)}) %collective-permute-start.19) | collective-permute-done | bytes 524320 | tf_op jit(solution)/shard_map/ppermute | solution.py:37
  60.7 1.7 %collective-permute-done.18.refs_2_ = bf16[2,1,128,2,512]{4,3,2,1,0:T(2,128)(2,1)S(1)} collective-permute-done((bf16[2,1,128,2,512]{4,3,2,1,0:T(2,128)(2,1)S(1)}, bf16[2,1,128,2,512]{4,3,2,1,0:T(2,128)(2,1)S(1)}, u32[]{:S(2)}, u32[]{:S(2)}) %collective-permute-start.18) | collective-permute-done | bytes 524320 | tf_op jit(solution)/shard_map/ppermute | solution.py:37
  64.3 2.5 %collective-permute-done.23.rest_0_ = f32[256,512]{1,0:T(8,128)S(1)} collective-permute-done((f32[256,512]{1,0:T(8,128)S(1)}, f32[256,512]{1,0:T(8,128)S(1)}, u32[]{:S(2)}, u32[]{:S(2)}) %collective-permute-start.23) | collective-permute-done | bytes 524320 | tf_op jit(solution)/shard_map/ppermute | solution.py:37
  69.1 1.8 %collective-permute-start.28 = (f32[256,512]{1,0:T(8,128)S(1)}, f32[256,512]{1,0:T(8,128)S(1)}, u32[]{:S(2)}, u32[]{:S(2)}) collective-permute-start(f32[256,512]{1,0:T(8,128)S(1)} %term.13), channel_id=1, source_target_pairs={{0,14},{1,3},{2,0},{3,5},{4,2},{5,7},{6,4},{7,9},{8,6},{9,11},{10,... | collective-permute-start | bytes 1572872 | tf_op jit(solution)/shard_map/ppermute | solution.py:37
  71.1 2.1 %collective-permute-done.25.rest_0_ = f32[256,512]{1,0:T(8,128)S(1)} collective-permute-done((f32[256,512]{1,0:T(8,128)S(1)}, f32[256,512]{1,0:T(8,128)S(1)}, u32[]{:S(2)}, u32[]{:S(2)}) %collective-permute-start.25) | collective-permute-done | bytes 524320 | tf_op jit(solution)/shard_map/ppermute | solution.py:37
  78.6 3.1 %collective-permute-done.28.c = f32[256,512]{1,0:T(8,128)S(1)} collective-permute-done((f32[256,512]{1,0:T(8,128)S(1)}, f32[256,512]{1,0:T(8,128)S(1)}, u32[]{:S(2)}, u32[]{:S(2)}) %collective-permute-start.28) | collective-permute-done | bytes 524320 | tf_op jit(solution)/shard_map/ppermute | solution.py:37
  81.7 3.1 %collective-permute-done.27.b = f32[256,512]{1,0:T(8,128)S(1)} collective-permute-done((f32[256,512]{1,0:T(8,128)S(1)}, f32[256,512]{1,0:T(8,128)S(1)}, u32[]{:S(2)}, u32[]{:S(2)}) %collective-permute-start.27) | collective-permute-done | bytes 524320 | tf_op jit(solution)/shard_map/ppermute | solution.py:37
  (70 shorter events, 26.6 us)
Async XLA Ops:
  1.9 16.1 %collective-permute-start.3 = (bf16[2,2,128,2,512]{4,3,2,1,0:T(2,128)(2,1)S(1)}, bf16[2,2,128,2,512]{4,3,2,1,0:T(2,128)(2,1)S(1)}, u32[]{:S(2)}, u32[]{:S(2)}) collective-permute-start(bf16[2,2,128,2,512]{4,3,2,1,0:T(2,128)(2,1)S(1)} %cut_matrix.3), channel_id=1, source_target_pairs={{0,16},{1,145},{2,18},{3,147},{4,20},{5,149},{6,22},{7,151},{8,24}... | collective-permute-start | bytes 3145736 | tf_op jit(solution)/shard_map/ppermute | solution.py:37
  3.5 7.4 %collective-permute-start = (bf16[8,64,128]{2,1,0:T(8,128)(2,1)S(1)}, bf16[8,64,128]{2,1,0:T(8,128)(2,1)S(1)}, u32[]{:S(2)}, u32[]{:S(2)}) collective-permute-start(bf16[8,64,128]{2,1,0:T(8,128)(2,1)S(1)} %bitcast.21), channel_id=1, source_target_pairs={{0,96},{1,97},{2,98},{3,99},{4,100},{5,101},{6,102},{7,103},{8,104... | collective-permute-start | bytes 393224 | tf_op jit(solution)/shard_map/ppermute | solution.py:37
  4.2 9.3 %collective-permute-start.2 = (bf16[8,64,128]{2,1,0:T(8,128)(2,1)S(1)}, bf16[8,64,128]{2,1,0:T(8,128)(2,1)S(1)}, u32[]{:S(2)}, u32[]{:S(2)}) collective-permute-start(bf16[8,64,128]{2,1,0:T(8,128)(2,1)S(1)} %bitcast.22), channel_id=1, source_target_pairs={{0,32},{1,33},{2,34},{3,35},{4,36},{5,37},{6,38},{7,39},{8,40},{9,... | collective-permute-start | bytes 393224 | tf_op jit(solution)/shard_map/ppermute | solution.py:37
  6.7 7.2 %collective-permute-start.1 = (bf16[8,64,128]{2,1,0:T(8,128)(2,1)S(1)}, bf16[8,64,128]{2,1,0:T(8,128)(2,1)S(1)}, u32[]{:S(2)}, u32[]{:S(2)}) collective-permute-start(bf16[8,64,128]{2,1,0:T(8,128)(2,1)S(1)} %bitcast.23), channel_id=1, source_target_pairs={{0,64},{1,65},{2,66},{3,67},{4,68},{5,69},{6,70},{7,71},{8,72},{9,... | collective-permute-start | bytes 393224 | tf_op jit(solution)/shard_map/ppermute | solution.py:37
  18.0 8.8 %collective-permute-start.4 = (bf16[8,128,2,512]{3,2,1,0:T(2,128)(2,1)S(1)}, bf16[8,128,2,512]{3,2,1,0:T(2,128)(2,1)S(1)}, u32[]{:S(2)}, u32[]{:S(2)}) collective-permute-start(bf16[8,128,2,512]{3,2,1,0:T(2,128)(2,1)S(1)} %get-tuple-element.64), channel_id=1, source_target_pairs={{0,1},{1,0},{2,3},{3,2},{4,5},{5,4},{6,7},{7,6},{8,9},{9,8},{10,11... | collective-permute-start | bytes 6291464 | tf_op jit(solution)/shard_map/ppermute | solution.py:37
  18.4 8.4 %collective-permute-start.5 = (bf16[2,128,2,512]{3,2,1,0:T(2,128)(2,1)S(1)}, bf16[2,128,2,512]{3,2,1,0:T(2,128)(2,1)S(1)}, u32[]{:S(2)}, u32[]{:S(2)}) collective-permute-start(bf16[2,128,2,512]{3,2,1,0:T(2,128)(2,1)S(1)} %slice_bitcast_fusion), channel_id=1, source_target_pairs={{0,1},{1,0},{2,3},{3,2},{4,5},{5,4},{6,7},{7,6},{8,9},{9,8},{10,11... | collective-permute-start | bytes 1572872 | tf_op jit(solution)/shard_map/ppermute | solution.py:37
  19.0 7.9 %collective-permute-start.8 = (f32[4,64,128]{2,1,0:T(8,128)S(1)}, f32[4,64,128]{2,1,0:T(8,128)S(1)}, u32[]{:S(2)}, u32[]{:S(2)}) collective-permute-start(f32[4,64,128]{2,1,0:T(8,128)S(1)} %get-tuple-element.69), channel_id=1, source_target_pairs={{0,128},{1,129},{2,130},{3,131},{4,132},{5,133},{6,134},{7,135},{8... | collective-permute-start | bytes 393224 | tf_op jit(solution)/shard_map/ppermute | solution.py:37
  20.8 8.0 %collective-permute-start.6 = (f32[4,64,128]{2,1,0:T(8,128)S(1)}, f32[4,64,128]{2,1,0:T(8,128)S(1)}, u32[]{:S(2)}, u32[]{:S(2)}) collective-permute-start(f32[4,64,128]{2,1,0:T(8,128)S(1)} %get-tuple-element.66), channel_id=1, source_target_pairs={{0,16},{1,17},{2,18},{3,19},{4,20},{5,21},{6,22},{7,23},{8,24},{9,... | collective-permute-start | bytes 393224 | tf_op jit(solution)/shard_map/ppermute | solution.py:37
  21.4 7.4 %collective-permute-start.7 = (f32[4,64,128]{2,1,0:T(8,128)S(1)}, f32[4,64,128]{2,1,0:T(8,128)S(1)}, u32[]{:S(2)}, u32[]{:S(2)}) collective-permute-start(f32[4,64,128]{2,1,0:T(8,128)S(1)} %get-tuple-element.67), channel_id=1, source_target_pairs={{0,144},{1,145},{2,146},{3,147},{4,148},{5,149},{6,150},{7,151},{8... | collective-permute-start | bytes 393224 | tf_op jit(solution)/shard_map/ppermute | solution.py:37
  29.5 10.5 %collective-permute-start.11 = (bf16[2,1,128,2,512]{4,3,2,1,0:T(2,128)(2,1)S(1)}, bf16[2,1,128,2,512]{4,3,2,1,0:T(2,128)(2,1)S(1)}, u32[]{:S(2)}, u32[]{:S(2)}) collective-permute-start(bf16[2,1,128,2,512]{4,3,2,1,0:T(2,128)(2,1)S(1)} %get-tuple-element.80), channel_id=1, source_target_pairs={{0,16},{1,145},{2,18},{3,147},{4,20},{5,149},{6,22},{7,151},{8,24}... | collective-permute-start | bytes 1572872 | tf_op jit(solution)/shard_map/ppermute | solution.py:37
  32.1 14.4 %collective-permute-start.13 = (f32[256,512]{1,0:T(8,128)S(1)}, f32[256,512]{1,0:T(8,128)S(1)}, u32[]{:S(2)}, u32[]{:S(2)}) collective-permute-start(f32[256,512]{1,0:T(8,128)S(1)} %term.8), channel_id=1, source_target_pairs={{0,2},{1,15},{2,4},{3,1},{4,6},{5,3},{6,8},{7,5},{8,10},{9,7},{10,... | collective-permute-start | bytes 1572872 | tf_op jit(solution)/shard_map/ppermute | solution.py:37
  37.1 10.5 %collective-permute-start.10 = (bf16[2,1,128,2,512]{4,3,2,1,0:T(2,128)(2,1)S(1)}, bf16[2,1,128,2,512]{4,3,2,1,0:T(2,128)(2,1)S(1)}, u32[]{:S(2)}, u32[]{:S(2)}) collective-permute-start(bf16[2,1,128,2,512]{4,3,2,1,0:T(2,128)(2,1)S(1)} %get-tuple-element.78), channel_id=1, source_target_pairs={{0,16},{1,145},{2,18},{3,147},{4,20},{5,149},{6,22},{7,151},{8,24}... | collective-permute-start | bytes 1572872 | tf_op jit(solution)/shard_map/ppermute | solution.py:37
  40.1 6.2 %collective-permute-start.12 = (bf16[1,128,2,512]{3,2,1,0:T(2,128)(2,1)S(1)}, bf16[1,128,2,512]{3,2,1,0:T(2,128)(2,1)S(1)}, u32[]{:S(2)}, u32[]{:S(2)}) collective-permute-start(bf16[1,128,2,512]{3,2,1,0:T(2,128)(2,1)S(1)} %slice_bitcast_fusion.6), channel_id=1, source_target_pairs={{0,1},{1,0},{2,3},{3,2},{4,5},{5,4},{6,7},{7,6},{8,9},{9,8},{10,11... | collective-permute-start | bytes 786440 | tf_op jit(solution)/shard_map/ppermute | solution.py:37
  43.7 9.9 %collective-permute-start.15 = (f32[256,512]{1,0:T(8,128)S(1)}, f32[256,512]{1,0:T(8,128)S(1)}, u32[]{:S(2)}, u32[]{:S(2)}) collective-permute-start(f32[256,512]{1,0:T(8,128)S(1)} %term.9), channel_id=1, source_target_pairs={{0,14},{1,3},{2,0},{3,5},{4,2},{5,7},{6,4},{7,9},{8,6},{9,11},{10,... | collective-permute-start | bytes 1572872 | tf_op jit(solution)/shard_map/ppermute | solution.py:37
  46.4 10.4 %collective-permute-start.19 = (bf16[2,1,128,2,512]{4,3,2,1,0:T(2,128)(2,1)S(1)}, bf16[2,1,128,2,512]{4,3,2,1,0:T(2,128)(2,1)S(1)}, u32[]{:S(2)}, u32[]{:S(2)}) collective-permute-start(bf16[2,1,128,2,512]{4,3,2,1,0:T(2,128)(2,1)S(1)} %get-tuple-element.94), channel_id=1, source_target_pairs={{0,16},{1,145},{2,18},{3,147},{4,20},{5,149},{6,22},{7,151},{8,24}... | collective-permute-start | bytes 1572872 | tf_op jit(solution)/shard_map/ppermute | solution.py:37
  47.7 3.1 %collective-permute-start.14 = (bf16[1,128,2,512]{3,2,1,0:T(2,128)(2,1)S(1)}, bf16[1,128,2,512]{3,2,1,0:T(2,128)(2,1)S(1)}, u32[]{:S(2)}, u32[]{:S(2)}) collective-permute-start(bf16[1,128,2,512]{3,2,1,0:T(2,128)(2,1)S(1)} %slice_bitcast_fusion.5), channel_id=1, source_target_pairs={{0,1},{1,0},{2,3},{3,2},{4,5},{5,4},{6,7},{7,6},{8,9},{9,8},{10,11... | collective-permute-start | bytes 786440 | tf_op jit(solution)/shard_map/ppermute | solution.py:37
  49.6 10.4 %collective-permute-start.21 = (f32[256,512]{1,0:T(8,128)S(1)}, f32[256,512]{1,0:T(8,128)S(1)}, u32[]{:S(2)}, u32[]{:S(2)}) collective-permute-start(f32[256,512]{1,0:T(8,128)S(1)} %term.10), channel_id=1, source_target_pairs={{0,2},{1,15},{2,4},{3,1},{4,6},{5,3},{6,8},{7,5},{8,10},{9,7},{10,... | collective-permute-start | bytes 1572872 | tf_op jit(solution)/shard_map/ppermute | solution.py:37
  49.8 12.6 %collective-permute-start.18 = (bf16[2,1,128,2,512]{4,3,2,1,0:T(2,128)(2,1)S(1)}, bf16[2,1,128,2,512]{4,3,2,1,0:T(2,128)(2,1)S(1)}, u32[]{:S(2)}, u32[]{:S(2)}) collective-permute-start(bf16[2,1,128,2,512]{4,3,2,1,0:T(2,128)(2,1)S(1)} %get-tuple-element.93), channel_id=1, source_target_pairs={{0,16},{1,145},{2,18},{3,147},{4,20},{5,149},{6,22},{7,151},{8,24}... | collective-permute-start | bytes 1572872 | tf_op jit(solution)/shard_map/ppermute | solution.py:37
  57.0 9.7 %collective-permute-start.23 = (f32[256,512]{1,0:T(8,128)S(1)}, f32[256,512]{1,0:T(8,128)S(1)}, u32[]{:S(2)}, u32[]{:S(2)}) collective-permute-start(f32[256,512]{1,0:T(8,128)S(1)} %term.11), channel_id=1, source_target_pairs={{0,14},{1,3},{2,0},{3,5},{4,2},{5,7},{6,4},{7,9},{8,6},{9,11},{10,... | collective-permute-start | bytes 1572872 | tf_op jit(solution)/shard_map/ppermute | solution.py:37
  58.4 10.4 %collective-permute-start.17 = (bf16[2,1,128,2,512]{4,3,2,1,0:T(2,128)(2,1)S(1)}, bf16[2,1,128,2,512]{4,3,2,1,0:T(2,128)(2,1)S(1)}, u32[]{:S(2)}, u32[]{:S(2)}) collective-permute-start(bf16[2,1,128,2,512]{4,3,2,1,0:T(2,128)(2,1)S(1)} %get-tuple-element.92), channel_id=1, source_target_pairs={{0,16},{1,145},{2,18},{3,147},{4,20},{5,149},{6,22},{7,151},{8,24}... | collective-permute-start | bytes 1572872 | tf_op jit(solution)/shard_map/ppermute | solution.py:37
  62.6 10.5 %collective-permute-start.25 = (f32[256,512]{1,0:T(8,128)S(1)}, f32[256,512]{1,0:T(8,128)S(1)}, u32[]{:S(2)}, u32[]{:S(2)}) collective-permute-start(f32[256,512]{1,0:T(8,128)S(1)} %term.12), channel_id=1, source_target_pairs={{0,2},{1,15},{2,4},{3,1},{4,6},{5,3},{6,8},{7,5},{8,10},{9,7},{10,... | collective-permute-start | bytes 1572872 | tf_op jit(solution)/shard_map/ppermute | solution.py:37
  62.7 11.7 %collective-permute-start.16 = (bf16[2,1,128,2,512]{4,3,2,1,0:T(2,128)(2,1)S(1)}, bf16[2,1,128,2,512]{4,3,2,1,0:T(2,128)(2,1)S(1)}, u32[]{:S(2)}, u32[]{:S(2)}) collective-permute-start(bf16[2,1,128,2,512]{4,3,2,1,0:T(2,128)(2,1)S(1)} %get-tuple-element.91), channel_id=1, source_target_pairs={{0,16},{1,145},{2,18},{3,147},{4,20},{5,149},{6,22},{7,151},{8,24}... | collective-permute-start | bytes 1572872 | tf_op jit(solution)/shard_map/ppermute | solution.py:37
  69.1 12.6 %collective-permute-start.28 = (f32[256,512]{1,0:T(8,128)S(1)}, f32[256,512]{1,0:T(8,128)S(1)}, u32[]{:S(2)}, u32[]{:S(2)}) collective-permute-start(f32[256,512]{1,0:T(8,128)S(1)} %term.13), channel_id=1, source_target_pairs={{0,14},{1,3},{2,0},{3,5},{4,2},{5,7},{6,4},{7,9},{8,6},{9,11},{10,... | collective-permute-start | bytes 1572872 | tf_op jit(solution)/shard_map/ppermute | solution.py:37
  74.5 10.4 %collective-permute-start.27 = (f32[256,512]{1,0:T(8,128)S(1)}, f32[256,512]{1,0:T(8,128)S(1)}, u32[]{:S(2)}, u32[]{:S(2)}) collective-permute-start(f32[256,512]{1,0:T(8,128)S(1)} %term.14), channel_id=1, source_target_pairs={{0,2},{1,15},{2,4},{3,1},{4,6},{5,3},{6,8},{7,5},{8,10},{9,7},{10,... | collective-permute-start | bytes 1572872 | tf_op jit(solution)/shard_map/ppermute | solution.py:37
  (8 other events, 33.0 us)
